TPU v7x, 128 devices: a whole 4x4x4 slice. The times are simulated.
128 devices in a mesh: row: 16 (over y, x), col: 4 (over z), layer: 2 (over core).
Axes of the slice: x: 4, y: 4, z: 4, core: 2. Of those that a mesh axis runs over, the one named last changes fastest.
Arguments:
- left_blocks: float32 [2, 8192, 8192], P('layer', 'row', 'col'), may hold values from -6 to 6
- left_pattern: int32 [2, 64, 64], P('layer', 'row', 'col'), may hold values 0 or 1
- right_blocks: float32 [2, 8192, 4096], P('layer', 'row', 'col'), may hold values from -0.078125 to 0.078125
- right_pattern: int32 [2, 64, 32], P('layer', 'row', 'col'), may hold values 0 or 1
- keep_mask: int32 [16, 4, 32], P('row', 'col'), may hold values 0 or 1
- owner: int32 [16, 4, 32, 1], P('row', 'col'), may hold values from 0 to 1; in each aligned block of 32 rows (0 to 31, 32 to 63, ..., all dimensions but the last counted through in order) at most 32 rows name the same one
Outputs:
- owned: float32 [16, 4, 64, 128, 128], P('row', 'col', 'layer')
Inputs may be any that keep to these rules, and one draw needn't show every extreme that they name: An owner may be named by all 32 blocks of a tile, and some tile reaches that, so each owner needs 32 slots.
All inputs are finite; a program needn't handle non-finite values. No bound on the sum of `left_pattern` or of `right_pattern` or of `keep_mask` on one device may be relied on, other than what follows from the above.
Results may differ from a plain program's by a relative error of at most 0.0001.
Values sent between devices are 32-bit elements; how exact they have to be, the bound alone decides.
No kernel may reach another device: no remote copies, remote signals or barrier semaphores. Data moves between devices by JAX's collectives and lax.ppermute only.
A program may use at most 128 MiB of HBM per device.

v0:
```python
import jax
import jax.numpy as jnp
from jax import lax
from jax.sharding import PartitionSpec as P

BS = 128


def spread(pattern):
    wide = jnp.repeat(jnp.repeat(pattern, BS, axis=0), BS, axis=1)
    return wide.astype(jnp.float32)


def local(left_blocks, left_pattern, right_blocks, right_pattern, keep_mask, owner):
    left_eff = left_blocks[0] * spread(left_pattern[0])
    right_eff = right_blocks[0] * spread(right_pattern[0])
    row_blocks = left_pattern.shape[1]
    col_blocks = right_pattern.shape[2]
    right_all = lax.all_gather(right_eff, "row", axis=0, tiled=True)
    partial_sum = jnp.dot(
        lax.all_gather(left_eff, "col", axis=1, tiled=True),
        right_all,
        preferred_element_type=jnp.float32,
        precision=lax.Precision.HIGHEST,
    )
    tile_count = row_blocks * col_blocks
    tiles = (
        partial_sum.reshape(row_blocks, BS, col_blocks, BS)
        .transpose(0, 2, 1, 3)
        .reshape(tile_count, BS, BS)
    )
    tiles = tiles * keep_mask[0, 0].astype(jnp.float32)[:, None, None]
    layers = lax.axis_size("layer")
    capacity = 2 * tile_count // layers
    share_count = tile_count // layers
    owners = owner[0, 0, :, 0]
    onehot = (owners[:, None] == jnp.arange(layers, dtype=jnp.int32)[None, :]).astype(jnp.int32)
    before = jnp.cumsum(onehot, axis=0) - onehot
    rank = jnp.sum(before * onehot, axis=1)
    slot = owners * capacity + rank
    share = lax.psum_scatter(tiles, "layer", scatter_dimension=0, tiled=True)
    layer_id = lax.axis_index("layer")
    mine = lax.dynamic_slice_in_dim(owners, layer_id * share_count, share_count, 0)
    select = (mine[None, :] == jnp.arange(layers, dtype=jnp.int32)[:, None]).astype(jnp.float32)
    outgoing = select[:, :, None, None] * share[None]
    incoming = lax.all_to_all(outgoing, "layer", split_axis=0, concat_axis=0, tiled=True)
    flat = incoming.reshape(tile_count, BS, BS)
    wanted = layer_id * capacity + jnp.arange(capacity, dtype=jnp.int32)
    pick = (slot[None, :] == wanted[:, None]).astype(jnp.float32)
    owned = jnp.einsum("st,tab->sab", pick, flat, precision=lax.Precision.HIGHEST)
    return owned[None, None]


def solution(mesh):
    return jax.shard_map(
        local,
        mesh=mesh,
        in_specs=(
            P("layer", "row", "col"),
            P("layer", "row", "col"),
            P("layer", "row", "col"),
            P("layer", "row", "col"),
            P("row", "col", None),
            P("row", "col", None, None),
        ),
        out_specs=P("row", "col", "layer", None, None),
        check_vma=False,
    )
```

profile of v0, /device:TPU:1, one launch (start us, length us, event | category | flops | bytes accessed | tf_op | source)
XLA Modules:
  0.0 463.0 jit_solution(2540187784473713864)
XLA Ops:
  6.5 0.7 convert_bitcast_fusion.1
  7.3 1.1 broadcast_in_dim.11
  8.4 1.0 copy-done
  9.4 4.3 bitcast_multiply_fusion
  13.8 0.6 copy-done.3
  14.5 0.6 broadcast_in_dim.26
  15.1 0.3 copy-done.1
  15.4 2.0 bitcast_multiply_fusion.1
  17.4 0.2 reduce-scatter.2.cloned.1.call-start
  17.7 0.4 copy-done.4
  18.1 153.2 %all-gather.3.cloned.1.call-done = f32[512,8192]{1,0:T(8,128)} async-done(((f32[512,2048]{1,0:T(8,128)}), f32[512,8192]{1,0:T(8,128)}) %all-gather.3.cloned.1.call-update) | async-done | bytes 16777232 | tf_op jit(solution)/shard_map/all_gather | solution.py:21
  171.3 200.1 %all-gather.5.cloned.1.call-done = f32[8192,1024]{1,0:T(8,128)} async-done(((f32[512,1024]{1,0:T(8,128)}), f32[8192,1024]{1,0:T(8,128)}) %all-gather.5.cloned.1.call-update) | async-done | bytes 33554448 | tf_op jit(solution)/shard_map/all_gather | solution.py:19
  371.4 58.6 %convolution_bitcast_fusion.1 = f32[64,8,8,128]{3,1,2,0:T(8,128)S(1)} fusion(f32[512,8192]{1,0:T(8,128)} %all-gather.3.cloned.1.call-done, f32[8192,1024]{1,0:T(8,128)} %all-gather.5.cloned.1.call-done), kind=kOutput, calls=%fused_computation.4 | convolution fusion | flops 51539607552 | bytes 52428800 | tf_op jit(solution)/shard_map/dot_general | solution.py:20
  430.0 0.5 copy.17
  430.5 0.4 copy.11
  430.9 1.5 bitcast_multiply_fusion.2
  432.4 0.6 copy-done.2
  433.5 11.7 %reduce-scatter.2.cloned.1.call-done = f32[16,128,128]{2,1,0:T(8,128)} async-done(((f32[32,128,128]{2,1,0:T(8,128)}), f32[16,128,128]{2,1,0:T(8,128)}) %reduce-scatter.2.cloned.1.call-update) | async-done | bytes 1048592 | tf_op jit(solution)/shard_map/reduce_scatter | solution.py:41
  445.2 1.8 copy.12
  447.0 0.2 broadcast_multiply_fusion
  447.2 5.2 %all_to_all.5 = f32[2,16,128,128]{3,1,2,0:T(8,128)S(1)} all-to-all(f32[2,16,128,128]{3,1,2,0:T(8,128)S(1)} %broadcast_multiply_fusion), channel_id=1, replica_groups=mesh['row'=16,'col'=4,'layer'=2] {'layer'}, dimensions={0} | all-to-all | bytes 4194304 | tf_op jit(solution)/shard_map/all_to_all | solution.py:46
  452.4 0.3 copy.13
  452.7 1.2 convolution_bitcast_fusion
  453.9 2.5 copy.14
  (20 shorter events, 0.5 us)
Async XLA Ops:
  6.5 164.7 %all-gather.3.cloned.1.call-start = ((), (), s32[]{:S(2)}) async-start(), calls=%async_computation.2 | async-start | bytes 20971520 | tf_op jit(solution)/shard_map/all_gather | solution.py:21
  7.2 2.2 copy-start
  13.7 0.7 copy-start.3
  13.8 1.6 copy-start.1
  13.8 357.6 %all-gather.5.cloned.1.call-start = ((), (), s32[]{:S(2)}) async-start(), calls=%async_computation.3 | async-start | bytes 35651584 | tf_op jit(solution)/shard_map/all_gather | solution.py:19
  17.4 0.7 copy-start.4
  17.4 427.7 %reduce-scatter.2.cloned.1.call-start = ((), (), s32[]{:S(2)}) async-start(), calls=%async_computation.4 | async-start | bytes 3145728 | tf_op jit(solution)/shard_map/reduce_scatter | solution.py:41
  432.4 0.7 copy-start.2
Sparse Core Ops, SparseCore 0:
  13.9 157.3 all-gather.2
  173.4 197.9 all-gather.4
  432.6 12.5 reduce-scatter.1
where the time goes:
time: 463 us
  waiting for transfers between devices  365 us (79%)
  matrix products  59.8 us (13%)
  between operations  13.2 us (3%)
  local copies, waits for them, and re-layouts  10.3 us (2%)
  other arithmetic  9.08 us (2%)
  blocking collectives  5.19 us (1%)
    all_gather x1, waiting for transfers between devices, local(): right_all = lax.all_gather(right_eff, 'row', axis=0, tiled=True)  200 us
    all_gather x1, waiting for transfers between devices, local(): lax.all_gather(left_eff, 'col', axis=1, tiled=True)  153 us
    dot_general x1, matrix products, local(): jnp.dot(lax.all_gather(left_eff, 'col', axis=1, tiled=True), right_all, p...  58.6 us
    reduce_scatter x1, waiting for transfers between devices, local(): share = lax.psum_scatter(tiles, 'layer', scatter_dimension=0, tiled=True)  11.7 us
  transfers between devices with their start and end apart: 3, of which 3 were waited for; matrix products, arithmetic and copies ran while one was open for 1% of the time, Pallas kernels for 0%

commit v1 on v0

v1 whole, which is shorter than its diff:
```python
import functools

import jax
import jax.numpy as jnp
from jax import lax
from jax.experimental import pallas as pl
from jax.experimental.pallas import tpu as pltpu
from jax.sharding import PartitionSpec as P

BS = 128
HDR = 8
COUNT = 127
FLAG = 126
L_CAP = 36
R_HALF = 11
G_A = 16
G_B = 16
G_CAP = G_A + G_B
AXES = ("row", "col", "layer")
F32 = jnp.float32
BF16 = jnp.bfloat16


def dense(left_blocks, left_pattern, right_blocks, right_pattern, keep_mask, owner):
    def spread(pattern):
        wide = jnp.repeat(jnp.repeat(pattern, BS, axis=0), BS, axis=1)
        return wide.astype(F32)

    left_eff = left_blocks[0] * spread(left_pattern[0])
    right_eff = right_blocks[0] * spread(right_pattern[0])
    row_blocks = left_pattern.shape[1]
    col_blocks = right_pattern.shape[2]
    right_all = lax.all_gather(right_eff, "row", axis=0, tiled=True)
    partial_sum = jnp.dot(
        lax.all_gather(left_eff, "col", axis=1, tiled=True),
        right_all,
        preferred_element_type=F32,
        precision=lax.Precision.HIGHEST,
    )
    tile_count = row_blocks * col_blocks
    tiles = (
        partial_sum.reshape(row_blocks, BS, col_blocks, BS)
        .transpose(0, 2, 1, 3)
        .reshape(tile_count, BS, BS)
    )
    tiles = tiles * keep_mask[0, 0].astype(F32)[:, None, None]
    other = lax.ppermute(tiles, "layer", [(0, 1), (1, 0)])
    tiles = tiles + other
    owners = owner[0, 0, :, 0]
    onehot = (owners[:, None] == jnp.arange(2, dtype=jnp.int32)[None, :]).astype(jnp.int32)
    before = jnp.cumsum(onehot, axis=0) - onehot
    rank = jnp.sum(before * onehot, axis=1)
    slot = owners * tile_count + rank
    wanted = lax.axis_index("layer") * tile_count + jnp.arange(tile_count, dtype=jnp.int32)
    pick = (slot[None, :] == wanted[:, None]).astype(F32)
    return jnp.einsum("st,tab->sab", pick, tiles, precision=lax.Precision.HIGHEST)


def ring(array, axis):
    pairs = []
    for y in range(4):
        for x in range(4):
            for z in range(4):
                for core in range(2):
                    to = {"y": y, "x": x, "z": z}
                    to[axis] = (to[axis] + 1 - 2 * core) % 4
                    source = ((y * 4 + x) * 4 + z) * 2 + core
                    target = ((to["y"] * 4 + to["x"]) * 4 + to["z"]) * 2 + core
                    pairs.append((source, target))
    return lax.ppermute(array, AXES, pairs)


def hops(array, axis):
    out = [array]
    for _ in range(3):
        out.append(ring(out[-1], axis))
    return out


def block_rows(slot, head=HDR):
    return pl.ds(pl.multiple_of(head + slot * BS, 8), BS)


def blank():
    return jnp.zeros((HDR, BS), F32)


def place(header, lane, value):
    lanes = lax.broadcasted_iota(jnp.int32, (HDR, BS), 1)
    return jnp.where(lanes == lane, value, header)


def pack_right_kernel(lpat, rpat, right, a_out, b_out, codes, head, sems, hsems):
    row = lax.axis_index("row")
    flip = row & 1

    def scan(i, n):
        codes[n] = i
        return n + rpat[0, i >> 3, i & 7]

    n = lax.fori_loop(0, 32, scan, jnp.int32(0))
    n_left = lax.fori_loop(0, 64, lambda i, s: s + lpat[0, i >> 4, i & 15], jnp.int32(0))
    over = (n > 2 * R_HALF) | (n_left > L_CAP)
    m = jnp.minimum(n, 2 * R_HALF)

    def copies(s):
        code = codes[s]
        source = right.at[0, pl.ds(pl.multiple_of((code >> 3) * BS, BS), BS), pl.ds(pl.multiple_of((code & 7) * BS, BS), BS)]
        rows = block_rows(s >> 1)
        return (
            pltpu.make_async_copy(source, a_out.at[rows], sems.at[s]),
            pltpu.make_async_copy(source, b_out.at[rows], sems.at[s]),
        )

    def start(s, headers):
        in_a = ((s + flip) & 1) == 0
        to_a, to_b = copies(s)

        @pl.when(in_a)
        def _():
            to_a.start()

        @pl.when(jnp.logical_not(in_a))
        def _():
            to_b.start()

        code = (row * 32 + codes[s]).astype(F32)
        slot = s >> 1
        return (
            place(headers[0], jnp.where(in_a, slot, -1), code),
            place(headers[1], jnp.where(in_a, -1, slot), code),
        )

    header_a, header_b = lax.fori_loop(0, m, start, (blank(), blank()))
    count_a = (m + 1 - flip) >> 1
    flag = over.astype(F32)
    head[0] = place(place(header_a, COUNT, count_a.astype(F32)), FLAG, flag)
    head[1] = place(place(header_b, COUNT, (m - count_a).astype(F32)), FLAG, flag)
    ha = pltpu.make_async_copy(head.at[0], a_out.at[pl.ds(0, HDR)], hsems.at[0])
    hb = pltpu.make_async_copy(head.at[1], b_out.at[pl.ds(0, HDR)], hsems.at[1])
    ha.start()
    hb.start()

    def finish(s, _):
        copies(s)[0].wait()
        return 0

    lax.fori_loop(0, m, finish, 0)
    ha.wait()
    hb.wait()


def pack_left_kernel(lpat, left, out, codes, head, sems, hsem):
    base = lax.axis_index("col") * 64

    def scan(i, n):
        codes[n] = i
        return n + lpat[0, i & 3, i >> 2]

    n = lax.fori_loop(0, 64, scan, jnp.int32(0))
    m = jnp.minimum(n, L_CAP)

    def copy(s):
        code = codes[s]
        source = left.at[0, pl.ds(pl.multiple_of((code & 3) * BS, BS), BS), pl.ds(pl.multiple_of((code >> 2) * BS, BS), BS)]
        return pltpu.make_async_copy(source, out.at[block_rows(s)], sems.at[s])

    def start(s, header):
        copy(s).start()
        return place(header, s, (base + codes[s]).astype(F32))

    header = lax.fori_loop(0, m, start, blank())
    head[...] = place(header, COUNT, m.astype(F32))
    h = pltpu.make_async_copy(head, out.at[pl.ds(0, HDR)], hsem)
    h.start()

    def finish(s, _):
        copy(s).wait()
        return 0

    lax.fori_loop(0, m, finish, 0)
    h.wait()


def merge_kernel(*refs):
    ins = (refs[0:4], refs[4:8])
    outs = (refs[8:10], refs[10:12])
    seen, head, sems, hsems = refs[12:]
    reads = []
    for half in range(2):
        for i in range(4):
            read = pltpu.make_async_copy(ins[half][i].at[pl.ds(0, HDR)], seen.at[half, i], hsems.at[half * 4 + i])
            read.start()
            reads.append(read)
    for read in reads:
        read.wait()
    totals = []
    for half in range(2):
        first, second = outs[half]
        header = blank()
        total = jnp.int32(0)
        flag = F32(0) if False else jnp.float32(0)
        for i in range(4):
            count = seen[half, i, 0, COUNT].astype(jnp.int32)
            flag = jnp.maximum(flag, seen[half, i, 0, FLAG])

            def start(s, header, half=half, i=i, total=total, first=first, second=second):
                g = total + s
                source = ins[half][i].at[block_rows(s)]

                @pl.when(g < G_A)
                def _():
                    pltpu.make_async_copy(source, first.at[block_rows(g)], sems.at[half, g]).start()

                @pl.when((g >= G_A) & (g < G_CAP))
                def _():
                    pltpu.make_async_copy(source, second.at[block_rows(g - G_A, 0)], sems.at[half, g]).start()

                return place(header, jnp.where(g < G_CAP, g, -1), seen[half, i, 0, s])

            header = lax.fori_loop(0, count, start, header)
            total = total + count
        kept = jnp.minimum(total, G_CAP)
        flag = jnp.where(total > G_CAP, jnp.float32(1), flag)
        head[half] = place(place(header, COUNT, kept.astype(F32)), FLAG, flag)
        pltpu.make_async_copy(head.at[half], first.at[pl.ds(0, HDR)], hsems.at[8 + half]).start()
        totals.append(kept)
    for half in range(2):
        first, second = outs[half]

        def finish(s, _, half=half, first=first):
            pltpu.make_async_copy(ins[half][0].at[block_rows(0)], first.at[block_rows(0)], sems.at[half, s]).wait()
            return 0

        lax.fori_loop(0, totals[half], finish, 0)
        pltpu.make_async_copy(head.at[half], first.at[pl.ds(0, HDR)], hsems.at[8 + half]).wait()


def split(block):
    high = block.astype(BF16)
    low = (block - high.astype(F32)).astype(BF16)
    return jnp.concatenate([high, low], axis=1)


def multiply_kernel(groups, begin, final, *refs):
    refs = list(refs)
    lefts = refs[:4]
    del refs[:4]
    parts = []
    for first, second in groups:
        parts.append((refs.pop(0), refs.pop(0) if second else None))
    acc_in = None if begin else refs.pop(0)
    if final:
        keep_ref, owner_ref = refs.pop(0), refs.pop(0)
        mine_ref, send_ref, flag_ref = refs.pop(0), refs.pop(0), refs.pop(0)
        acc = refs.pop(0)
    else:
        acc = refs.pop(0)
    lv, rv, lhead, rhead, table, work, lsems, rsems, asem, hsems = refs
    heads = []
    for i in range(4):
        heads.append(pltpu.make_async_copy(lefts[i].at[pl.ds(0, HDR)], lhead.at[i], hsems.at[i]))
    for g, (first, _) in enumerate(parts):
        heads.append(pltpu.make_async_copy(first.at[pl.ds(0, HDR)], rhead.at[g], hsems.at[4 + g]))
    for copy in heads:
        copy.start()
    loads = []
    for i in range(4):
        loads.append(pltpu.make_async_copy(lefts[i].at[pl.ds(HDR, L_CAP * BS)], lv.at[pl.ds(i * L_CAP * BS, L_CAP * BS)], lsems.at[i]))
    for g, (first, second) in enumerate(parts):
        if groups[g][0]:
            loads.append(pltpu.make_async_copy(first.at[pl.ds(HDR, G_A * BS)], rv.at[pl.ds(g * G_CAP * BS, G_A * BS)], rsems.at[2 * g]))
        if second is not None:
            loads.append(pltpu.make_async_copy(second, rv.at[pl.ds((g * G_CAP + G_A) * BS, G_B * BS)], rsems.at[2 * g + 1]))
    for copy in loads:
        copy.start()
    if begin:
        acc[...] = jnp.zeros(acc.shape, F32)
    else:
        acc_load = pltpu.make_async_copy(acc_in, acc, asem)
        acc_load.start()
    zero_slot = 4 * L_CAP
    lv[pl.ds(zero_slot * BS, BS)] = jnp.zeros((BS, BS), F32)

    def clear(i, _):
        table[i] = zero_slot
        return 0

    lax.fori_loop(0, 256, clear, 0)
    for copy in heads:
        copy.wait()
    for i in range(4):

        def note(s, _, i=i):
            table[lhead[i, 0, s].astype(jnp.int32)] = i * L_CAP + s
            return 0

        lax.fori_loop(0, lhead[i, 0, COUNT].astype(jnp.int32), note, 0)
    items = jnp.int32(0)
    for g in range(len(parts)):
        count = rhead[g, 0, COUNT].astype(jnp.int32)
        low = 0 if groups[g][0] else G_A
        high = count if groups[g][1] else jnp.minimum(count, G_A)

        def note(s, n, g=g):
            work[n] = rhead[g, 0, s].astype(jnp.int32) * 256 + g * G_CAP + s
            return n + 1

        items = lax.fori_loop(low, high, note, items)
    for copy in loads:
        copy.wait()
    if not begin:
        acc_load.wait()

    def step(w, _):
        entry = work[w]
        code = lax.shift_right_logical(entry, 8)
        source = entry & 255
        k4 = lax.shift_right_logical(code, 3) * 4
        c = code & 7
        right = split(rv[pl.ds(pl.multiple_of(source * BS, BS), BS)])
        weights = jnp.concatenate([right, right], axis=0)
        rows = [split(lv[pl.ds(pl.multiple_of(table[k4 + r] * BS, BS), BS)]) for r in range(4)]
        result = jnp.dot(jnp.concatenate(rows, axis=0), weights, preferred_element_type=F32)
        acc[c] += result[:, :BS] + result[:, BS:]
        return 0

    lax.fori_loop(0, items, step, 0)

    if final:
        me = lax.axis_index("layer")
        mine_ref[...] = jnp.zeros(mine_ref.shape, F32)
        send_ref[...] = jnp.zeros(send_ref.shape, F32)
        counts = [jnp.int32(0), jnp.int32(0)]
        for t in range(32):
            who = owner_ref[0, 0, t]
            slot = jnp.where(who == 0, counts[0], counts[1])
            block = acc[t % 8, pl.ds((t // 8) * BS, BS)] * keep_ref[0, 0, t].astype(F32)

            @pl.when(who == me)
            def _(block=block, slot=slot):
                mine_ref[slot] = block

            @pl.when(who != me)
            def _(block=block, slot=slot):
                send_ref[slot] = block

            counts[0] = counts[0] + (who == 0).astype(jnp.int32)
            counts[1] = counts[1] + (who != 0).astype(jnp.int32)
        flag = jnp.float32(0)
        for g in range(len(parts)):
            flag = jnp.maximum(flag, rhead[g, 0, FLAG])
        flag_ref[...] = jnp.full((HDR, BS), flag)


ANY = pl.BlockSpec(memory_space=pl.ANY)
SMEM = pl.BlockSpec(memory_space=pltpu.SMEM)
VMEM = pl.BlockSpec(memory_space=pltpu.VMEM)
PARAMS = pltpu.CompilerParams(vmem_limit_bytes=40 * 2**20)


def packed(blocks, head=HDR):
    return jax.ShapeDtypeStruct((head + blocks * BS, BS), F32)


def multiply(lefts, groups, parts, acc, keep=None, owner=None):
    begin, final = acc is None, keep is not None
    operands = list(lefts)
    specs = [ANY] * 4
    for (first, second), (one, two) in zip(groups, parts):
        operands.append(one)
        specs.append(ANY)
        if second:
            operands.append(two)
            specs.append(ANY)
    if not begin:
        operands.append(acc)
        specs.append(ANY)
    tile = (8, 4 * BS, BS)
    scratch = []
    if final:
        operands += [keep, owner]
        specs += [SMEM, SMEM]
        out_shape = [jax.ShapeDtypeStruct((32, BS, BS), F32)] * 2 + [jax.ShapeDtypeStruct((HDR, BS), F32)]
        out_specs = [VMEM] * 3
        scratch.append(pltpu.VMEM(tile, F32))
    else:
        out_shape = jax.ShapeDtypeStruct(tile, F32)
        out_specs = VMEM
    number = len(groups)
    scratch += [
        pltpu.VMEM(((4 * L_CAP + 1) * BS, BS), F32),
        pltpu.VMEM((number * G_CAP * BS, BS), F32),
        pltpu.SMEM((4, HDR, BS), F32),
        pltpu.SMEM((number, HDR, BS), F32),
        pltpu.SMEM((256,), jnp.int32),
        pltpu.SMEM((number * G_CAP,), jnp.int32),
        pltpu.SemaphoreType.DMA((4,)),
        pltpu.SemaphoreType.DMA((2 * number,)),
        pltpu.SemaphoreType.DMA,
        pltpu.SemaphoreType.DMA((4 + number,)),
    ]
    work = 12 * number
    return pl.pallas_call(
        functools.partial(multiply_kernel, groups, begin, final),
        out_shape=out_shape,
        in_specs=specs,
        out_specs=out_specs,
        scratch_shapes=scratch,
        compiler_params=PARAMS,
        cost_estimate=pl.CostEstimate(flops=work * 4 * 2 * 512 * BS * BS, bytes_accessed=16 * 2**20, transcendentals=0),
    )(*operands)


def local(left_blocks, left_pattern, right_blocks, right_pattern, keep_mask, owner):
    a0, b0 = pl.pallas_call(
        pack_right_kernel,
        out_shape=[packed(R_HALF)] * 2,
        in_specs=[SMEM, SMEM, ANY],
        out_specs=[ANY, ANY],
        scratch_shapes=[
            pltpu.SMEM((33,), jnp.int32),
            pltpu.VMEM((2, HDR, BS), F32),
            pltpu.SemaphoreType.DMA((2 * R_HALF,)),
            pltpu.SemaphoreType.DMA((2,)),
        ],
        compiler_params=PARAMS,
    )(left_pattern, right_pattern, right_blocks)
    l0 = pl.pallas_call(
        pack_left_kernel,
        out_shape=packed(L_CAP),
        in_specs=[SMEM, ANY],
        out_specs=ANY,
        scratch_shapes=[
            pltpu.SMEM((65,), jnp.int32),
            pltpu.VMEM((HDR, BS), F32),
            pltpu.SemaphoreType.DMA((L_CAP,)),
            pltpu.SemaphoreType.DMA,
        ],
        compiler_params=PARAMS,
    )(left_pattern, left_blocks)
    halves_a = hops(a0, "x")
    halves_b = hops(b0, "y")
    lefts = hops(l0, "z")
    merged = pl.pallas_call(
        merge_kernel,
        out_shape=[packed(G_A), packed(G_B, 0)] * 2,
        in_specs=[ANY] * 8,
        out_specs=[ANY] * 4,
        scratch_shapes=[
            pltpu.SMEM((2, 4, HDR, BS), F32),
            pltpu.VMEM((2, HDR, BS), F32),
            pltpu.SemaphoreType.DMA((2, G_CAP)),
            pltpu.SemaphoreType.DMA((10,)),
        ],
        compiler_params=PARAMS,
    )(*halves_a, *halves_b)
    ga = list(zip(hops(merged[0], "y"), hops(merged[1], "y")))
    gb = list(zip(hops(merged[2], "x"), hops(merged[3], "x")))
    both = (True, True)
    acc = multiply(lefts, [both] * 6, [ga[0], gb[0], ga[1], gb[1], ga[2], gb[2]], None)
    mine, send, flag = multiply(lefts, [both] * 2, [ga[3], gb[3]], acc, keep_mask, owner.reshape(1, 1, 32))
    heads = [g[0][:1, FLAG] for g in ga + gb]
    flag = functools.reduce(jnp.maximum, heads)
    for _ in range(3):
        flag = jnp.maximum(flag, ring(flag, "z"))
    flag = jnp.maximum(flag, lax.ppermute(flag, "layer", [(0, 1), (1, 0)]))
    other = lax.ppermute(send, "layer", [(0, 1), (1, 0)])
    owned = lax.cond(
        flag[0] > 0,
        lambda: dense(left_blocks, left_pattern, right_blocks, right_pattern, keep_mask, owner),
        lambda: mine + other,
    )
    return owned[None, None]


def solution(mesh):
    return jax.shard_map(
        local,
        mesh=mesh,
        in_specs=(
            P("layer", "row", "col"),
            P("layer", "row", "col"),
            P("layer", "row", "col"),
            P("layer", "row", "col"),
            P("row", "col", None),
            P("row", "col", None, None),
        ),
        out_specs=P("row", "col", "layer", None, None),
        check_vma=False,
    )
```

time: 463 us -> 236 us (0.51)
  waiting for transfers between devices: 365 us -> 66.4 us
  Pallas kernels: 0 us -> 70.5 us
  matrix products: 59.8 us -> 0 us
  starting transfers between devices: 0.27 us -> 59.1 us
  between operations: 13.2 us -> 21.1 us
  local copies, waits for them, and re-layouts: 10.3 us -> 17.2 us
  blocking collectives: 5.19 us -> 0 us
  other arithmetic: 9.08 us -> 3.89 us
    all_gather x2 -> x0, waiting for transfers between devices: 353 us -> none  [the longest x1 200 us: local(): right_all = lax.all_gather(right_eff, 'row', axis=0, tiled=True)]
    pallas_call x0 -> x5, Pallas kernels: none -> 70.5 us  [the longest x2 57.9 us: multiply(): pl.pallas_call(functools.partial(multiply_kernel, groups, begin, final),...]
    ppermute x0 -> x26, waiting for transfers between devices: none -> 66.4 us  [the longest x24 66.3 us: ring(): return lax.ppermute(array, AXES, pairs)]
    dot_general x2 -> x0, matrix products: 59.8 us -> none  [the longest x1 58.6 us: local(): jnp.dot(lax.all_gather(left_eff, 'col', axis=1, tiled=True), right_all, p...]
    ppermute x0 -> x26, starting transfers between devices: none -> 59.1 us  [the longest x24 51.6 us: ring(): return lax.ppermute(array, AXES, pairs)]
    reduce_scatter x1 -> x0, waiting for transfers between devices: 11.7 us -> none  [local(): share = lax.psum_scatter(tiles, 'layer', scatter_dimension=0, tiled=True)]
    mul x4 -> x0, other arithmetic: 8.07 us -> none  [the longest x1 4.31 us: local(): left_eff = left_blocks[0] * spread(left_pattern[0])]
    unnamed x11 -> x36, local copies, waits for them, and re-layouts: 3.45 us -> 9.93 us
  transfers between devices with their start and end apart: 3 -> 26, of which waited for: 3 -> 10; matrix products, arithmetic and copies ran while one was open for 1% -> 2% of each run, Pallas kernels for 0% -> 20%
where the time goes in v1:
time: 236 us; the launch traced here: 238 us
  Pallas kernels  70.5 us (30%)
  waiting for transfers between devices  66.4 us (28%)
  starting transfers between devices  59.1 us (25%)
  between operations  21.1 us (9%)
  local copies, waits for them, and re-layouts  17.2 us (7%)
  other arithmetic  3.89 us (2%)
    ppermute x24, waiting for transfers between devices, ring(): return lax.ppermute(array, AXES, pairs)  66.3 us
    pallas_call x2, Pallas kernels, multiply(): pl.pallas_call(functools.partial(multiply_kernel, groups, begin, final),...  57.9 us
    ppermute x24, starting transfers between devices, ring(): return lax.ppermute(array, AXES, pairs)  51.6 us
    unnamed x36, local copies, waits for them, and re-layouts  9.93 us
    ppermute x1, starting transfers between devices, local(): flag = jnp.maximum(flag, lax.ppermute(flag, 'layer', [(0, 1), (1, 0)]))  7.36 us
    pallas_call x1, Pallas kernels, local(): pl.pallas_call(merge_kernel, out_shape=[packed(G_A), packed(G_B, 0)] * 2,...  7.31 us
    slice x8, local copies, waits for them, and re-layouts, local(): heads = [g[0][:1, FLAG] for g in ga + gb]  4.75 us
  transfers between devices with their start and end apart: 26, of which 10 were waited for; matrix products, arithmetic and copies ran while one was open for 2% of the time, Pallas kernels for 20%

profile of v1, /device:TPU:1, one launch (start us, length us, event | category | flops | bytes accessed | tf_op | source)
XLA Modules:
  0.0 238.1 jit_solution(13928539023932630783)
XLA Ops:
  6.5 3.2 %shard_map.68.refs_0_ = f32[4616,128]{1,0:T(8,128)S(1)} custom-call(s32[1,4,16]{2,1,0:T(4,128)} %lpat.3, f32[1,512,2048]{2,1,0:T(8,128)} %left.1), custom_call_target="tpu_custom_call" | custom-call | tf_op jit(solution)/shard_map/pallas_call | solution.py:429
  9.7 4.5 %collective-permute-start.17 = (f32[4616,128]{1,0:T(8,128)S(1)}, f32[4616,128]{1,0:T(8,128)S(1)}, u32[]{:S(2)}, u32[]{:S(2)}) collective-permute-start(f32[4616,128]{1,0:T(8,128)S(1)} %shard_map.68.refs_0_), channel_id=1, source_target_pairs={{0,2},{1,7},{2,4},{3,1},{4,6},{5,3},{6,0},{7,5},{8,10},{9,15},{10,... | collective-permute-start | bytes 7090184 | tf_op jit(solution)/shard_map/ppermute | solution.py:70
  18.9 2.7 %collective-permute-start.4 = (f32[1416,128]{1,0:T(8,128)S(1)}, f32[1416,128]{1,0:T(8,128)S(1)}, u32[]{:S(2)}, u32[]{:S(2)}) collective-permute-start(f32[1416,128]{1,0:T(8,128)S(1)} %get-tuple-element.42.refs_4_), channel_id=1, source_target_pairs={{0,32},{1,97},{2,34},{3,99},{4,36},{5,101},{6,38},{7,103},{8,40},{... | collective-permute-start | bytes 2174984 | tf_op jit(solution)/shard_map/ppermute | solution.py:70
  21.6 18.5 %collective-permute-done.17.refs_1_ = f32[4616,128]{1,0:T(8,128)S(1)} collective-permute-done((f32[4616,128]{1,0:T(8,128)S(1)}, f32[4616,128]{1,0:T(8,128)S(1)}, u32[]{:S(2)}, u32[]{:S(2)}) %collective-permute-start.17) | collective-permute-done | bytes 2363424 | tf_op jit(solution)/shard_map/ppermute | solution.py:70
  40.1 3.1 %collective-permute-start.18 = (f32[4616,128]{1,0:T(8,128)S(1)}, f32[4616,128]{1,0:T(8,128)S(1)}, u32[]{:S(2)}, u32[]{:S(2)}) collective-permute-start(f32[4616,128]{1,0:T(8,128)S(1)} %collective-permute-done.17.refs_1_), channel_id=1, source_target_pairs={{0,2},{1,7},{2,4},{3,1},{4,6},{5,3},{6,0},{7,5},{8,10},{9,15},{10,... | collective-permute-start | bytes 7090184 | tf_op jit(solution)/shard_map/ppermute | solution.py:70
  43.2 2.7 %collective-permute-start.2 = (f32[1416,128]{1,0:T(8,128)S(1)}, f32[1416,128]{1,0:T(8,128)S(1)}, u32[]{:S(2)}, u32[]{:S(2)}) collective-permute-start(f32[1416,128]{1,0:T(8,128)S(1)} %collective-permute-done.1.refs_1_), channel_id=1, source_target_pairs={{0,8},{1,25},{2,10},{3,27},{4,12},{5,29},{6,14},{7,31},{8,16},{9,1... | collective-permute-start | bytes 2174984 | tf_op jit(solution)/shard_map/ppermute | solution.py:70
  48.4 5.8 %collective-permute-done.2.refs_2_ = f32[1416,128]{1,0:T(8,128)S(1)} collective-permute-done((f32[1416,128]{1,0:T(8,128)S(1)}, f32[1416,128]{1,0:T(8,128)S(1)}, u32[]{:S(2)}, u32[]{:S(2)}) %collective-permute-start.2) | collective-permute-done | bytes 725024 | tf_op jit(solution)/shard_map/ppermute | solution.py:70
  54.2 3.4 %collective-permute-start.3 = (f32[1416,128]{1,0:T(8,128)S(1)}, f32[1416,128]{1,0:T(8,128)S(1)}, u32[]{:S(2)}, u32[]{:S(2)}) collective-permute-start(f32[1416,128]{1,0:T(8,128)S(1)} %collective-permute-done.2.refs_2_), channel_id=1, source_target_pairs={{0,8},{1,25},{2,10},{3,27},{4,12},{5,29},{6,14},{7,31},{8,16},{9,1... | collective-permute-start | bytes 2174984 | tf_op jit(solution)/shard_map/ppermute | solution.py:70
  60.1 5.8 %collective-permute-done.3.refs_3_ = f32[1416,128]{1,0:T(8,128)S(1)} collective-permute-done((f32[1416,128]{1,0:T(8,128)S(1)}, f32[1416,128]{1,0:T(8,128)S(1)}, u32[]{:S(2)}, u32[]{:S(2)}) %collective-permute-start.3) | collective-permute-done | bytes 725024 | tf_op jit(solution)/shard_map/ppermute | solution.py:70
  68.4 7.3 %shard_map.67 = (f32[2056,128]{1,0:T(8,128)S(1)}, f32[2048,128]{1,0:T(8,128)S(1)}, f32[2056,128]{1,0:T(8,128)S(1)}, f32[2048,128]{1,0:T(8,128)S(1)}) custom-call(f32[1416,128]{1,0:T(8,128)S(1)} %get-tuple-element.41.refs_0_, f32[1416,128]{1,0:T(8,128)S(1)} %collective-permute-done.1.refs_1_, f32[1416,128]{1,0:T(8,128)S(1)} %collective-permute-done.2.refs_2_, ...), custom_call_target="tpu_custom_call" | custom-call | tf_op jit(solution)/shard_map/pallas_call | solution.py:445
  79.9 10.0 %collective-permute-done.10.refs_10_ = f32[2056,128]{1,0:T(8,128)S(1)} collective-permute-done((f32[2056,128]{1,0:T(8,128)S(1)}, f32[2056,128]{1,0:T(8,128)S(1)}, u32[]{:S(2)}, u32[]{:S(2)}) %collective-permute-start.10) | collective-permute-done | bytes 1052704 | tf_op jit(solution)/shard_map/ppermute | solution.py:70
  89.9 2.7 %collective-permute-start.11 = (f32[2056,128]{1,0:T(8,128)S(1)}, f32[2056,128]{1,0:T(8,128)S(1)}, u32[]{:S(2)}, u32[]{:S(2)}) collective-permute-start(f32[2056,128]{1,0:T(8,128)S(1)} %collective-permute-done.10.refs_10_), channel_id=1, source_target_pairs={{0,8},{1,25},{2,10},{3,27},{4,12},{5,29},{6,14},{7,31},{8,16},{9,1... | collective-permute-start | bytes 3158024 | tf_op jit(solution)/shard_map/ppermute | solution.py:70
  95.0 7.7 %collective-permute-done.20.refs_9_ = f32[2048,128]{1,0:T(8,128)S(1)} collective-permute-done((f32[2048,128]{1,0:T(8,128)S(1)}, f32[2048,128]{1,0:T(8,128)S(1)}, u32[]{:S(2)}, u32[]{:S(2)}) %collective-permute-start.20) | collective-permute-done | bytes 1048608 | tf_op jit(solution)/shard_map/ppermute | solution.py:70
  102.7 3.5 %collective-permute-start.21 = (f32[2048,128]{1,0:T(8,128)S(1)}, f32[2048,128]{1,0:T(8,128)S(1)}, u32[]{:S(2)}, u32[]{:S(2)}) collective-permute-start(f32[2048,128]{1,0:T(8,128)S(1)} %collective-permute-done.20.refs_9_), channel_id=1, source_target_pairs={{0,32},{1,97},{2,34},{3,99},{4,36},{5,101},{6,38},{7,103},{8,40},{... | collective-permute-start | bytes 3145736 | tf_op jit(solution)/shard_map/ppermute | solution.py:70
  106.3 6.0 %collective-permute-done.11.refs_14_ = f32[2056,128]{1,0:T(8,128)S(1)} collective-permute-done((f32[2056,128]{1,0:T(8,128)S(1)}, f32[2056,128]{1,0:T(8,128)S(1)}, u32[]{:S(2)}, u32[]{:S(2)}) %collective-permute-start.11) | collective-permute-done | bytes 1052704 | tf_op jit(solution)/shard_map/ppermute | solution.py:70
  112.3 2.7 %collective-permute-start.12 = (f32[2056,128]{1,0:T(8,128)S(1)}, f32[2056,128]{1,0:T(8,128)S(1)}, u32[]{:S(2)}, u32[]{:S(2)}) collective-permute-start(f32[2056,128]{1,0:T(8,128)S(1)} %collective-permute-done.11.refs_14_), channel_id=1, source_target_pairs={{0,8},{1,25},{2,10},{3,27},{4,12},{5,29},{6,14},{7,31},{8,16},{9,1... | collective-permute-start | bytes 3158024 | tf_op jit(solution)/shard_map/ppermute | solution.py:70
  117.4 7.8 %collective-permute-done.21.refs_13_ = f32[2048,128]{1,0:T(8,128)S(1)} collective-permute-done((f32[2048,128]{1,0:T(8,128)S(1)}, f32[2048,128]{1,0:T(8,128)S(1)}, u32[]{:S(2)}, u32[]{:S(2)}) %collective-permute-start.21) | collective-permute-done | bytes 1048608 | tf_op jit(solution)/shard_map/ppermute | solution.py:70
  125.2 3.4 %collective-permute-start.22 = (f32[2048,128]{1,0:T(8,128)S(1)}, f32[2048,128]{1,0:T(8,128)S(1)}, u32[]{:S(2)}, u32[]{:S(2)}) collective-permute-start(f32[2048,128]{1,0:T(8,128)S(1)} %collective-permute-done.21.refs_13_), channel_id=1, source_target_pairs={{0,32},{1,97},{2,34},{3,99},{4,36},{5,101},{6,38},{7,103},{8,40},{... | collective-permute-start | bytes 3145736 | tf_op jit(solution)/shard_map/ppermute | solution.py:70
  128.7 38.9 %shard_map.69.refs_8_ = f32[8,512,128]{2,1,0:T(8,128)} custom-call(f32[4616,128]{1,0:T(8,128)} %copy-done, f32[4616,128]{1,0:T(8,128)} %copy-done.2, f32[4616,128]{1,0:T(8,128)} %copy-done.12, f32[4616,128]{1,0:T(8,128)} %collective-permute-done.19.refs_3_, f32[2056,128]{1,0:T(8,128)S(1)} %get-tuple-element.43.refs_4_, ...), custom_call_target="tpu_custom_call" | custom-call | flops 4831838208 | bytes 16777216 | tf_op jit(solution)/shard_map/pallas_call | solution.py:404
  177.5 19.0 %shard_map.70 = (f32[32,128,128]{2,1,0:T(8,128)}, f32[32,128,128]{2,1,0:T(8,128)S(1)}, f32[8,128]{1,0:T(8,128)}) custom-call(f32[4616,128]{1,0:T(8,128)S(1)} %copy-done.1, f32[4616,128]{1,0:T(8,128)S(1)} %copy-done.3, f32[4616,128]{1,0:T(8,128)} %copy-done.12, f32[4616,128]{1,0:T(8,128)} %collective-permute-done.19.refs_3_, f32[2056,128]{1,0:T(8,128)S(1)} %copy-done.8, ...), custom_call_target="tpu_custom_call" | custom-call | flops 1610612736 | bytes 16777216 | tf_op jit(solution)/shard_map/pallas_call | solution.py:404
  213.0 3.2 %collective-permute-start.15 = (f32[1]{0:T(128)}, f32[1]{0:T(128)}, u32[]{:S(2)}, u32[]{:S(2)}) collective-permute-start(f32[1]{0:T(128)} %max.48), channel_id=1, source_target_pairs={{0,2},{1,7},{2,4},{3,1},{4,6},{5,3},{6,0},{7,5},{8,10},{9,15},{10,... | collective-permute-start | bytes 20 | tf_op jit(solution)/shard_map/ppermute | solution.py:70
  216.8 7.4 %collective-permute-start.16 = (f32[1]{0:T(128)}, f32[1]{0:T(128)}, u32[]{:S(2)}, u32[]{:S(2)}) collective-permute-start(f32[1]{0:T(128)} %max.49), channel_id=1, source_target_pairs={{0,1},{1,0},{2,3},{3,2},{4,5},{5,4},{6,7},{7,6},{8,9},{9,8},{10,11... | collective-permute-start | bytes 20 | tf_op jit(solution)/shard_map/ppermute | solution.py:467
  224.8 6.4 %conditional.1 = (f32[1,1,32,128,128]{4,3,2,1,0:T(8,128)}) conditional(s32[]{:T(128)} %bitcast.14, (f32[32,128,128]{2,1,0:T(8,128)}, f32[32,128,128]{2,1,0:T(8,128)S(1)}) %tuple.13, (s32[1,1,32,1]{2,3,1,0:T(1,128)S(1)}, f32[1,512,2048]{2,1,0:T(8,128)}, s32[1,4,16]{2,1,0:T(4,128)S(1)}, f32[1,512,1024]{2,1,0:T(8,128)S(1)}, s32[1,4,8]{2,1,0:T(4,128)S(1)}, ...), branch_computations={%region_0.0_spmd, %region_1.4_spmd} | conditional | flops 51743555584 | bytes 291606304 | solution.py:469
  224.8 3.9 %fusion = f32[1,1,32,128,128]{4,2,3,1,0:T(8,128)S(1)} fusion(f32[32,128,128]{2,1,0:T(8,128)S(1)} %get-tuple-element.51, f32[32,128,128]{2,1,0:T(8,128)} %get-tuple-element.50), kind=kLoop, calls=%fused_computation.1 | loop fusion | flops 524288 | bytes 6291456 | tf_op jit(solution)/shard_map/broadcast_in_dim | solution.py:474
  (80 shorter events, 44.0 us)
Async XLA Ops:
  9.7 30.3 %collective-permute-start.17 = (f32[4616,128]{1,0:T(8,128)S(1)}, f32[4616,128]{1,0:T(8,128)S(1)}, u32[]{:S(2)}, u32[]{:S(2)}) collective-permute-start(f32[4616,128]{1,0:T(8,128)S(1)} %shard_map.68.refs_0_), channel_id=1, source_target_pairs={{0,2},{1,7},{2,4},{3,1},{4,6},{5,3},{6,0},{7,5},{8,10},{9,15},{10,... | collective-permute-start | bytes 7090184 | tf_op jit(solution)/shard_map/ppermute | solution.py:70
  16.3 26.9 %collective-permute-start.1 = (f32[1416,128]{1,0:T(8,128)S(1)}, f32[1416,128]{1,0:T(8,128)S(1)}, u32[]{:S(2)}, u32[]{:S(2)}) collective-permute-start(f32[1416,128]{1,0:T(8,128)S(1)} %get-tuple-element.41.refs_0_), channel_id=1, source_target_pairs={{0,8},{1,25},{2,10},{3,27},{4,12},{5,29},{6,14},{7,31},{8,16},{9,1... | collective-permute-start | bytes 2174984 | tf_op jit(solution)/shard_map/ppermute | solution.py:70
  18.9 27.0 %collective-permute-start.4 = (f32[1416,128]{1,0:T(8,128)S(1)}, f32[1416,128]{1,0:T(8,128)S(1)}, u32[]{:S(2)}, u32[]{:S(2)}) collective-permute-start(f32[1416,128]{1,0:T(8,128)S(1)} %get-tuple-element.42.refs_4_), channel_id=1, source_target_pairs={{0,32},{1,97},{2,34},{3,99},{4,36},{5,101},{6,38},{7,103},{8,40},{... | collective-permute-start | bytes 2174984 | tf_op jit(solution)/shard_map/ppermute | solution.py:70
  40.1 39.8 %collective-permute-start.18 = (f32[4616,128]{1,0:T(8,128)S(1)}, f32[4616,128]{1,0:T(8,128)S(1)}, u32[]{:S(2)}, u32[]{:S(2)}) collective-permute-start(f32[4616,128]{1,0:T(8,128)S(1)} %collective-permute-done.17.refs_1_), channel_id=1, source_target_pairs={{0,2},{1,7},{2,4},{3,1},{4,6},{5,3},{6,0},{7,5},{8,10},{9,15},{10,... | collective-permute-start | bytes 7090184 | tf_op jit(solution)/shard_map/ppermute | solution.py:70
  43.2 11.0 %collective-permute-start.2 = (f32[1416,128]{1,0:T(8,128)S(1)}, f32[1416,128]{1,0:T(8,128)S(1)}, u32[]{:S(2)}, u32[]{:S(2)}) collective-permute-start(f32[1416,128]{1,0:T(8,128)S(1)} %collective-permute-done.1.refs_1_), channel_id=1, source_target_pairs={{0,8},{1,25},{2,10},{3,27},{4,12},{5,29},{6,14},{7,31},{8,16},{9,1... | collective-permute-start | bytes 2174984 | tf_op jit(solution)/shard_map/ppermute | solution.py:70
  45.9 11.7 %collective-permute-start.5 = (f32[1416,128]{1,0:T(8,128)S(1)}, f32[1416,128]{1,0:T(8,128)S(1)}, u32[]{:S(2)}, u32[]{:S(2)}) collective-permute-start(f32[1416,128]{1,0:T(8,128)S(1)} %collective-permute-done.4.refs_5_), channel_id=1, source_target_pairs={{0,32},{1,97},{2,34},{3,99},{4,36},{5,101},{6,38},{7,103},{8,40},{... | collective-permute-start | bytes 2174984 | tf_op jit(solution)/shard_map/ppermute | solution.py:70
  54.2 11.7 %collective-permute-start.3 = (f32[1416,128]{1,0:T(8,128)S(1)}, f32[1416,128]{1,0:T(8,128)S(1)}, u32[]{:S(2)}, u32[]{:S(2)}) collective-permute-start(f32[1416,128]{1,0:T(8,128)S(1)} %collective-permute-done.2.refs_2_), channel_id=1, source_target_pairs={{0,8},{1,25},{2,10},{3,27},{4,12},{5,29},{6,14},{7,31},{8,16},{9,1... | collective-permute-start | bytes 2174984 | tf_op jit(solution)/shard_map/ppermute | solution.py:70
  57.6 10.8 %collective-permute-start.6 = (f32[1416,128]{1,0:T(8,128)S(1)}, f32[1416,128]{1,0:T(8,128)S(1)}, u32[]{:S(2)}, u32[]{:S(2)}) collective-permute-start(f32[1416,128]{1,0:T(8,128)S(1)} %collective-permute-done.5.refs_6_), channel_id=1, source_target_pairs={{0,32},{1,97},{2,34},{3,99},{4,36},{5,101},{6,38},{7,103},{8,40},{... | collective-permute-start | bytes 2174984 | tf_op jit(solution)/shard_map/ppermute | solution.py:70
  75.7 14.2 %collective-permute-start.10 = (f32[2056,128]{1,0:T(8,128)S(1)}, f32[2056,128]{1,0:T(8,128)S(1)}, u32[]{:S(2)}, u32[]{:S(2)}) collective-permute-start(f32[2056,128]{1,0:T(8,128)S(1)} %get-tuple-element.44.refs_6_), channel_id=1, source_target_pairs={{0,8},{1,25},{2,10},{3,27},{4,12},{5,29},{6,14},{7,31},{8,16},{9,1... | collective-permute-start | bytes 3158024 | tf_op jit(solution)/shard_map/ppermute | solution.py:70
  77.2 15.3 %collective-permute-start.7 = (f32[2056,128]{1,0:T(8,128)S(1)}, f32[2056,128]{1,0:T(8,128)S(1)}, u32[]{:S(2)}, u32[]{:S(2)}) collective-permute-start(f32[2056,128]{1,0:T(8,128)S(1)} %get-tuple-element.43.refs_4_), channel_id=1, source_target_pairs={{0,32},{1,97},{2,34},{3,99},{4,36},{5,101},{6,38},{7,103},{8,40},{... | collective-permute-start | bytes 3158024 | tf_op jit(solution)/shard_map/ppermute | solution.py:70
  79.7 23.0 %collective-permute-start.20 = (f32[2048,128]{1,0:T(8,128)S(1)}, f32[2048,128]{1,0:T(8,128)S(1)}, u32[]{:S(2)}, u32[]{:S(2)}) collective-permute-start(f32[2048,128]{1,0:T(8,128)S(1)} %get-tuple-element.45.refs_5_), channel_id=1, source_target_pairs={{0,32},{1,97},{2,34},{3,99},{4,36},{5,101},{6,38},{7,103},{8,40},{... | collective-permute-start | bytes 3145736 | tf_op jit(solution)/shard_map/ppermute | solution.py:70
  79.8 26.4 %collective-permute-start.23 = (f32[2048,128]{1,0:T(8,128)S(1)}, f32[2048,128]{1,0:T(8,128)S(1)}, u32[]{:S(2)}, u32[]{:S(2)}) collective-permute-start(f32[2048,128]{1,0:T(8,128)S(1)} %get-tuple-element.46.refs_7_), channel_id=1, source_target_pairs={{0,8},{1,25},{2,10},{3,27},{4,12},{5,29},{6,14},{7,31},{8,16},{9,1... | collective-permute-start | bytes 3145736 | tf_op jit(solution)/shard_map/ppermute | solution.py:70
  79.9 48.8 %collective-permute-start.19 = (f32[4616,128]{1,0:T(8,128)S(1)}, f32[4616,128]{1,0:T(8,128)}, u32[]{:S(2)}, u32[]{:S(2)}) collective-permute-start(f32[4616,128]{1,0:T(8,128)S(1)} %collective-permute-done.18.refs_2_), channel_id=1, source_target_pairs={{0,2},{1,7},{2,4},{3,1},{4,6},{5,3},{6,0},{7,5},{8,10},{9,15},{10,... | collective-permute-start | bytes 7090184 | tf_op jit(solution)/shard_map/ppermute | solution.py:70
  89.9 22.4 %collective-permute-start.11 = (f32[2056,128]{1,0:T(8,128)S(1)}, f32[2056,128]{1,0:T(8,128)S(1)}, u32[]{:S(2)}, u32[]{:S(2)}) collective-permute-start(f32[2056,128]{1,0:T(8,128)S(1)} %collective-permute-done.10.refs_10_), channel_id=1, source_target_pairs={{0,8},{1,25},{2,10},{3,27},{4,12},{5,29},{6,14},{7,31},{8,16},{9,1... | collective-permute-start | bytes 3158024 | tf_op jit(solution)/shard_map/ppermute | solution.py:70
  92.5 22.4 %collective-permute-start.8 = (f32[2056,128]{1,0:T(8,128)S(1)}, f32[2056,128]{1,0:T(8,128)S(1)}, u32[]{:S(2)}, u32[]{:S(2)}) collective-permute-start(f32[2056,128]{1,0:T(8,128)S(1)} %collective-permute-done.7.refs_8_), channel_id=1, source_target_pairs={{0,32},{1,97},{2,34},{3,99},{4,36},{5,101},{6,38},{7,103},{8,40},{... | collective-permute-start | bytes 3158024 | tf_op jit(solution)/shard_map/ppermute | solution.py:70
  102.7 22.5 %collective-permute-start.21 = (f32[2048,128]{1,0:T(8,128)S(1)}, f32[2048,128]{1,0:T(8,128)S(1)}, u32[]{:S(2)}, u32[]{:S(2)}) collective-permute-start(f32[2048,128]{1,0:T(8,128)S(1)} %collective-permute-done.20.refs_9_), channel_id=1, source_target_pairs={{0,32},{1,97},{2,34},{3,99},{4,36},{5,101},{6,38},{7,103},{8,40},{... | collective-permute-start | bytes 3145736 | tf_op jit(solution)/shard_map/ppermute | solution.py:70
  106.2 22.4 %collective-permute-start.24 = (f32[2048,128]{1,0:T(8,128)S(1)}, f32[2048,128]{1,0:T(8,128)S(1)}, u32[]{:S(2)}, u32[]{:S(2)}) collective-permute-start(f32[2048,128]{1,0:T(8,128)S(1)} %collective-permute-done.23.refs_11_), channel_id=1, source_target_pairs={{0,8},{1,25},{2,10},{3,27},{4,12},{5,29},{6,14},{7,31},{8,16},{9,1... | collective-permute-start | bytes 3145736 | tf_op jit(solution)/shard_map/ppermute | solution.py:70
  112.3 56.4 %collective-permute-start.12 = (f32[2056,128]{1,0:T(8,128)S(1)}, f32[2056,128]{1,0:T(8,128)S(1)}, u32[]{:S(2)}, u32[]{:S(2)}) collective-permute-start(f32[2056,128]{1,0:T(8,128)S(1)} %collective-permute-done.11.refs_14_), channel_id=1, source_target_pairs={{0,8},{1,25},{2,10},{3,27},{4,12},{5,29},{6,14},{7,31},{8,16},{9,1... | collective-permute-start | bytes 3158024 | tf_op jit(solution)/shard_map/ppermute | solution.py:70
  114.9 54.7 %collective-permute-start.9 = (f32[2056,128]{1,0:T(8,128)S(1)}, f32[2056,128]{1,0:T(8,128)S(1)}, u32[]{:S(2)}, u32[]{:S(2)}) collective-permute-start(f32[2056,128]{1,0:T(8,128)S(1)} %collective-permute-done.8.refs_12_), channel_id=1, source_target_pairs={{0,32},{1,97},{2,34},{3,99},{4,36},{5,101},{6,38},{7,103},{8,40},{... | collective-permute-start | bytes 3158024 | tf_op jit(solution)/shard_map/ppermute | solution.py:70
  125.2 42.4 %collective-permute-start.22 = (f32[2048,128]{1,0:T(8,128)S(1)}, f32[2048,128]{1,0:T(8,128)S(1)}, u32[]{:S(2)}, u32[]{:S(2)}) collective-permute-start(f32[2048,128]{1,0:T(8,128)S(1)} %collective-permute-done.21.refs_13_), channel_id=1, source_target_pairs={{0,32},{1,97},{2,34},{3,99},{4,36},{5,101},{6,38},{7,103},{8,40},{... | collective-permute-start | bytes 3145736 | tf_op jit(solution)/shard_map/ppermute | solution.py:70
  128.6 39.0 %collective-permute-start.25 = (f32[2048,128]{1,0:T(8,128)S(1)}, f32[2048,128]{1,0:T(8,128)S(1)}, u32[]{:S(2)}, u32[]{:S(2)}) collective-permute-start(f32[2048,128]{1,0:T(8,128)S(1)} %collective-permute-done.24.refs_15_), channel_id=1, source_target_pairs={{0,8},{1,25},{2,10},{3,27},{4,12},{5,29},{6,14},{7,31},{8,16},{9,1... | collective-permute-start | bytes 3145736 | tf_op jit(solution)/shard_map/ppermute | solution.py:70
  196.5 28.3 %collective-permute-start.26 = (f32[32,128,128]{2,1,0:T(8,128)S(1)}, f32[32,128,128]{2,1,0:T(8,128)S(1)}, u32[]{:S(2)}, u32[]{:S(2)}) collective-permute-start(f32[32,128,128]{2,1,0:T(8,128)S(1)} %get-tuple-element.48), channel_id=1, source_target_pairs={{0,1},{1,0},{2,3},{3,2},{4,5},{5,4},{6,7},{7,6},{8,9},{9,8},{10,11... | collective-permute-start | bytes 6291464 | tf_op jit(solution)/shard_map/ppermute | solution.py:468
  213.0 3.2 %collective-permute-start.15 = (f32[1]{0:T(128)}, f32[1]{0:T(128)}, u32[]{:S(2)}, u32[]{:S(2)}) collective-permute-start(f32[1]{0:T(128)} %max.48), channel_id=1, source_target_pairs={{0,2},{1,7},{2,4},{3,1},{4,6},{5,3},{6,0},{7,5},{8,10},{9,15},{10,... | collective-permute-start | bytes 20 | tf_op jit(solution)/shard_map/ppermute | solution.py:70
  216.8 7.4 %collective-permute-start.16 = (f32[1]{0:T(128)}, f32[1]{0:T(128)}, u32[]{:S(2)}, u32[]{:S(2)}) collective-permute-start(f32[1]{0:T(128)} %max.49), channel_id=1, source_target_pairs={{0,1},{1,0},{2,3},{3,2},{4,5},{5,4},{6,7},{7,6},{8,9},{9,8},{10,11... | collective-permute-start | bytes 20 | tf_op jit(solution)/shard_map/ppermute | solution.py:467
  (20 other events, 561.4 us)

commit v2 on v0

v2 whole, which is shorter than its diff:
```python
import functools

import jax
import jax.numpy as jnp
from jax import lax
from jax.experimental import pallas as pl
from jax.experimental.pallas import tpu as pltpu
from jax.sharding import PartitionSpec as P

BS = 128
HDR = 8
COUNT = 127
FLAG = 126
L_CAP = 36
R_PART = 6
R_HALF = 2 * R_PART
PARCEL = HDR + R_PART * BS
G_LATE = 4
HEADS = 4 * HDR
GROUP = HEADS + (2 * R_PART + G_LATE) * BS
MERGE_COST = 70
UNROLL = 8
AXES = ("row", "col", "layer")
F32 = jnp.float32
BF16 = jnp.bfloat16


def dense(left_blocks, left_pattern, right_blocks, right_pattern, keep_mask, owner):
    def spread(pattern):
        wide = jnp.repeat(jnp.repeat(pattern, BS, axis=0), BS, axis=1)
        return wide.astype(F32)

    left_eff = left_blocks[0] * spread(left_pattern[0])
    right_eff = right_blocks[0] * spread(right_pattern[0])
    row, col = lax.axis_index("row"), lax.axis_index("col")
    way = 1 - 2 * lax.axis_index("layer")
    left_all = jnp.zeros((4 * BS, 64 * BS), F32)
    for step, part in enumerate(hops(left_eff, "z")):
        start = ((col - step * way) & 3) * (16 * BS)
        left_all = lax.dynamic_update_slice(left_all, part, (0, start))
    total = jnp.zeros((4 * BS, 8 * BS), F32)
    for step_x, along_x in enumerate(hops(right_eff, "x")):
        for step_y, part in enumerate(hops(along_x, "y")):
            origin = (((row >> 2) - step_y * way) & 3) * 4 + (((row & 3) - step_x * way) & 3)
            columns = lax.dynamic_slice(left_all, (0, origin * (4 * BS)), (4 * BS, 4 * BS))
            total = total + jnp.dot(columns, part, preferred_element_type=F32, precision=lax.Precision.HIGHEST)
    tiles = total.reshape(4, BS, 8, BS).transpose(0, 2, 1, 3).reshape(32, BS, BS)
    tiles = tiles * keep_mask[0, 0].astype(F32)[:, None, None]
    tiles = tiles + swap(tiles)
    owners = owner[0, 0, :, 0]
    onehot = (owners[:, None] == jnp.arange(2, dtype=jnp.int32)[None, :]).astype(jnp.int32)
    before = jnp.cumsum(onehot, axis=0) - onehot
    slot = owners * 32 + jnp.sum(before * onehot, axis=1)
    wanted = lax.axis_index("layer") * 32 + jnp.arange(32, dtype=jnp.int32)
    pick = (slot[None, :] == wanted[:, None]).astype(F32)
    return jnp.einsum("st,tab->sab", pick, tiles, precision=lax.Precision.HIGHEST)


def swap(array):
    return lax.ppermute(array, "layer", [(0, 1), (1, 0)])


def ring(array, axis, distance=1):
    pairs = []
    for y in range(4):
        for x in range(4):
            for z in range(4):
                for core in range(2):
                    to = {"y": y, "x": x, "z": z}
                    to[axis] = (to[axis] + distance * (1 - 2 * core)) % 4
                    source = ((y * 4 + x) * 4 + z) * 2 + core
                    target = ((to["y"] * 4 + to["x"]) * 4 + to["z"]) * 2 + core
                    pairs.append((source, target))
    return lax.ppermute(array, AXES, pairs)


def hops(array, axis, number=3):
    out = [array]
    for _ in range(number):
        out.append(ring(out[-1], axis))
    return out


def block_rows(slot, head=HDR):
    return pl.ds(pl.multiple_of(head + slot * BS, 8), BS)


def blank():
    return jnp.zeros((HDR, BS), F32)


def place(header, lane, value):
    lanes = lax.broadcasted_iota(jnp.int32, (HDR, BS), 1)
    return jnp.where(lanes == lane, value, header)


def pack_kernel(lpat, rpat, left, right, a_early, b_early, a_late, b_late, l_out, codes, lcodes, head, lhead, sems, lsems, hsems):
    row = lax.axis_index("row")
    flip = row & 1
    base = lax.axis_index("col") * 64

    def scan(i, n):
        codes[n] = i
        return n + rpat[0, i >> 3, i & 7]

    n = lax.fori_loop(0, 32, scan, jnp.int32(0))
    m = jnp.minimum(n, 2 * R_HALF)

    def start(s, headers):
        in_a = ((s + flip) & 1) == 0
        code = codes[s]
        slot = s >> 1
        source = right.at[0, pl.ds(pl.multiple_of((code >> 3) * BS, BS), BS), pl.ds(pl.multiple_of((code & 7) * BS, BS), BS)]
        which = jnp.where(in_a, 0, 1) + jnp.where(slot < R_PART, 0, 2)
        rows = block_rows(jnp.where(slot < R_PART, slot, slot - R_PART))
        for i, out in enumerate((a_early, b_early, a_late, b_late)):

            @pl.when(which == i)
            def _(out=out):
                pltpu.make_async_copy(source, out.at[rows], sems.at[s]).start()

        value = (row * 32 + code).astype(F32)
        return (
            place(headers[0], jnp.where(in_a, slot, -1), value),
            place(headers[1], jnp.where(in_a, -1, slot), value),
        )

    header_a, header_b = lax.fori_loop(0, m, start, (blank(), blank()))

    def scan_left(i, n):
        lcodes[n] = i
        return n + lpat[0, i & 3, i >> 2]

    n_left = lax.fori_loop(0, 64, scan_left, jnp.int32(0))
    m_left = jnp.minimum(n_left, L_CAP)

    def start_left(s, header):
        code = lcodes[s]
        source = left.at[0, pl.ds(pl.multiple_of((code & 3) * BS, BS), BS), pl.ds(pl.multiple_of((code >> 2) * BS, BS), BS)]
        pltpu.make_async_copy(source, l_out.at[block_rows(s)], lsems.at[s]).start()
        return place(header, s, (base + code).astype(F32))

    header_l = lax.fori_loop(0, m_left, start_left, blank())
    flag = ((n > 2 * R_HALF) | (n_left > L_CAP)).astype(F32)
    count_a = (m + 1 - flip) >> 1
    head[0] = place(place(header_a, COUNT, count_a.astype(F32)), FLAG, flag)
    head[1] = place(place(header_b, COUNT, (m - count_a).astype(F32)), FLAG, flag)
    lhead[...] = place(header_l, COUNT, m_left.astype(F32))
    copies = [
        pltpu.make_async_copy(head.at[0], a_early.at[pl.ds(0, HDR)], hsems.at[0]),
        pltpu.make_async_copy(head.at[1], b_early.at[pl.ds(0, HDR)], hsems.at[1]),
        pltpu.make_async_copy(lhead, l_out.at[pl.ds(0, HDR)], hsems.at[2]),
    ]
    for copy in copies:
        copy.start()

    def finish(s, _):
        pltpu.make_async_copy(right.at[0, pl.ds(0, BS), pl.ds(0, BS)], a_early.at[block_rows(0)], sems.at[s]).wait()
        return 0

    def finish_left(s, _):
        pltpu.make_async_copy(left.at[0, pl.ds(0, BS), pl.ds(0, BS)], l_out.at[block_rows(0)], lsems.at[s]).wait()
        return 0

    lax.fori_loop(0, m, finish, 0)
    lax.fori_loop(0, m_left, finish_left, 0)
    for copy in copies:
        copy.wait()


def merge_kernel(*refs):
    early, late = (refs[0:4], refs[4:8]), (refs[8:12], refs[12:16])
    outs = (refs[16:18], refs[18:20])
    seen, sems, lsems, hsems = refs[20:]
    reads = []
    copies = []
    for half in range(2):
        for i in range(4):
            head = early[half][i].at[pl.ds(0, HDR)]
            reads.append(pltpu.make_async_copy(head, seen.at[half, i], hsems.at[half * 8 + i]))
            reads[-1].start()
            copies.append(pltpu.make_async_copy(head, outs[half][0].at[pl.ds(i * HDR, HDR)], hsems.at[half * 8 + 4 + i]))
            rows = pl.ds(HEADS + (i % 2) * R_PART * BS, R_PART * BS)
            source = early[half][i].at[pl.ds(HDR, R_PART * BS)]
            copies.append(pltpu.make_async_copy(source, outs[half][i // 2].at[rows], sems.at[half * 4 + i]))
    for copy in copies:
        copy.start()
    for read in reads:
        read.wait()
    totals = []
    for half in range(2):
        total = jnp.int32(0)
        for i in range(4):
            count = seen[half, i, 0, COUNT].astype(jnp.int32)

            def start(s, g, half=half, i=i):
                source = late[half][i].at[block_rows(s - R_PART)]
                for j in range(2):

                    @pl.when((g >= j * G_LATE) & (g < (j + 1) * G_LATE))
                    def _(j=j):
                        rows = block_rows(2 * R_PART + g - j * G_LATE, HEADS)
                        pltpu.make_async_copy(source, outs[half][j].at[rows], lsems.at[half, g]).start()

                return g + 1

            total = lax.fori_loop(R_PART, count, start, total)
        totals.append(jnp.minimum(total, 2 * G_LATE))
    for half in range(2):

        def finish(s, _, half=half):
            pltpu.make_async_copy(late[half][0].at[block_rows(0)], outs[half][0].at[block_rows(0, HEADS)], lsems.at[half, s]).wait()
            return 0

        lax.fori_loop(0, totals[half], finish, 0)
    for copy in copies:
        copy.wait()


def flag_kernel(*refs):
    groups, out, heads, sems = refs[0:8], refs[9], refs[10], refs[11]
    copies = []
    for g in range(8):
        copies.append(pltpu.make_async_copy(groups[g].at[pl.ds(0, HEADS)], heads.at[g], sems.at[g]))
        copies[-1].start()
    for copy in copies:
        copy.wait()
    worst = blank()
    most = blank()
    for g in range(8):
        late = blank()
        for i in range(4):
            header = heads[g, i * HDR : (i + 1) * HDR]
            worst = jnp.maximum(worst, header)
            late = late + jnp.maximum(header - R_PART, 0.0)
        most = jnp.maximum(most, late)
    first = lax.broadcasted_iota(jnp.int32, (HDR, BS), 0) == 0
    lanes = lax.broadcasted_iota(jnp.int32, (HDR, BS), 1)
    over = first & (((lanes == FLAG) & (worst > 0.5)) | ((lanes == COUNT) & (most > 2 * G_LATE + 0.5)))
    out[...] = jnp.full((HDR, BS), jnp.max(jnp.where(over, 1.0, 0.0)))


def split(block):
    high = block.astype(BF16)
    low = (block - high.astype(F32)).astype(BF16)
    return jnp.concatenate([high, low], axis=1)


def hold_kernel(step, *refs):
    packed_ref, held, sem = refs[0], refs[-2], refs[-1]
    rows = pl.ds(step * L_CAP * BS, L_CAP * BS)
    copy = pltpu.make_async_copy(packed_ref.at[pl.ds(HDR, L_CAP * BS)], held.at[rows], sem)
    copy.start()
    if step == 0:
        held[pl.ds(4 * L_CAP * BS, BS)] = jnp.zeros((BS, BS), F32)
    copy.wait()


def hold(packed_left, step, held=None, after=()):
    shape = jax.ShapeDtypeStruct(((4 * L_CAP + 1) * BS, BS), F32)
    return pl.pallas_call(
        functools.partial(hold_kernel, step),
        out_shape=shape,
        in_specs=[HBM] + ([] if held is None else [VMEM]) + [ANY] * len(after),
        out_specs=VMEM,
        input_output_aliases={} if held is None else {1: 0},
        scratch_shapes=[pltpu.SemaphoreType.DMA],
        compiler_params=params(1),
    )(packed_left, *([] if held is None else [held]), *after)


def multiply_kernel(n_left, lows, halves, begin, final, *refs):
    refs = list(refs)
    number = len(lows)
    keep, lv = refs.pop(0), refs.pop(0)
    lefts = [refs.pop(0) for _ in range(n_left)]
    parts = [[refs.pop(0) if j == 0 or j in halves else None for j in range(2)] for _ in range(number)]
    if not begin:
        refs.pop(0)
    if final:
        owner, flag_in = refs.pop(0), refs.pop(0)
    acc = refs.pop(0)
    if final:
        mine, send = refs.pop(0), refs.pop(0)
    rv, lhead, rhead, table, work, rsems, hsems = refs
    heads = []
    for i in range(n_left):
        heads.append(pltpu.make_async_copy(lefts[i].at[pl.ds(0, HDR)], lhead.at[i], hsems.at[i]))
    for g in range(number):
        for i in range(4):
            heads.append(pltpu.make_async_copy(parts[g][0].at[pl.ds(i * HDR, HDR)], rhead.at[g, i], hsems.at[4 + g * 4 + i]))
    for copy in heads:
        copy.start()
    loads = []
    for g in range(number):
        for n, j in enumerate(halves):
            rows = pl.ds((g * len(halves) + n) * GROUP, GROUP)
            loads.append(pltpu.make_async_copy(parts[g][j], rv.at[rows], rsems.at[g * len(halves) + n]))
    for copy in loads:
        copy.start()
    if begin:
        acc[...] = jnp.zeros(acc.shape, F32)
    no_left, no_right = 4 * L_CAP, number * len(halves) * GROUP
    rv[pl.ds(no_right, BS)] = jnp.zeros((BS, BS), F32)

    def clear(i, _):
        for j in range(8):
            table[i * 8 + j] = no_left
        return 0

    lax.fori_loop(0, 32, clear, 0)
    for copy in heads:
        copy.wait()
    for i in range(n_left):

        def enter(s, _, i=i):
            table[lhead[i, 0, s].astype(jnp.int32)] = i * L_CAP + s
            return 0

        lax.fori_loop(0, lhead[i, 0, COUNT].astype(jnp.int32), enter, 0)
    pairs = jnp.int32(0)

    def note(code, at, n, low):
        k4 = (code >> 3) * 4
        c = code & 7
        for r in range(4):
            slot = table[k4 + r]
            work[n] = (slot << 20) | (at << 5) | (r * 8 + c)
            n = n + jnp.where((slot >= low * L_CAP) & (slot < no_left), keep[0, 0, r * 8 + c], 0)
        return n

    for g in range(number):
        late = jnp.int32(0)
        for i in range(4):
            count = rhead[g, i, 0, COUNT].astype(jnp.int32)
            if i // 2 in halves:
                first = ((g * len(halves) + halves.index(i // 2)) * GROUP + HEADS + (i % 2) * R_PART * BS) // 8

                def early_one(s, n, g=g, i=i, first=first):
                    return note(rhead[g, i, 0, s].astype(jnp.int32), first + s * (BS // 8), n, lows[g])

                pairs = lax.fori_loop(0, jnp.minimum(count, R_PART), early_one, pairs)
            low = min(halves) * G_LATE
            first = (g * len(halves) * GROUP + HEADS + 2 * R_PART * BS) // 8

            def late_one(s, state, g=g, i=i, low=low, first=first):
                n, at = state
                place_of = jnp.clip(at - low, 0, len(halves) * G_LATE - 1)
                place_of = first + (place_of // G_LATE) * (GROUP // 8) + (place_of % G_LATE) * (BS // 8)
                after = note(rhead[g, i, 0, s].astype(jnp.int32), place_of, n, lows[g])
                inside = (at >= low) & (at < low + len(halves) * G_LATE)
                return jnp.where(inside, after, n), at + 1

            pairs, late = lax.fori_loop(R_PART, count, late_one, (pairs, late))
    for j in range(UNROLL):
        work[pairs + j] = (no_left << 20) | (no_right // 8 << 5)

    for copy in loads:
        copy.wait()

    def step(w, _):
        results = []
        for j in range(UNROLL):
            entry = work[w * UNROLL + j]
            left = split(lv[block_rows(entry >> 20, 0)])
            right = split(rv[pl.ds(pl.multiple_of(((entry >> 5) & 32767) * 8, 8), BS)])
            result = jnp.dot(left, jnp.concatenate([right, right], axis=0), preferred_element_type=F32)
            results.append((entry & 31, result[:, :BS] + result[:, BS:]))
        for tile, result in results:
            acc[tile] += result
        return 0

    lax.fori_loop(0, (pairs + UNROLL - 1) // UNROLL, step, 0)

    if final:
        me = lax.axis_index("layer")
        mine[...] = jnp.zeros(mine.shape, F32)
        send[...] = jnp.zeros(send.shape, F32)
        counts = [jnp.int32(0), jnp.int32(0)]
        for t in range(32):
            who = owner[0, 0, t]
            slot = jnp.where(who == 0, counts[0], counts[1])

            @pl.when(who == me)
            def _(t=t, slot=slot):
                mine[slot] = acc[t]

            @pl.when(who != me)
            def _(t=t, slot=slot):
                send[slot] = acc[t]

            counts[0] = counts[0] + (who == 0).astype(jnp.int32)
            counts[1] = counts[1] + (who != 0).astype(jnp.int32)


ANY = pl.BlockSpec(memory_space=pl.ANY)
SMEM = pl.BlockSpec(memory_space=pltpu.SMEM)
VMEM = pl.BlockSpec(memory_space=pltpu.VMEM)
HBM = pl.BlockSpec(memory_space=pltpu.HBM)


def params(mebibytes):
    return pltpu.CompilerParams(vmem_limit_bytes=int(mebibytes * 2**20))


def packed(blocks, head=HDR):
    return jax.ShapeDtypeStruct((head + blocks * BS, BS), F32)


def multiply(micros, keep, held, lefts, parts, lows, halves, acc=None, owner=None, flag=None):
    begin, final = acc is None, owner is not None
    number = len(parts)
    arrays = [part[j] for part in parts for j in range(2) if j == 0 or j in halves]
    operands = [keep, held, *lefts, *arrays]
    specs = [SMEM, VMEM] + [HBM] * (len(lefts) + len(arrays))
    aliases = {}
    if not begin:
        aliases = {len(operands): 0}
        operands.append(acc)
        specs.append(VMEM)
    if final:
        operands += [owner, flag]
        specs += [SMEM, VMEM]
    return pl.pallas_call(
        functools.partial(multiply_kernel, len(lefts), lows, halves, begin, final),
        out_shape=[jax.ShapeDtypeStruct((32, BS, BS), F32)] * (3 if final else 1),
        in_specs=specs,
        out_specs=[VMEM] * (3 if final else 1),
        input_output_aliases=aliases,
        scratch_shapes=[
            pltpu.VMEM((number * len(halves) * GROUP + BS, BS), F32),
            pltpu.SMEM((4, HDR, BS), F32),
            pltpu.SMEM((number, 4, HDR, BS), F32),
            pltpu.SMEM((256,), jnp.int32),
            pltpu.SMEM((number * 4 * R_HALF * 4 + UNROLL,), jnp.int32),
            pltpu.SemaphoreType.DMA((2 * number,)),
            pltpu.SemaphoreType.DMA((4 + 4 * number,)),
        ],
        compiler_params=params(4 + 1.1 * len(halves) * number),
        cost_estimate=pl.CostEstimate(flops=0, bytes_accessed=int(micros * 3.6e6), transcendentals=0),
    )(*operands)


def fence(arrays, after):
    shapes = [jax.ShapeDtypeStruct(array.shape, F32) for array in arrays]

    def nothing(*refs):
        pass

    return pl.pallas_call(
        nothing,
        out_shape=shapes,
        in_specs=[HBM] * len(arrays) + [ANY] * len(after),
        out_specs=[HBM] * len(arrays),
        input_output_aliases={i: i for i in range(len(arrays))},
        compiler_params=params(1),
    )(*arrays, *after)


def add_kernel(mine, other, out, total, sems):
    copies = []
    for i in range(4):
        rows = pl.ds(i * 8, 8)
        total[rows] = mine[rows] + other[rows]
        copies.append(pltpu.make_async_copy(total.at[rows], out.at[0, 0, rows], sems.at[i]))
        copies[-1].start()
    for copy in copies:
        copy.wait()


def add(mine, other):
    return pl.pallas_call(
        add_kernel,
        out_shape=jax.ShapeDtypeStruct((1, 1, 32, BS, BS), F32),
        in_specs=[VMEM, VMEM],
        out_specs=HBM,
        scratch_shapes=[pltpu.VMEM((32, BS, BS), F32), pltpu.SemaphoreType.DMA((4,))],
        compiler_params=params(8),
    )(mine, other)


def local(left_blocks, left_pattern, right_blocks, right_pattern, keep_mask, owner):
    early_a, early_b, late_a, late_b, packed_left = pl.pallas_call(
        pack_kernel,
        out_shape=[packed(R_PART)] * 4 + [packed(L_CAP)],
        in_specs=[SMEM, SMEM, HBM, HBM],
        out_specs=[HBM] * 5,
        scratch_shapes=[
            pltpu.SMEM((33,), jnp.int32),
            pltpu.SMEM((65,), jnp.int32),
            pltpu.VMEM((2, HDR, BS), F32),
            pltpu.VMEM((HDR, BS), F32),
            pltpu.SemaphoreType.DMA((2 * R_HALF,)),
            pltpu.SemaphoreType.DMA((L_CAP,)),
            pltpu.SemaphoreType.DMA((3,)),
        ],
        compiler_params=params(1),
    )(left_pattern, right_pattern, left_blocks, right_blocks)
    early_a, early_b = hops(early_a, "x"), hops(early_b, "y")
    late_a, late_b = hops(late_a, "x"), hops(late_b, "y")
    lefts = hops(packed_left, "z", 1)
    (lefts[1],) = fence([lefts[1]], [early_a[3], early_b[3], late_a[3], late_b[3]])
    lefts += hops(lefts[1], "z", 2)[1:]
    array = jax.ShapeDtypeStruct((GROUP, BS), F32)
    merged = pl.pallas_call(
        merge_kernel,
        out_shape=[array] * 4,
        in_specs=[HBM] * 16,
        out_specs=[HBM] * 4,
        scratch_shapes=[
            pltpu.SMEM((2, 4, HDR, BS), F32),
            pltpu.SemaphoreType.DMA((8,)),
            pltpu.SemaphoreType.DMA((2, 2 * G_LATE)),
            pltpu.SemaphoreType.DMA((16,)),
        ],
        compiler_params=params(1),
        cost_estimate=pl.CostEstimate(flops=0, bytes_accessed=int(MERGE_COST * 3.6e6), transcendentals=0),
    )(*early_a, *early_b, *late_a, *late_b)
    a0, b0 = hops(merged[0], "y"), hops(merged[2], "x")
    a1, b1 = hops(merged[1], "y", 2), hops(merged[3], "x", 2)
    parts = [(a0[0], a1[0]), (b0[0], b1[0]), (a0[1], a1[1]), (b0[1], b1[1])]
    held = hold(lefts[0], 0)
    held = hold(lefts[1], 1, held)
    held = hold(lefts[2], 2, held)
    (acc,) = multiply(9, keep_mask, held, lefts[:3], parts, (0,) * 4, (0, 1))
    held = hold(lefts[3], 3, held, [acc])
    a1[2], b1[2] = fence([a1[2], b1[2]], [acc])
    a1.append(ring(a1[2], "y"))
    b1.append(ring(b1[2], "x"))
    parts += [(a0[2], a1[2]), (b0[2], b1[2])]
    (acc,) = multiply(9, keep_mask, held, lefts, parts, (3,) * 4 + (0,) * 2, (0, 1), acc)
    flag = pl.pallas_call(
        flag_kernel,
        out_shape=jax.ShapeDtypeStruct((HDR, BS), F32),
        in_specs=[HBM] * 8 + [ANY],
        out_specs=VMEM,
        scratch_shapes=[pltpu.VMEM((8, HEADS, BS), F32), pltpu.SemaphoreType.DMA((8,))],
        compiler_params=params(1),
    )(*a0, *b0, acc)
    flag = functools.reduce(jnp.maximum, [flag] + [ring(flag, "z", distance) for distance in (1, 2, 3)])
    last = [(a0[3], a1[3]), (b0[3], b1[3])]
    (acc,) = multiply(5, keep_mask, held, lefts, last, (0, 0), (0,), acc)
    _, mine, send = multiply(6, keep_mask, held, lefts, last, (0, 0), (1,), acc, owner.reshape(1, 1, 32), flag)
    flag = jnp.maximum(flag, swap(flag))
    return lax.cond(
        flag[0, 0] > 0,
        lambda _: dense(left_blocks, left_pattern, right_blocks, right_pattern, keep_mask, owner)[None, None],
        lambda parts: add(*parts),
        (mine, swap(send)),
    )


def solution(mesh):
    return jax.shard_map(
        local,
        mesh=mesh,
        in_specs=(
            P("layer", "row", "col"),
            P("layer", "row", "col"),
            P("layer", "row", "col"),
            P("layer", "row", "col"),
            P("row", "col", None),
            P("row", "col", None, None),
        ),
        out_specs=P("row", "col", "layer", None, None),
        check_vma=False,
    )
```

time: 463 us -> 136 us (0.29)
  waiting for transfers between devices: 365 us -> 46.1 us
  matrix products: 59.8 us -> 0 us
  starting transfers between devices: 0.27 us -> 49.7 us
  Pallas kernels: 0 us -> 35 us
  between operations: 13.2 us -> 0.93 us
  other arithmetic: 9.08 us -> 0.01 us
  local copies, waits for them, and re-layouts: 10.3 us -> 4 us
  blocking collectives: 5.19 us -> 0 us
    all_gather x2 -> x0, waiting for transfers between devices: 353 us -> none  [the longest x1 200 us: local(): right_all = lax.all_gather(right_eff, 'row', axis=0, tiled=True)]
    dot_general x2 -> x0, matrix products: 59.8 us -> none  [the longest x1 58.6 us: local(): jnp.dot(lax.all_gather(left_eff, 'col', axis=1, tiled=True), right_all, p...]
    ppermute x0 -> x32, starting transfers between devices: none -> 49.7 us  [the longest x30 47.8 us: ring(): return lax.ppermute(array, AXES, pairs)]
    ppermute x0 -> x32, waiting for transfers between devices: none -> 46.1 us  [the longest x30 42.4 us: ring(): return lax.ppermute(array, AXES, pairs)]
    pallas_call x0 -> x14, Pallas kernels: none -> 35 us  [the longest x4 27.9 us: multiply(): pl.pallas_call(functools.partial(multiply_kernel, len(lefts), lows, halve...]
    reduce_scatter x1 -> x0, waiting for transfers between devices: 11.7 us -> none  [local(): share = lax.psum_scatter(tiles, 'layer', scatter_dimension=0, tiled=True)]
    mul x4 -> x0, other arithmetic: 8.07 us -> none  [the longest x1 4.31 us: local(): left_eff = left_blocks[0] * spread(left_pattern[0])]
    all_to_all x1 -> x0, blocking collectives: 5.19 us -> none  [local(): lax.all_to_all(outgoing, 'layer', split_axis=0, concat_axis=0, tiled=True)]
  transfers between devices with their start and end apart: 3 -> 32, of which waited for: 3 -> 11; matrix products, arithmetic and copies ran while one was open for 1% -> 0% of each run, Pallas kernels for 0% -> 19%
where the time goes in v2:
time: 136 us
  starting transfers between devices  49.7 us (37%)
  waiting for transfers between devices  46.1 us (34%)
  Pallas kernels  35 us (26%)
  local copies, waits for them, and re-layouts  4 us (3%)
    ppermute x30, starting transfers between devices, ring(): return lax.ppermute(array, AXES, pairs)  47.8 us
    ppermute x30, waiting for transfers between devices, ring(): return lax.ppermute(array, AXES, pairs)  42.4 us
    pallas_call x4, Pallas kernels, multiply(): pl.pallas_call(functools.partial(multiply_kernel, len(lefts), lows, halve...  27.9 us
    ppermute x2, waiting for transfers between devices, swap(): return lax.ppermute(array, 'layer', [(0, 1), (1, 0)])  3.7 us
    unnamed x22, local copies, waits for them, and re-layouts  3.49 us
    pallas_call x1, Pallas kernels, local(): pl.pallas_call(pack_kernel, out_shape=[packed(R_PART)] * 4 + [packed(L_CA...  3.43 us
  transfers between devices with their start and end apart: 32, of which 11 were waited for; matrix products, arithmetic and copies ran while one was open for 0% of the time, Pallas kernels for 19%

profile of v2, /device:TPU:1, one launch (start us, length us, event | category | flops | bytes accessed | tf_op | source)
XLA Modules:
  0.0 136.0 jit_solution(10935867878893655126)
XLA Ops:
  0.0 3.4 %shard_map.66 = (f32[776,128]{1,0:T(8,128)S(1)}, f32[776,128]{1,0:T(8,128)S(1)}, f32[776,128]{1,0:T(8,128)S(1)}, f32[776,128]{1,0:T(8,128)S(1)}, f32[4616,128]{1,0:T(8,128)S(1)}) custom-call(s32[1,4,16]{2,1,0:T(4,128)} %lpat.1, s32[1,4,8]{2,1,0:T(4,128)} %rpat.1, f32[1,512,2048]{2,1,0:T(8,128)} %left.1, f32[1,512,1024]{2,1,0:T(8,128)} %right.1), custom_call_target="tpu_custom_call" | custom-call | tf_op jit(solution)/shard_map/pallas_call | solution.py:483
  3.4 5.1 %collective-permute-start.37 = (f32[4616,128]{1,0:T(8,128)S(1)}, f32[4616,128]{1,0:T(8,128)S(1)}, u32[]{:S(2)}, u32[]{:S(2)}) collective-permute-start(f32[4616,128]{1,0:T(8,128)S(1)} %get-tuple-element.51.refs_0_.refs_2_), channel_id=1, source_target_pairs={{0,2},{1,7},{2,4},{3,1},{4,6},{5,3},{6,0},{7,5},{8,10},{9,15},{10,... | collective-permute-start | bytes 7090184 | tf_op jit(solution)/shard_map/ppermute | solution.py:74
  8.6 2.2 %collective-permute-start.19 = (f32[776,128]{1,0:T(8,128)S(1)}, f32[776,128]{1,0:T(8,128)S(1)}, u32[]{:S(2)}, u32[]{:S(2)}) collective-permute-start(f32[776,128]{1,0:T(8,128)S(1)} %get-tuple-element.45.refs_0_), channel_id=1, source_target_pairs={{0,8},{1,25},{2,10},{3,27},{4,12},{5,29},{6,14},{7,31},{8,16},{9,1... | collective-permute-start | bytes 1191944 | tf_op jit(solution)/shard_map/ppermute | solution.py:74
  10.8 2.7 %collective-permute-start.22 = (f32[776,128]{1,0:T(8,128)S(1)}, f32[776,128]{1,0:T(8,128)S(1)}, u32[]{:S(2)}, u32[]{:S(2)}) collective-permute-start(f32[776,128]{1,0:T(8,128)S(1)} %get-tuple-element.46.refs_4_), channel_id=1, source_target_pairs={{0,32},{1,97},{2,34},{3,99},{4,36},{5,101},{6,38},{7,103},{8,40},{... | collective-permute-start | bytes 1191944 | tf_op jit(solution)/shard_map/ppermute | solution.py:74
  15.6 3.4 %collective-permute-start.20 = (f32[776,128]{1,0:T(8,128)S(1)}, f32[776,128]{1,0:T(8,128)S(1)}, u32[]{:S(2)}, u32[]{:S(2)}) collective-permute-start(f32[776,128]{1,0:T(8,128)S(1)} %collective-permute-done.19.refs_1_), channel_id=1, source_target_pairs={{0,8},{1,25},{2,10},{3,27},{4,12},{5,29},{6,14},{7,31},{8,16},{9,1... | collective-permute-start | bytes 1191944 | tf_op jit(solution)/shard_map/ppermute | solution.py:74
  19.0 2.7 %collective-permute-start.23 = (f32[776,128]{1,0:T(8,128)S(1)}, f32[776,128]{1,0:T(8,128)S(1)}, u32[]{:S(2)}, u32[]{:S(2)}) collective-permute-start(f32[776,128]{1,0:T(8,128)S(1)} %collective-permute-done.22.refs_5_), channel_id=1, source_target_pairs={{0,32},{1,97},{2,34},{3,99},{4,36},{5,101},{6,38},{7,103},{8,40},{... | collective-permute-start | bytes 1191944 | tf_op jit(solution)/shard_map/ppermute | solution.py:74
  23.2 2.7 %collective-permute-start.29 = (f32[776,128]{1,0:T(8,128)S(1)}, f32[776,128]{1,0:T(8,128)S(1)}, u32[]{:S(2)}, u32[]{:S(2)}) collective-permute-start(f32[776,128]{1,0:T(8,128)S(1)} %collective-permute-done.28.refs_13_), channel_id=1, source_target_pairs={{0,32},{1,97},{2,34},{3,99},{4,36},{5,101},{6,38},{7,103},{8,40},{... | collective-permute-start | bytes 1191944 | tf_op jit(solution)/shard_map/ppermute | solution.py:74
  27.5 2.7 %collective-permute-start.24 = (f32[776,128]{1,0:T(8,128)S(1)}, f32[776,128]{1,0:T(8,128)S(1)}, u32[]{:S(2)}, u32[]{:S(2)}) collective-permute-start(f32[776,128]{1,0:T(8,128)S(1)} %collective-permute-done.23.refs_6_), channel_id=1, source_target_pairs={{0,32},{1,97},{2,34},{3,99},{4,36},{5,101},{6,38},{7,103},{8,40},{... | collective-permute-start | bytes 1191944 | tf_op jit(solution)/shard_map/ppermute | solution.py:74
  31.7 2.7 %collective-permute-start.30 = (f32[776,128]{1,0:T(8,128)S(1)}, f32[776,128]{1,0:T(8,128)S(1)}, u32[]{:S(2)}, u32[]{:S(2)}) collective-permute-start(f32[776,128]{1,0:T(8,128)S(1)} %collective-permute-done.29.refs_14_), channel_id=1, source_target_pairs={{0,32},{1,97},{2,34},{3,99},{4,36},{5,101},{6,38},{7,103},{8,40},{... | collective-permute-start | bytes 1191944 | tf_op jit(solution)/shard_map/ppermute | solution.py:74
  35.3 2.2 %collective-permute-done.27.refs_11_.refs_3_ = f32[776,128]{1,0:T(8,128)S(1)} collective-permute-done((f32[776,128]{1,0:T(8,128)S(1)}, f32[776,128]{1,0:T(8,128)S(1)}, u32[]{:S(2)}, u32[]{:S(2)}) %collective-permute-start.27) | collective-permute-done | bytes 397344 | tf_op jit(solution)/shard_map/ppermute | solution.py:74
  37.5 2.1 %collective-permute-done.30.refs_15_.refs_4_ = f32[776,128]{1,0:T(8,128)S(1)} collective-permute-done((f32[776,128]{1,0:T(8,128)S(1)}, f32[776,128]{1,0:T(8,128)S(1)}, u32[]{:S(2)}, u32[]{:S(2)}) %collective-permute-start.30) | collective-permute-done | bytes 397344 | tf_op jit(solution)/shard_map/ppermute | solution.py:74
  39.7 2.2 %shard_map.67 = (f32[2080,128]{1,0:T(8,128)S(1)}, f32[2080,128]{1,0:T(8,128)S(1)}, f32[2080,128]{1,0:T(8,128)S(1)}, f32[2080,128]{1,0:T(8,128)S(1)}) custom-call(f32[776,128]{1,0:T(8,128)S(1)} %get-tuple-element.45.refs_0_, f32[776,128]{1,0:T(8,128)S(1)} %collective-permute-done.19.refs_1_, f32[776,128]{1,0:T(8,128)S(1)} %collective-permute-done.20.refs_2_, ...), custom_call_target="tpu_custom_call" | custom-call | bytes 252000000 | tf_op jit(solution)/shard_map/pallas_call | solution.py:505
  42.0 3.2 %collective-permute-start.31 = (f32[2080,128]{1,0:T(8,128)S(1)}, f32[2080,128]{1,0:T(8,128)S(1)}, u32[]{:S(2)}, u32[]{:S(2)}) collective-permute-start(f32[2080,128]{1,0:T(8,128)S(1)} %get-tuple-element.49.refs_5_.refs_6_.refs_0_), channel_id=1, source_target_pairs={{0,32},{1,97},{2,34},{3,99},{4,36},{5,101},{6,38},{7,103},{8,40},{... | collective-permute-start | bytes 3194888 | tf_op jit(solution)/shard_map/ppermute | solution.py:74
  46.1 21.5 %collective-permute-done.38.refs_0_.refs_4_ = f32[4616,128]{1,0:T(8,128)S(1)} collective-permute-done((f32[4616,128]{1,0:T(8,128)S(1)}, f32[4616,128]{1,0:T(8,128)S(1)}, u32[]{:S(2)}, u32[]{:S(2)}) %collective-permute-start.38) | collective-permute-done | bytes 2363424 | tf_op jit(solution)/shard_map/ppermute | solution.py:74
  69.0 3.1 %collective-permute-start.32 = (f32[2080,128]{1,0:T(8,128)S(1)}, f32[2080,128]{1,0:T(8,128)S(1)}, u32[]{:S(2)}, u32[]{:S(2)}) collective-permute-start(f32[2080,128]{1,0:T(8,128)S(1)} %collective-permute-done.31.refs_9_.refs_10_.refs_1_), channel_id=1, source_target_pairs={{0,32},{1,97},{2,34},{3,99},{4,36},{5,101},{6,38},{7,103},{8,40},{... | collective-permute-start | bytes 3194888 | tf_op jit(solution)/shard_map/ppermute | solution.py:74
  72.7 11.3 %collective-permute-done.32.refs_14_.refs_2_ = f32[2080,128]{1,0:T(8,128)S(1)} collective-permute-done((f32[2080,128]{1,0:T(8,128)S(1)}, f32[2080,128]{1,0:T(8,128)S(1)}, u32[]{:S(2)}, u32[]{:S(2)}) %collective-permute-start.32) | collective-permute-done | bytes 1064992 | tf_op jit(solution)/shard_map/ppermute | solution.py:74
  84.0 3.4 %collective-permute-start.33 = (f32[2080,128]{1,0:T(8,128)S(1)}, f32[2080,128]{1,0:T(8,128)S(1)}, u32[]{:S(2)}, u32[]{:S(2)}) collective-permute-start(f32[2080,128]{1,0:T(8,128)S(1)} %collective-permute-done.32.refs_14_.refs_2_), channel_id=1, source_target_pairs={{0,32},{1,97},{2,34},{3,99},{4,36},{5,101},{6,38},{7,103},{8,40},{... | collective-permute-start | bytes 3194888 | tf_op jit(solution)/shard_map/ppermute | solution.py:74
  88.7 8.3 %shard_map.72.refs_2_.refs_18_ = f32[32,128,128]{2,1,0:T(8,128)S(1)} custom-call(s32[1,1,32]{2,1,0:T(1,128)S(1)} %copy-done.16, f32[18560,128]{1,0:T(8,128)S(1)} %shard_map.71.refs_1_, f32[4616,128]{1,0:T(8,128)S(1)} %get-tuple-element.51.refs_0_.refs_2_, f32[4616,128]{1,0:T(8,128)S(1)} %shard_map.68.refs_0_.refs_3_, ...), custom_call_target="tpu_custom_call" | custom-call | bytes 32400000 | tf_op jit(solution)/shard_map/pallas_call | solution.py:424
  99.3 9.5 %shard_map.75.refs_8_ = f32[32,128,128]{2,1,0:T(8,128)S(1)} custom-call(s32[1,1,32]{2,1,0:T(1,128)S(1)} %copy-done.16, f32[18560,128]{1,0:T(8,128)S(1)} %shard_map.73.refs_1_, f32[4616,128]{1,0:T(8,128)S(1)} %get-tuple-element.51.refs_0_.refs_2_, f32[4616,128]{1,0:T(8,128)S(1)} %shard_map.68.refs_0_.refs_3_, ...), custom_call_target="tpu_custom_call", output_to_operand_aliasing={{}: (18, {})} | custom-call | bytes 32400000 | tf_op jit(solution)/shard_map/pallas_call | solution.py:424
  110.6 2.2 %collective-permute-start.45 = (f32[8,128]{1,0:T(8,128)S(1)}, f32[8,128]{1,0:T(8,128)S(1)}, u32[]{:S(2)}, u32[]{:S(2)}) collective-permute-start(f32[8,128]{1,0:T(8,128)S(1)} %shard_map.76), channel_id=1, source_target_pairs={{0,4},{1,5},{2,6},{3,7},{4,0},{5,1},{6,2},{7,3},{8,12},{9,13},{10,... | collective-permute-start | bytes 12296 | tf_op jit(solution)/shard_map/ppermute | solution.py:74
  112.8 5.0 %shard_map.77.refs_10_ = f32[32,128,128]{2,1,0:T(8,128)S(1)} custom-call(s32[1,1,32]{2,1,0:T(1,128)S(1)} %copy-done.16, f32[18560,128]{1,0:T(8,128)S(1)} %shard_map.73.refs_1_, f32[4616,128]{1,0:T(8,128)S(1)} %copy-done.1, f32[4616,128]{1,0:T(8,128)S(1)} %shard_map.68.refs_0_.refs_3_, f32[4616,128]{1,0:T(8,128)S(1)} %copy-done.3, ...), custom_call_target="tpu_custom_call", output_to_operand_aliasing={{}: (8, {})} | custom-call | bytes 18000000 | tf_op jit(solution)/shard_map/pallas_call | solution.py:424
  118.3 2.2 %collective-permute-done.49.refs_9_ = f32[2080,128]{1,0:T(8,128)S(1)} collective-permute-done((f32[2080,128]{1,0:T(8,128)S(1)}, f32[2080,128]{1,0:T(8,128)S(1)}, u32[]{:S(2)}, u32[]{:S(2)}) %collective-permute-start.49) | collective-permute-done | bytes 1064992 | tf_op jit(solution)/shard_map/ppermute | solution.py:74
  122.1 5.0 %shard_map.78 = (f32[32,128,128]{2,1,0:T(8,128)S(1)}, f32[32,128,128]{2,1,0:T(8,128)S(1)}, f32[32,128,128]{2,1,0:T(8,128)S(1)}) custom-call(s32[1,1,32]{2,1,0:T(1,128)S(1)} %copy-done.16, f32[18560,128]{1,0:T(8,128)S(1)} %shard_map.73.refs_1_, f32[4616,128]{1,0:T(8,128)S(1)} %copy-done.1, ...), custom_call_target="tpu_custom_call", output_to_operand_aliasing={{0}: (10, {})} | custom-call | bytes 21600000 | tf_op jit(solution)/shard_map/pallas_call | solution.py:424
  129.1 3.7 %collective-permute-done.47 = f32[8,128]{1,0:T(8,128)S(1)} collective-permute-done((f32[8,128]{1,0:T(8,128)S(1)}, f32[8,128]{1,0:T(8,128)S(1)}, u32[]{:S(2)}, u32[]{:S(2)}) %collective-permute-start.47) | collective-permute-done | bytes 4128 | tf_op jit(solution)/shard_map/ppermute | solution.py:60
  (80 shorter events, 22.8 us)
Async XLA Ops:
  3.4 36.1 %collective-permute-start.37 = (f32[4616,128]{1,0:T(8,128)S(1)}, f32[4616,128]{1,0:T(8,128)S(1)}, u32[]{:S(2)}, u32[]{:S(2)}) collective-permute-start(f32[4616,128]{1,0:T(8,128)S(1)} %get-tuple-element.51.refs_0_.refs_2_), channel_id=1, source_target_pairs={{0,2},{1,7},{2,4},{3,1},{4,6},{5,3},{6,0},{7,5},{8,10},{9,15},{10,... | collective-permute-start | bytes 7090184 | tf_op jit(solution)/shard_map/ppermute | solution.py:74
  10.8 8.2 %collective-permute-start.22 = (f32[776,128]{1,0:T(8,128)S(1)}, f32[776,128]{1,0:T(8,128)S(1)}, u32[]{:S(2)}, u32[]{:S(2)}) collective-permute-start(f32[776,128]{1,0:T(8,128)S(1)} %get-tuple-element.46.refs_4_), channel_id=1, source_target_pairs={{0,32},{1,97},{2,34},{3,99},{4,36},{5,101},{6,38},{7,103},{8,40},{... | collective-permute-start | bytes 1191944 | tf_op jit(solution)/shard_map/ppermute | solution.py:74
  13.5 8.2 %collective-permute-start.25 = (f32[776,128]{1,0:T(8,128)S(1)}, f32[776,128]{1,0:T(8,128)S(1)}, u32[]{:S(2)}, u32[]{:S(2)}) collective-permute-start(f32[776,128]{1,0:T(8,128)S(1)} %get-tuple-element.47.refs_8_), channel_id=1, source_target_pairs={{0,8},{1,25},{2,10},{3,27},{4,12},{5,29},{6,14},{7,31},{8,16},{9,1... | collective-permute-start | bytes 1191944 | tf_op jit(solution)/shard_map/ppermute | solution.py:74
  14.0 9.2 %collective-permute-start.28 = (f32[776,128]{1,0:T(8,128)S(1)}, f32[776,128]{1,0:T(8,128)S(1)}, u32[]{:S(2)}, u32[]{:S(2)}) collective-permute-start(f32[776,128]{1,0:T(8,128)S(1)} %get-tuple-element.48.refs_12_), channel_id=1, source_target_pairs={{0,32},{1,97},{2,34},{3,99},{4,36},{5,101},{6,38},{7,103},{8,40},{... | collective-permute-start | bytes 1191944 | tf_op jit(solution)/shard_map/ppermute | solution.py:74
  15.6 10.4 %collective-permute-start.20 = (f32[776,128]{1,0:T(8,128)S(1)}, f32[776,128]{1,0:T(8,128)S(1)}, u32[]{:S(2)}, u32[]{:S(2)}) collective-permute-start(f32[776,128]{1,0:T(8,128)S(1)} %collective-permute-done.19.refs_1_), channel_id=1, source_target_pairs={{0,8},{1,25},{2,10},{3,27},{4,12},{5,29},{6,14},{7,31},{8,16},{9,1... | collective-permute-start | bytes 1191944 | tf_op jit(solution)/shard_map/ppermute | solution.py:74
  19.0 8.5 %collective-permute-start.23 = (f32[776,128]{1,0:T(8,128)S(1)}, f32[776,128]{1,0:T(8,128)S(1)}, u32[]{:S(2)}, u32[]{:S(2)}) collective-permute-start(f32[776,128]{1,0:T(8,128)S(1)} %collective-permute-done.22.refs_5_), channel_id=1, source_target_pairs={{0,32},{1,97},{2,34},{3,99},{4,36},{5,101},{6,38},{7,103},{8,40},{... | collective-permute-start | bytes 1191944 | tf_op jit(solution)/shard_map/ppermute | solution.py:74
  21.7 8.5 %collective-permute-start.26 = (f32[776,128]{1,0:T(8,128)S(1)}, f32[776,128]{1,0:T(8,128)S(1)}, u32[]{:S(2)}, u32[]{:S(2)}) collective-permute-start(f32[776,128]{1,0:T(8,128)S(1)} %collective-permute-done.25.refs_9_), channel_id=1, source_target_pairs={{0,8},{1,25},{2,10},{3,27},{4,12},{5,29},{6,14},{7,31},{8,16},{9,1... | collective-permute-start | bytes 1191944 | tf_op jit(solution)/shard_map/ppermute | solution.py:74
  23.2 8.5 %collective-permute-start.29 = (f32[776,128]{1,0:T(8,128)S(1)}, f32[776,128]{1,0:T(8,128)S(1)}, u32[]{:S(2)}, u32[]{:S(2)}) collective-permute-start(f32[776,128]{1,0:T(8,128)S(1)} %collective-permute-done.28.refs_13_), channel_id=1, source_target_pairs={{0,32},{1,97},{2,34},{3,99},{4,36},{5,101},{6,38},{7,103},{8,40},{... | collective-permute-start | bytes 1191944 | tf_op jit(solution)/shard_map/ppermute | solution.py:74
  25.9 8.5 %collective-permute-start.21 = (f32[776,128]{1,0:T(8,128)S(1)}, f32[776,128]{1,0:T(8,128)S(1)}, u32[]{:S(2)}, u32[]{:S(2)}) collective-permute-start(f32[776,128]{1,0:T(8,128)S(1)} %collective-permute-done.20.refs_2_), channel_id=1, source_target_pairs={{0,8},{1,25},{2,10},{3,27},{4,12},{5,29},{6,14},{7,31},{8,16},{9,1... | collective-permute-start | bytes 1191944 | tf_op jit(solution)/shard_map/ppermute | solution.py:74
  39.5 28.0 %collective-permute-start.38 = (f32[4616,128]{1,0:T(8,128)S(1)}, f32[4616,128]{1,0:T(8,128)S(1)}, u32[]{:S(2)}, u32[]{:S(2)}) collective-permute-start(f32[4616,128]{1,0:T(8,128)S(1)} %shard_map.68.refs_0_.refs_3_), channel_id=1, source_target_pairs={{0,2},{1,7},{2,4},{3,1},{4,6},{5,3},{6,0},{7,5},{8,10},{9,15},{10,... | collective-permute-start | bytes 7090184 | tf_op jit(solution)/shard_map/ppermute | solution.py:74
  42.0 27.0 %collective-permute-start.31 = (f32[2080,128]{1,0:T(8,128)S(1)}, f32[2080,128]{1,0:T(8,128)S(1)}, u32[]{:S(2)}, u32[]{:S(2)}) collective-permute-start(f32[2080,128]{1,0:T(8,128)S(1)} %get-tuple-element.49.refs_5_.refs_6_.refs_0_), channel_id=1, source_target_pairs={{0,32},{1,97},{2,34},{3,99},{4,36},{5,101},{6,38},{7,103},{8,40},{... | collective-permute-start | bytes 3194888 | tf_op jit(solution)/shard_map/ppermute | solution.py:74
  45.2 27.0 %collective-permute-start.34 = (f32[2080,128]{1,0:T(8,128)S(1)}, f32[2080,128]{1,0:T(8,128)S(1)}, u32[]{:S(2)}, u32[]{:S(2)}) collective-permute-start(f32[2080,128]{1,0:T(8,128)S(1)} %get-tuple-element.50.refs_7_.refs_8_.refs_4_), channel_id=1, source_target_pairs={{0,8},{1,25},{2,10},{3,27},{4,12},{5,29},{6,14},{7,31},{8,16},{9,1... | collective-permute-start | bytes 3194888 | tf_op jit(solution)/shard_map/ppermute | solution.py:74
  45.8 26.6 %collective-permute-start.40 = (f32[2080,128]{1,0:T(8,128)S(1)}, f32[2080,128]{1,0:T(8,128)S(1)}, u32[]{:S(2)}, u32[]{:S(2)}) collective-permute-start(f32[2080,128]{1,0:T(8,128)S(1)} %get-tuple-element.52.refs_6_.refs_7_), channel_id=1, source_target_pairs={{0,32},{1,97},{2,34},{3,99},{4,36},{5,101},{6,38},{7,103},{8,40},{... | collective-permute-start | bytes 3194888 | tf_op jit(solution)/shard_map/ppermute | solution.py:74
  45.8 26.6 %collective-permute-start.41 = (f32[2080,128]{1,0:T(8,128)S(1)}, f32[2080,128]{1,0:T(8,128)S(1)}, u32[]{:S(2)}, u32[]{:S(2)}) collective-permute-start(f32[2080,128]{1,0:T(8,128)S(1)} %get-tuple-element.53.refs_8_.refs_9_), channel_id=1, source_target_pairs={{0,8},{1,25},{2,10},{3,27},{4,12},{5,29},{6,14},{7,31},{8,16},{9,1... | collective-permute-start | bytes 3194888 | tf_op jit(solution)/shard_map/ppermute | solution.py:74
  67.6 31.6 %collective-permute-start.39 = (f32[4616,128]{1,0:T(8,128)S(1)}, f32[4616,128]{1,0:T(8,128)S(1)}, u32[]{:S(2)}, u32[]{:S(2)}) collective-permute-start(f32[4616,128]{1,0:T(8,128)S(1)} %collective-permute-done.38.refs_0_.refs_4_), channel_id=1, source_target_pairs={{0,2},{1,7},{2,4},{3,1},{4,6},{5,3},{6,0},{7,5},{8,10},{9,15},{10,... | collective-permute-start | bytes 7090184 | tf_op jit(solution)/shard_map/ppermute | solution.py:74
  69.0 15.0 %collective-permute-start.32 = (f32[2080,128]{1,0:T(8,128)S(1)}, f32[2080,128]{1,0:T(8,128)S(1)}, u32[]{:S(2)}, u32[]{:S(2)}) collective-permute-start(f32[2080,128]{1,0:T(8,128)S(1)} %collective-permute-done.31.refs_9_.refs_10_.refs_1_), channel_id=1, source_target_pairs={{0,32},{1,97},{2,34},{3,99},{4,36},{5,101},{6,38},{7,103},{8,40},{... | collective-permute-start | bytes 3194888 | tf_op jit(solution)/shard_map/ppermute | solution.py:74
  72.1 15.3 %collective-permute-start.35 = (f32[2080,128]{1,0:T(8,128)S(1)}, f32[2080,128]{1,0:T(8,128)S(1)}, u32[]{:S(2)}, u32[]{:S(2)}) collective-permute-start(f32[2080,128]{1,0:T(8,128)S(1)} %collective-permute-done.34.refs_11_.refs_12_.refs_5_), channel_id=1, source_target_pairs={{0,8},{1,25},{2,10},{3,27},{4,12},{5,29},{6,14},{7,31},{8,16},{9,1... | collective-permute-start | bytes 3194888 | tf_op jit(solution)/shard_map/ppermute | solution.py:74
  72.3 24.7 %collective-permute-start.42 = (f32[2080,128]{1,0:T(8,128)S(1)}, f32[2080,128]{1,0:T(8,128)S(1)}, u32[]{:S(2)}, u32[]{:S(2)}) collective-permute-start(f32[2080,128]{1,0:T(8,128)S(1)} %collective-permute-done.40.refs_10_.refs_11_), channel_id=1, source_target_pairs={{0,32},{1,97},{2,34},{3,99},{4,36},{5,101},{6,38},{7,103},{8,40},{... | collective-permute-start | bytes 3194888 | tf_op jit(solution)/shard_map/ppermute | solution.py:74
  72.4 25.2 %collective-permute-start.43 = (f32[2080,128]{1,0:T(8,128)S(1)}, f32[2080,128]{1,0:T(8,128)S(1)}, u32[]{:S(2)}, u32[]{:S(2)}) collective-permute-start(f32[2080,128]{1,0:T(8,128)S(1)} %collective-permute-done.41.refs_12_.refs_13_), channel_id=1, source_target_pairs={{0,8},{1,25},{2,10},{3,27},{4,12},{5,29},{6,14},{7,31},{8,16},{9,1... | collective-permute-start | bytes 3194888 | tf_op jit(solution)/shard_map/ppermute | solution.py:74
  84.0 24.9 %collective-permute-start.33 = (f32[2080,128]{1,0:T(8,128)S(1)}, f32[2080,128]{1,0:T(8,128)S(1)}, u32[]{:S(2)}, u32[]{:S(2)}) collective-permute-start(f32[2080,128]{1,0:T(8,128)S(1)} %collective-permute-done.32.refs_14_.refs_2_), channel_id=1, source_target_pairs={{0,32},{1,97},{2,34},{3,99},{4,36},{5,101},{6,38},{7,103},{8,40},{... | collective-permute-start | bytes 3194888 | tf_op jit(solution)/shard_map/ppermute | solution.py:74
  87.4 21.6 %collective-permute-start.36 = (f32[2080,128]{1,0:T(8,128)S(1)}, f32[2080,128]{1,0:T(8,128)S(1)}, u32[]{:S(2)}, u32[]{:S(2)}) collective-permute-start(f32[2080,128]{1,0:T(8,128)S(1)} %collective-permute-done.35.refs_16_.refs_6_), channel_id=1, source_target_pairs={{0,8},{1,25},{2,10},{3,27},{4,12},{5,29},{6,14},{7,31},{8,16},{9,1... | collective-permute-start | bytes 3194888 | tf_op jit(solution)/shard_map/ppermute | solution.py:74
  97.6 20.6 %collective-permute-start.48 = (f32[2080,128]{1,0:T(8,128)S(1)}, f32[2080,128]{1,0:T(8,128)S(1)}, u32[]{:S(2)}, u32[]{:S(2)}) collective-permute-start(f32[2080,128]{1,0:T(8,128)S(1)} %get-tuple-element.54.refs_15_), channel_id=1, source_target_pairs={{0,32},{1,97},{2,34},{3,99},{4,36},{5,101},{6,38},{7,103},{8,40},{... | collective-permute-start | bytes 3194888 | tf_op jit(solution)/shard_map/ppermute | solution.py:74
  98.9 21.6 %collective-permute-start.49 = (f32[2080,128]{1,0:T(8,128)S(1)}, f32[2080,128]{1,0:T(8,128)S(1)}, u32[]{:S(2)}, u32[]{:S(2)}) collective-permute-start(f32[2080,128]{1,0:T(8,128)S(1)} %get-tuple-element.55.refs_17_), channel_id=1, source_target_pairs={{0,8},{1,25},{2,10},{3,27},{4,12},{5,29},{6,14},{7,31},{8,16},{9,1... | collective-permute-start | bytes 3194888 | tf_op jit(solution)/shard_map/ppermute | solution.py:74
  109.5 8.3 %collective-permute-start.44 = (f32[8,128]{1,0:T(8,128)S(1)}, f32[8,128]{1,0:T(8,128)S(1)}, u32[]{:S(2)}, u32[]{:S(2)}) collective-permute-start(f32[8,128]{1,0:T(8,128)S(1)} %shard_map.76), channel_id=1, source_target_pairs={{0,2},{1,7},{2,4},{3,1},{4,6},{5,3},{6,0},{7,5},{8,10},{9,15},{10,... | collective-permute-start | bytes 12296 | tf_op jit(solution)/shard_map/ppermute | solution.py:74
  (19 other events, 240.1 us)

commit v3 on v2

--- a/solution.py
+++ b/solution.py
@@ -12,13 +12,14 @@
 COUNT = 127
 FLAG = 126
 L_CAP = 36
-R_PART = 6
-R_HALF = 2 * R_PART
+R_PART, R_LATE = 6, 5
+R_HALF = R_PART + R_LATE
 PARCEL = HDR + R_PART * BS
 G_LATE = 4
 HEADS = 4 * HDR
 GROUP = HEADS + (2 * R_PART + G_LATE) * BS
 MERGE_COST = 70
+PLAN = 2 * 4 * R_HALF * 4 + 8
 UNROLL = 8
 AXES = ("row", "col", "layer")
 F32 = jnp.float32
@@ -60,7 +61,7 @@
     return lax.ppermute(array, "layer", [(0, 1), (1, 0)])
 
 
-def ring(array, axis, distance=1):
+def ring(array, axis, distance=1, cross=False):
     pairs = []
     for y in range(4):
         for x in range(4):
@@ -69,7 +70,7 @@
                     to = {"y": y, "x": x, "z": z}
                     to[axis] = (to[axis] + distance * (1 - 2 * core)) % 4
                     source = ((y * 4 + x) * 4 + z) * 2 + core
-                    target = ((to["y"] * 4 + to["x"]) * 4 + to["z"]) * 2 + core
+                    target = ((to["y"] * 4 + to["x"]) * 4 + to["z"]) * 2 + (core ^ cross)
                     pairs.append((source, target))
     return lax.ppermute(array, AXES, pairs)
 
@@ -112,7 +113,8 @@
         slot = s >> 1
         source = right.at[0, pl.ds(pl.multiple_of((code >> 3) * BS, BS), BS), pl.ds(pl.multiple_of((code & 7) * BS, BS), BS)]
         which = jnp.where(in_a, 0, 1) + jnp.where(slot < R_PART, 0, 2)
-        rows = block_rows(jnp.where(slot < R_PART, slot, slot - R_PART))
+        rows = jnp.where(slot < R_PART, HDR + slot * BS, (slot - R_PART) * BS)
+        rows = pl.ds(pl.multiple_of(rows, 8), BS)
         for i, out in enumerate((a_early, b_early, a_late, b_late)):
 
             @pl.when(which == i)
@@ -194,7 +196,7 @@
             count = seen[half, i, 0, COUNT].astype(jnp.int32)
 
             def start(s, g, half=half, i=i):
-                source = late[half][i].at[block_rows(s - R_PART)]
+                source = late[half][i].at[block_rows(s - R_PART, 0)]
                 for j in range(2):
 
                     @pl.when((g >= j * G_LATE) & (g < (j + 1) * G_LATE))
@@ -209,7 +211,7 @@
     for half in range(2):
 
         def finish(s, _, half=half):
-            pltpu.make_async_copy(late[half][0].at[block_rows(0)], outs[half][0].at[block_rows(0, HEADS)], lsems.at[half, s]).wait()
+            pltpu.make_async_copy(late[half][0].at[block_rows(0, 0)], outs[half][0].at[block_rows(0, HEADS)], lsems.at[half, s]).wait()
             return 0
 
         lax.fori_loop(0, totals[half], finish, 0)
@@ -247,117 +249,46 @@
 
 
 def hold_kernel(step, *refs):
-    packed_ref, held, sem = refs[0], refs[-2], refs[-1]
+    packed_ref, old = refs[0], refs[2]
+    held, table, head, sem, hsem = refs[-5:]
     rows = pl.ds(step * L_CAP * BS, L_CAP * BS)
     copy = pltpu.make_async_copy(packed_ref.at[pl.ds(HDR, L_CAP * BS)], held.at[rows], sem)
     copy.start()
+    read = pltpu.make_async_copy(packed_ref.at[pl.ds(0, HDR)], head, hsem)
+    read.start()
     if step == 0:
         held[pl.ds(4 * L_CAP * BS, BS)] = jnp.zeros((BS, BS), F32)
+
+    def keep_entries(i, _):
+        for j in range(8):
+            table[i * 8 + j] = jnp.int32(4 * L_CAP) if step == 0 else old[i * 8 + j]
+        return 0
+
+    lax.fori_loop(0, 32, keep_entries, 0)
+    read.wait()
+
+    def enter(s, _):
+        table[head[0, s].astype(jnp.int32)] = step * L_CAP + s
+        return 0
+
+    lax.fori_loop(0, head[0, COUNT].astype(jnp.int32), enter, 0)
     copy.wait()
 
 
-def hold(packed_left, step, held=None, after=()):
+def hold(packed_left, step, held=(), after=()):
     shape = jax.ShapeDtypeStruct(((4 * L_CAP + 1) * BS, BS), F32)
     return pl.pallas_call(
         functools.partial(hold_kernel, step),
-        out_shape=shape,
-        in_specs=[HBM] + ([] if held is None else [VMEM]) + [ANY] * len(after),
-        out_specs=VMEM,
-        input_output_aliases={} if held is None else {1: 0},
-        scratch_shapes=[pltpu.SemaphoreType.DMA],
+        out_shape=[shape, jax.ShapeDtypeStruct((256,), jnp.int32)],
+        in_specs=[HBM] + [VMEM, SMEM][: len(held)] + [ANY] * len(after),
+        out_specs=[VMEM, SMEM],
+        input_output_aliases={1: 0} if held else {},
+        scratch_shapes=[pltpu.SMEM((HDR, BS), F32), pltpu.SemaphoreType.DMA, pltpu.SemaphoreType.DMA],
         compiler_params=params(1),
-    )(packed_left, *([] if held is None else [held]), *after)
-
-
-def multiply_kernel(n_left, lows, halves, begin, final, *refs):
-    refs = list(refs)
-    number = len(lows)
-    keep, lv = refs.pop(0), refs.pop(0)
-    lefts = [refs.pop(0) for _ in range(n_left)]
-    parts = [[refs.pop(0) if j == 0 or j in halves else None for j in range(2)] for _ in range(number)]
-    if not begin:
-        refs.pop(0)
-    if final:
-        owner, flag_in = refs.pop(0), refs.pop(0)
-    acc = refs.pop(0)
-    if final:
-        mine, send = refs.pop(0), refs.pop(0)
-    rv, lhead, rhead, table, work, rsems, hsems = refs
-    heads = []
-    for i in range(n_left):
-        heads.append(pltpu.make_async_copy(lefts[i].at[pl.ds(0, HDR)], lhead.at[i], hsems.at[i]))
-    for g in range(number):
-        for i in range(4):
-            heads.append(pltpu.make_async_copy(parts[g][0].at[pl.ds(i * HDR, HDR)], rhead.at[g, i], hsems.at[4 + g * 4 + i]))
-    for copy in heads:
-        copy.start()
-    loads = []
-    for g in range(number):
-        for n, j in enumerate(halves):
-            rows = pl.ds((g * len(halves) + n) * GROUP, GROUP)
-            loads.append(pltpu.make_async_copy(parts[g][j], rv.at[rows], rsems.at[g * len(halves) + n]))
-    for copy in loads:
-        copy.start()
-    if begin:
-        acc[...] = jnp.zeros(acc.shape, F32)
-    no_left, no_right = 4 * L_CAP, number * len(halves) * GROUP
-    rv[pl.ds(no_right, BS)] = jnp.zeros((BS, BS), F32)
-
-    def clear(i, _):
-        for j in range(8):
-            table[i * 8 + j] = no_left
-        return 0
-
-    lax.fori_loop(0, 32, clear, 0)
-    for copy in heads:
-        copy.wait()
-    for i in range(n_left):
-
-        def enter(s, _, i=i):
-            table[lhead[i, 0, s].astype(jnp.int32)] = i * L_CAP + s
-            return 0
-
-        lax.fori_loop(0, lhead[i, 0, COUNT].astype(jnp.int32), enter, 0)
-    pairs = jnp.int32(0)
-
-    def note(code, at, n, low):
-        k4 = (code >> 3) * 4
-        c = code & 7
-        for r in range(4):
-            slot = table[k4 + r]
-            work[n] = (slot << 20) | (at << 5) | (r * 8 + c)
-            n = n + jnp.where((slot >= low * L_CAP) & (slot < no_left), keep[0, 0, r * 8 + c], 0)
-        return n
-
-    for g in range(number):
-        late = jnp.int32(0)
-        for i in range(4):
-            count = rhead[g, i, 0, COUNT].astype(jnp.int32)
-            if i // 2 in halves:
-                first = ((g * len(halves) + halves.index(i // 2)) * GROUP + HEADS + (i % 2) * R_PART * BS) // 8
-
-                def early_one(s, n, g=g, i=i, first=first):
-                    return note(rhead[g, i, 0, s].astype(jnp.int32), first + s * (BS // 8), n, lows[g])
-
-                pairs = lax.fori_loop(0, jnp.minimum(count, R_PART), early_one, pairs)
-            low = min(halves) * G_LATE
-            first = (g * len(halves) * GROUP + HEADS + 2 * R_PART * BS) // 8
-
-            def late_one(s, state, g=g, i=i, low=low, first=first):
-                n, at = state
-                place_of = jnp.clip(at - low, 0, len(halves) * G_LATE - 1)
-                place_of = first + (place_of // G_LATE) * (GROUP // 8) + (place_of % G_LATE) * (BS // 8)
-                after = note(rhead[g, i, 0, s].astype(jnp.int32), place_of, n, lows[g])
-                inside = (at >= low) & (at < low + len(halves) * G_LATE)
-                return jnp.where(inside, after, n), at + 1
-
-            pairs, late = lax.fori_loop(R_PART, count, late_one, (pairs, late))
-    for j in range(UNROLL):
-        work[pairs + j] = (no_left << 20) | (no_right // 8 << 5)
-
-    for copy in loads:
-        copy.wait()
-
+    )(packed_left, *held, *after)
+
+
+def products(work, pairs, lv, rv, acc):
     def step(w, _):
         results = []
         for j in range(UNROLL):
@@ -372,73 +303,263 @@
 
     lax.fori_loop(0, (pairs + UNROLL - 1) // UNROLL, step, 0)
 
-    if final:
-        me = lax.axis_index("layer")
-        mine[...] = jnp.zeros(mine.shape, F32)
-        send[...] = jnp.zeros(send.shape, F32)
-        counts = [jnp.int32(0), jnp.int32(0)]
-        for t in range(32):
-            who = owner[0, 0, t]
-            slot = jnp.where(who == 0, counts[0], counts[1])
-
-            @pl.when(who == me)
-            def _(t=t, slot=slot):
-                mine[slot] = acc[t]
-
-            @pl.when(who != me)
-            def _(t=t, slot=slot):
-                send[slot] = acc[t]
-
-            counts[0] = counts[0] + (who == 0).astype(jnp.int32)
-            counts[1] = counts[1] + (who != 0).astype(jnp.int32)
+
+def load_parts(arrays, rv, sems, skip=0):
+    loads = []
+    for n, array in enumerate(arrays):
+        if n < skip:
+            continue
+        loads.append(pltpu.make_async_copy(array, rv.at[pl.ds(n * GROUP, GROUP)], sems.at[n]))
+        loads[-1].start()
+    rv[pl.ds(len(arrays) * GROUP, BS)] = jnp.zeros((BS, BS), F32)
+    return loads
+
+
+def multiply_kernel(lows, halves, begin, more, *refs):
+    refs = list(refs)
+    number, several = len(lows), len(halves)
+    keep, table, lv = refs.pop(0), refs.pop(0), refs.pop(0)
+    parts = [[refs.pop(0) if j in halves else None for j in range(2)] for _ in range(number)]
+    if not begin:
+        refs.pop(0)
+    left = refs.pop(0) if more else None
+    acc = refs.pop(0)
+    if more:
+        lv, old, table = refs.pop(0), table, refs.pop(0)
+    plan = refs.pop(0) if several == 1 else None
+    rv, rhead, fhead, ihead, work, rsems, hsems, bsem = refs[:8]
+    if more:
+        lhead, lsem, lhsem = refs[8:]
+        taken = pltpu.make_async_copy(left.at[pl.ds(HDR, L_CAP * BS)], lv.at[pl.ds(3 * L_CAP * BS, L_CAP * BS)], lsem)
+        taken.start()
+        lread = pltpu.make_async_copy(left.at[pl.ds(0, HDR)], lhead, lhsem)
+        lread.start()
+    sparse = sum(low > 0 for low in lows)
+    heads = []
+    for g in range(number):
+        heads.append(pltpu.make_async_copy(parts[g][0].at[pl.ds(0, HEADS)], fhead.at[g], hsems.at[g]))
+        heads[-1].start()
+    loads = load_parts([part[j] for part in parts for j in halves], rv, rsems, sparse * several)
+    if begin:
+        acc[...] = jnp.zeros(acc.shape, F32)
+    if more:
+
+        def keep_entries(i, _):
+            for j in range(8):
+                table[i * 8 + j] = old[i * 8 + j]
+            return 0
+
+        lax.fori_loop(0, 32, keep_entries, 0)
+        lread.wait()
+
+        def enter(s, _):
+            table[lhead[0, s].astype(jnp.int32)] = 3 * L_CAP + s
+            return 0
+
+        lax.fori_loop(0, lhead[0, COUNT].astype(jnp.int32), enter, 0)
+    for copy in heads:
+        copy.wait()
+    for g in range(number):
+        for i in range(4):
+            ihead[g * 4 + i] = fhead[g, i * HDR].astype(jnp.int32)
+    turn = pltpu.make_async_copy(ihead, rhead, hsems.at[0])
+    turn.start()
+    turn.wait()
+
+    def note(out, code, at, n, g, j, row):
+        k4 = (code >> 3) * 4
+        c = code & 7
+        before = n
+        for r in range(4):
+            slot = table[k4 + r]
+            out[n] = (slot << 20) | (at << 5) | (r * 8 + c)
+            n = n + jnp.where((slot >= lows[g] * L_CAP) & (slot < 4 * L_CAP), keep[0, 0, r * 8 + c], 0)
+        if lows[g] > 0:
+
+            @pl.when(n > before)
+            def _():
+                rows = pl.ds(pl.multiple_of(at * 8, 8), BS)
+                pltpu.make_async_copy(parts[g][j].at[pl.ds(pl.multiple_of(row, 8), BS)], rv.at[rows], bsem).start()
+
+        return n
+
+    fetched = []
+
+    def listed(out, chosen):
+        pairs = jnp.int32(0)
+        blocks = jnp.int32(0)
+        for g in range(number):
+            late = jnp.int32(0)
+            for i in range(4):
+                count = rhead[g * 4 + i, COUNT]
+                if i // 2 in chosen:
+                    row = HEADS + (i % 2) * R_PART * BS
+                    first = ((g * len(chosen) + chosen.index(i // 2)) * GROUP + row) // 8
+
+                    def early_one(s, state, g=g, i=i, first=first, row=row):
+                        n, blocks = state
+                        code = rhead[g * 4 + i, s]
+                        after = note(out, code, first + s * (BS // 8), n, g, i // 2, row + s * BS)
+                        return after, blocks + (after > n).astype(jnp.int32)
+
+                    if lows[g] > 0:
+
+                        def early_some(s, state, g=g, i=i, one=early_one):
+                            wanted = (rhead[g * 4 + i, s] >> 7) == deferred
+                            return lax.cond(wanted, lambda state: one(s, state), lambda state: state, state)
+
+                    else:
+                        early_some = early_one
+                    pairs, blocks = lax.fori_loop(0, jnp.minimum(count, R_PART), early_some, (pairs, blocks))
+                for j in chosen:
+                    low = j * G_LATE
+                    row = HEADS + 2 * R_PART * BS
+                    first = ((g * len(chosen) + chosen.index(j)) * GROUP + row) // 8
+                    begin_at = jnp.clip(low - late, 0, jnp.maximum(count - R_PART, 0))
+                    end_at = jnp.clip(low + G_LATE - late, 0, jnp.maximum(count - R_PART, 0))
+
+                    def late_one(s, state, g=g, i=i, j=j, first=first, row=row, late=late, low=low):
+                        n, blocks = state
+                        at = late + s - low
+                        code = rhead[g * 4 + i, R_PART + s]
+                        after = note(out, code, first + at * (BS // 8), n, g, j, row + at * BS)
+                        return after, blocks + (after > n).astype(jnp.int32)
+
+                    pairs, blocks = lax.fori_loop(begin_at, end_at, late_one, (pairs, blocks))
+                late = late + jnp.maximum(count - R_PART, 0)
+            if g == sparse - 1:
+                fetched.append(blocks)
+        for j in range(UNROLL):
+            out[pairs + j] = (4 * L_CAP << 20) | (number * len(chosen) * GROUP // 8 << 5)
+        return pairs
+
+    if sparse:
+        way = 1 - 2 * lax.axis_index("layer")
+        deferred = (lax.axis_index("col") - 3 * way) & 3
+    pairs = listed(work, halves)
+    for copy in loads:
+        copy.wait()
+    if more:
+        taken.wait()
+    if sparse:
+
+        def arrive(_, state):
+            pltpu.make_async_copy(parts[0][0].at[pl.ds(HEADS, BS)], rv.at[pl.ds(HEADS, BS)], bsem).wait()
+            return state
+
+        lax.fori_loop(0, fetched[0], arrive, 0)
+    products(work, pairs, lv, rv, acc)
+    if several == 1:
+        plan[PLAN] = listed(plan, (1,))
+
+
+def finish_kernel(*refs):
+    plan, owner, lv, part_a, part_b, _, _, acc, mine, send, rv, sems = refs
+    loads = load_parts([part_a, part_b], rv, sems)
+    for copy in loads:
+        copy.wait()
+    products(plan, plan[PLAN], lv, rv, acc)
+    me = lax.axis_index("layer")
+    counts = [jnp.int32(0), jnp.int32(0)]
+    for t in range(32):
+        who = owner[0, 0, t]
+        slot = jnp.where(who == 0, counts[0], counts[1])
+
+        @pl.when(who == me)
+        def _(t=t, slot=slot):
+            mine[slot] = acc[t]
+
+        @pl.when(who != me)
+        def _(t=t, slot=slot):
+            send[slot] = acc[t]
+
+        counts[0] = counts[0] + (who == 0).astype(jnp.int32)
+        counts[1] = counts[1] + (who != 0).astype(jnp.int32)
+
+    def clear(out, used):
+        def one(s, _):
+            out[s] = jnp.zeros((BS, BS), F32)
+            return 0
+
+        lax.fori_loop(used, 32, one, 0)
+
+    clear(mine, jnp.where(me == 0, counts[0], counts[1]))
+    clear(send, jnp.where(me == 0, counts[1], counts[0]))
 
 
 ANY = pl.BlockSpec(memory_space=pl.ANY)
 SMEM = pl.BlockSpec(memory_space=pltpu.SMEM)
 VMEM = pl.BlockSpec(memory_space=pltpu.VMEM)
 HBM = pl.BlockSpec(memory_space=pltpu.HBM)
+TILE = jax.ShapeDtypeStruct((32, BS, BS), F32)
 
 
 def params(mebibytes):
     return pltpu.CompilerParams(vmem_limit_bytes=int(mebibytes * 2**20))
 
 
+def cost(micros):
+    return pl.CostEstimate(flops=0, bytes_accessed=int(micros * 3.6e6), transcendentals=0)
+
+
 def packed(blocks, head=HDR):
     return jax.ShapeDtypeStruct((head + blocks * BS, BS), F32)
 
 
-def multiply(micros, keep, held, lefts, parts, lows, halves, acc=None, owner=None, flag=None):
-    begin, final = acc is None, owner is not None
+def multiply(micros, keep, held, parts, lows, halves, acc=None, left=None):
     number = len(parts)
-    arrays = [part[j] for part in parts for j in range(2) if j == 0 or j in halves]
-    operands = [keep, held, *lefts, *arrays]
-    specs = [SMEM, VMEM] + [HBM] * (len(lefts) + len(arrays))
+    arrays = [part[j] for part in parts for j in halves]
+    operands = [keep, held[1], held[0], *arrays]
+    specs = [SMEM, SMEM, VMEM] + [HBM] * len(arrays)
     aliases = {}
-    if not begin:
-        aliases = {len(operands): 0}
+    if acc is not None:
+        aliases[len(operands)] = 0
         operands.append(acc)
         specs.append(VMEM)
-    if final:
-        operands += [owner, flag]
-        specs += [SMEM, VMEM]
+    out_shape, out_specs = [TILE], [VMEM]
+    scratch = [
+        pltpu.VMEM((len(arrays) * GROUP + BS, BS), F32),
+        pltpu.SMEM((-(-number // 2) * 8, BS), jnp.int32),
+        pltpu.VMEM((number, HEADS, BS), F32),
+        pltpu.VMEM((-(-number // 2) * 8, BS), jnp.int32),
+        pltpu.SMEM((number * 4 * R_HALF * 4 + UNROLL,), jnp.int32),
+        pltpu.SemaphoreType.DMA((len(arrays),)),
+        pltpu.SemaphoreType.DMA((number,)),
+        pltpu.SemaphoreType.DMA,
+    ]
+    if left is not None:
+        aliases[2] = 1
+        operands.append(left)
+        specs.append(HBM)
+        out_shape += [jax.ShapeDtypeStruct(array.shape, array.dtype) for array in held]
+        out_specs += [VMEM, SMEM]
+        scratch += [pltpu.SMEM((HDR, BS), F32), pltpu.SemaphoreType.DMA, pltpu.SemaphoreType.DMA]
+    if len(halves) == 1:
+        out_shape.append(jax.ShapeDtypeStruct((PLAN + 1,), jnp.int32))
+        out_specs.append(SMEM)
     return pl.pallas_call(
-        functools.partial(multiply_kernel, len(lefts), lows, halves, begin, final),
-        out_shape=[jax.ShapeDtypeStruct((32, BS, BS), F32)] * (3 if final else 1),
+        functools.partial(multiply_kernel, lows, halves, acc is None, left is not None),
+        out_shape=out_shape,
         in_specs=specs,
-        out_specs=[VMEM] * (3 if final else 1),
+        out_specs=out_specs,
         input_output_aliases=aliases,
-        scratch_shapes=[
-            pltpu.VMEM((number * len(halves) * GROUP + BS, BS), F32),
-            pltpu.SMEM((4, HDR, BS), F32),
-            pltpu.SMEM((number, 4, HDR, BS), F32),
-            pltpu.SMEM((256,), jnp.int32),
-            pltpu.SMEM((number * 4 * R_HALF * 4 + UNROLL,), jnp.int32),
-            pltpu.SemaphoreType.DMA((2 * number,)),
-            pltpu.SemaphoreType.DMA((4 + 4 * number,)),
-        ],
-        compiler_params=params(4 + 1.1 * len(halves) * number),
-        cost_estimate=pl.CostEstimate(flops=0, bytes_accessed=int(micros * 3.6e6), transcendentals=0),
+        scratch_shapes=scratch,
+        compiler_params=params(4 + 1.1 * len(arrays)),
+        cost_estimate=cost(micros),
     )(*operands)
+
+
+def finish(micros, plan, owner, held, parts, acc, flag):
+    return pl.pallas_call(
+        finish_kernel,
+        out_shape=[TILE] * 3,
+        in_specs=[SMEM, SMEM, VMEM, HBM, HBM, VMEM, VMEM],
+        out_specs=[VMEM] * 3,
+        input_output_aliases={5: 0},
+        scratch_shapes=[pltpu.VMEM((2 * GROUP + BS, BS), F32), pltpu.SemaphoreType.DMA((2,))],
+        compiler_params=params(6),
+        cost_estimate=cost(micros),
+    )(plan, owner, held[0], *parts, acc, flag)[1:]
 
 
 def fence(arrays, after):
@@ -482,7 +603,7 @@
 def local(left_blocks, left_pattern, right_blocks, right_pattern, keep_mask, owner):
     early_a, early_b, late_a, late_b, packed_left = pl.pallas_call(
         pack_kernel,
-        out_shape=[packed(R_PART)] * 4 + [packed(L_CAP)],
+        out_shape=[packed(R_PART)] * 2 + [packed(R_LATE, 0)] * 2 + [packed(L_CAP)],
         in_specs=[SMEM, SMEM, HBM, HBM],
         out_specs=[HBM] * 5,
         scratch_shapes=[
@@ -500,7 +621,7 @@
     late_a, late_b = hops(late_a, "x"), hops(late_b, "y")
     lefts = hops(packed_left, "z", 1)
     (lefts[1],) = fence([lefts[1]], [early_a[3], early_b[3], late_a[3], late_b[3]])
-    lefts += hops(lefts[1], "z", 2)[1:]
+    lefts.append(ring(lefts[1], "z"))
     array = jax.ShapeDtypeStruct((GROUP, BS), F32)
     merged = pl.pallas_call(
         merge_kernel,
@@ -514,21 +635,24 @@
             pltpu.SemaphoreType.DMA((16,)),
         ],
         compiler_params=params(1),
-        cost_estimate=pl.CostEstimate(flops=0, bytes_accessed=int(MERGE_COST * 3.6e6), transcendentals=0),
+        cost_estimate=cost(MERGE_COST),
     )(*early_a, *early_b, *late_a, *late_b)
-    a0, b0 = hops(merged[0], "y"), hops(merged[2], "x")
+    a0, b0 = hops(merged[0], "y", 2), hops(merged[2], "x", 2)
     a1, b1 = hops(merged[1], "y", 2), hops(merged[3], "x", 2)
-    parts = [(a0[0], a1[0]), (b0[0], b1[0]), (a0[1], a1[1]), (b0[1], b1[1])]
     held = hold(lefts[0], 0)
     held = hold(lefts[1], 1, held)
+    (lefts[2],) = fence([lefts[2]], [a0[1], b0[1], held[1]])
+    lefts.append(ring(lefts[2], "z"))
+    parts = [(a0[0], a1[0]), (b0[0], b1[0]), (a0[1], a1[1]), (b0[1], b1[1])]
     held = hold(lefts[2], 2, held)
-    (acc,) = multiply(9, keep_mask, held, lefts[:3], parts, (0,) * 4, (0, 1))
-    held = hold(lefts[3], 3, held, [acc])
-    a1[2], b1[2] = fence([a1[2], b1[2]], [acc])
+    (acc,) = multiply(9, keep_mask, held, parts, (0,) * 4, (0, 1))
+    a0[2], b0[2] = fence([a0[2], b0[2]], [acc])
+    a0.append(ring(a0[2], "y"))
+    b0.append(ring(b0[2], "x"))
     a1.append(ring(a1[2], "y"))
     b1.append(ring(b1[2], "x"))
     parts += [(a0[2], a1[2]), (b0[2], b1[2])]
-    (acc,) = multiply(9, keep_mask, held, lefts, parts, (3,) * 4 + (0,) * 2, (0, 1), acc)
+    acc, *held = multiply(9, keep_mask, held, parts, (3,) * 4 + (0,) * 2, (0, 1), acc, lefts[3])
     flag = pl.pallas_call(
         flag_kernel,
         out_shape=jax.ShapeDtypeStruct((HDR, BS), F32),
@@ -539,8 +663,8 @@
     )(*a0, *b0, acc)
     flag = functools.reduce(jnp.maximum, [flag] + [ring(flag, "z", distance) for distance in (1, 2, 3)])
     last = [(a0[3], a1[3]), (b0[3], b1[3])]
-    (acc,) = multiply(5, keep_mask, held, lefts, last, (0, 0), (0,), acc)
-    _, mine, send = multiply(6, keep_mask, held, lefts, last, (0, 0), (1,), acc, owner.reshape(1, 1, 32), flag)
+    acc, plan = multiply(5, keep_mask, held, last, (0, 0), (0,), acc)
+    mine, send = finish(5, plan, owner.reshape(1, 1, 32), held, [a1[3], b1[3]], acc, flag)
     flag = jnp.maximum(flag, swap(flag))
     return lax.cond(
         flag[0, 0] > 0,

time: 136 us -> 130 us (0.956)
  waiting for transfers between devices: 46.1 us -> 42.4 us
  local copies, waits for them, and re-layouts: 4 us -> 0.53 us
    ppermute x30, waiting for transfers between devices: 42.4 us -> 38.7 us  [ring(): return lax.ppermute(array, AXES, pairs)]
    unnamed x22 -> x8, local copies, waits for them, and re-layouts: 3.49 us -> 0.01 us
    pallas_call x9 -> x8, Pallas kernels: 32 us -> 31.4 us  [the longest x3 19.7 us: multiply(): pl.pallas_call(functools.partial(multiply_kernel, lows, halves, acc is No...]
  transfers between devices with their start and end apart: 32 -> 32, of which waited for: 11 -> 13; matrix products, arithmetic and copies ran while one was open for 0% -> 0% of each run, Pallas kernels for 19% -> 22%
where the time goes in v3:
time: 130 us
  starting transfers between devices  50.1 us (39%)
  waiting for transfers between devices  42.4 us (33%)
  Pallas kernels  35.2 us (27%)
    ppermute x30, starting transfers between devices, ring(): return lax.ppermute(array, AXES, pairs)  49.1 us
    ppermute x30, waiting for transfers between devices, ring(): return lax.ppermute(array, AXES, pairs)  38.7 us
    pallas_call x3, Pallas kernels, multiply(): pl.pallas_call(functools.partial(multiply_kernel, lows, halves, acc is No...  19.7 us
    pallas_call x3, Pallas kernels, hold(): pl.pallas_call(functools.partial(hold_kernel, step), out_shape=[shape, ja...  5.74 us
    ppermute x2, waiting for transfers between devices, swap(): return lax.ppermute(array, 'layer', [(0, 1), (1, 0)])  3.7 us
    pallas_call x1, Pallas kernels, local(): pl.pallas_call(pack_kernel, out_shape=[packed(R_PART)] * 2 + [packed(R_LA...  3.49 us
  transfers between devices with their start and end apart: 32, of which 13 were waited for; matrix products, arithmetic and copies ran while one was open for 0% of the time, Pallas kernels for 22%

profile of v3, /device:TPU:1, one launch (start us, length us, event | category | flops | bytes accessed | tf_op | source)
XLA Modules:
  0.0 129.7 jit_solution(6529031670622930602)
XLA Ops:
  0.0 3.5 %shard_map.66 = (f32[776,128]{1,0:T(8,128)S(1)}, f32[776,128]{1,0:T(8,128)S(1)}, f32[640,128]{1,0:T(8,128)S(1)}, f32[640,128]{1,0:T(8,128)S(1)}, f32[4616,128]{1,0:T(8,128)S(1)}) custom-call(s32[1,4,16]{2,1,0:T(4,128)} %lpat.1, s32[1,4,8]{2,1,0:T(4,128)} %rpat.1, f32[1,512,2048]{2,1,0:T(8,128)} %left.1, f32[1,512,1024]{2,1,0:T(8,128)} %right.1), custom_call_target="tpu_custom_call" | custom-call | tf_op jit(solution)/shard_map/pallas_call | solution.py:604
  3.5 4.7 %collective-permute-start.35 = (f32[4616,128]{1,0:T(8,128)S(1)}, f32[4616,128]{1,0:T(8,128)S(1)}, u32[]{:S(2)}, u32[]{:S(2)}) collective-permute-start(f32[4616,128]{1,0:T(8,128)S(1)} %get-tuple-element.62.refs_0_), channel_id=1, source_target_pairs={{0,2},{1,7},{2,4},{3,1},{4,6},{5,3},{6,0},{7,5},{8,10},{9,15},{10,... | collective-permute-start | bytes 7090184 | tf_op jit(solution)/shard_map/ppermute | solution.py:75
  8.2 2.7 %collective-permute-start.19 = (f32[776,128]{1,0:T(8,128)S(1)}, f32[776,128]{1,0:T(8,128)S(1)}, u32[]{:S(2)}, u32[]{:S(2)}) collective-permute-start(f32[776,128]{1,0:T(8,128)S(1)} %get-tuple-element.56.refs_0_), channel_id=1, source_target_pairs={{0,8},{1,25},{2,10},{3,27},{4,12},{5,29},{6,14},{7,31},{8,16},{9,1... | collective-permute-start | bytes 1191944 | tf_op jit(solution)/shard_map/ppermute | solution.py:75
  10.8 2.7 %collective-permute-start.22 = (f32[776,128]{1,0:T(8,128)S(1)}, f32[776,128]{1,0:T(8,128)S(1)}, u32[]{:S(2)}, u32[]{:S(2)}) collective-permute-start(f32[776,128]{1,0:T(8,128)S(1)} %get-tuple-element.57.refs_4_), channel_id=1, source_target_pairs={{0,32},{1,97},{2,34},{3,99},{4,36},{5,101},{6,38},{7,103},{8,40},{... | collective-permute-start | bytes 1191944 | tf_op jit(solution)/shard_map/ppermute | solution.py:75
  15.6 3.4 %collective-permute-start.20 = (f32[776,128]{1,0:T(8,128)S(1)}, f32[776,128]{1,0:T(8,128)S(1)}, u32[]{:S(2)}, u32[]{:S(2)}) collective-permute-start(f32[776,128]{1,0:T(8,128)S(1)} %collective-permute-done.19.refs_1_), channel_id=1, source_target_pairs={{0,8},{1,25},{2,10},{3,27},{4,12},{5,29},{6,14},{7,31},{8,16},{9,1... | collective-permute-start | bytes 1191944 | tf_op jit(solution)/shard_map/ppermute | solution.py:75
  19.0 2.7 %collective-permute-start.23 = (f32[776,128]{1,0:T(8,128)S(1)}, f32[776,128]{1,0:T(8,128)S(1)}, u32[]{:S(2)}, u32[]{:S(2)}) collective-permute-start(f32[776,128]{1,0:T(8,128)S(1)} %collective-permute-done.22.refs_5_), channel_id=1, source_target_pairs={{0,32},{1,97},{2,34},{3,99},{4,36},{5,101},{6,38},{7,103},{8,40},{... | collective-permute-start | bytes 1191944 | tf_op jit(solution)/shard_map/ppermute | solution.py:75
  22.5 2.7 %collective-permute-start.29 = (f32[640,128]{1,0:T(8,128)S(1)}, f32[640,128]{1,0:T(8,128)S(1)}, u32[]{:S(2)}, u32[]{:S(2)}) collective-permute-start(f32[640,128]{1,0:T(8,128)S(1)} %collective-permute-done.28.refs_13_), channel_id=1, source_target_pairs={{0,32},{1,97},{2,34},{3,99},{4,36},{5,101},{6,38},{7,103},{8,40},{... | collective-permute-start | bytes 983048 | tf_op jit(solution)/shard_map/ppermute | solution.py:75
  27.2 2.7 %collective-permute-start.24 = (f32[776,128]{1,0:T(8,128)S(1)}, f32[776,128]{1,0:T(8,128)S(1)}, u32[]{:S(2)}, u32[]{:S(2)}) collective-permute-start(f32[776,128]{1,0:T(8,128)S(1)} %collective-permute-done.23.refs_6_), channel_id=1, source_target_pairs={{0,32},{1,97},{2,34},{3,99},{4,36},{5,101},{6,38},{7,103},{8,40},{... | collective-permute-start | bytes 1191944 | tf_op jit(solution)/shard_map/ppermute | solution.py:75
  30.7 2.7 %collective-permute-start.30 = (f32[640,128]{1,0:T(8,128)S(1)}, f32[640,128]{1,0:T(8,128)S(1)}, u32[]{:S(2)}, u32[]{:S(2)}) collective-permute-start(f32[640,128]{1,0:T(8,128)S(1)} %collective-permute-done.29.refs_14_), channel_id=1, source_target_pairs={{0,32},{1,97},{2,34},{3,99},{4,36},{5,101},{6,38},{7,103},{8,40},{... | collective-permute-start | bytes 983048 | tf_op jit(solution)/shard_map/ppermute | solution.py:75
  33.4 2.7 %collective-permute-done.27.refs_11_.refs_3_ = f32[640,128]{1,0:T(8,128)S(1)} collective-permute-done((f32[640,128]{1,0:T(8,128)S(1)}, f32[640,128]{1,0:T(8,128)S(1)}, u32[]{:S(2)}, u32[]{:S(2)}) %collective-permute-start.27) | collective-permute-done | bytes 327712 | tf_op jit(solution)/shard_map/ppermute | solution.py:75
  40.5 3.6 %collective-permute-start.31 = (f32[2080,128]{1,0:T(8,128)S(1)}, f32[2080,128]{1,0:T(8,128)S(1)}, u32[]{:S(2)}, u32[]{:S(2)}) collective-permute-start(f32[2080,128]{1,0:T(8,128)S(1)} %get-tuple-element.60.refs_3_.refs_0_), channel_id=1, source_target_pairs={{0,32},{1,97},{2,34},{3,99},{4,36},{5,101},{6,38},{7,103},{8,40},{... | collective-permute-start | bytes 3194888 | tf_op jit(solution)/shard_map/ppermute | solution.py:75
  49.6 6.5 %collective-permute-done.31.refs_1_.refs_7_ = f32[2080,128]{1,0:T(8,128)S(1)} collective-permute-done((f32[2080,128]{1,0:T(8,128)S(1)}, f32[2080,128]{1,0:T(8,128)S(1)}, u32[]{:S(2)}, u32[]{:S(2)}) %collective-permute-start.31) | collective-permute-done | bytes 1064992 | tf_op jit(solution)/shard_map/ppermute | solution.py:75
  56.0 2.2 %collective-permute-done.33.refs_2_.refs_9_.refs_5_ = f32[2080,128]{1,0:T(8,128)S(1)} collective-permute-done((f32[2080,128]{1,0:T(8,128)S(1)}, f32[2080,128]{1,0:T(8,128)S(1)}, u32[]{:S(2)}, u32[]{:S(2)}) %collective-permute-start.33) | collective-permute-done | bytes 1064992 | tf_op jit(solution)/shard_map/ppermute | solution.py:75
  58.2 8.0 %collective-permute-done.36.refs_0_ = f32[4616,128]{1,0:T(8,128)S(1)} collective-permute-done((f32[4616,128]{1,0:T(8,128)S(1)}, f32[4616,128]{1,0:T(8,128)S(1)}, u32[]{:S(2)}, u32[]{:S(2)}) %collective-permute-start.36) | collective-permute-done | bytes 2363424 | tf_op jit(solution)/shard_map/ppermute | solution.py:75
  67.7 3.4 %collective-permute-start.32 = (f32[2080,128]{1,0:T(8,128)S(1)}, f32[2080,128]{1,0:T(8,128)S(1)}, u32[]{:S(2)}, u32[]{:S(2)}) collective-permute-start(f32[2080,128]{1,0:T(8,128)S(1)} %collective-permute-done.31.refs_1_.refs_7_), channel_id=1, source_target_pairs={{0,32},{1,97},{2,34},{3,99},{4,36},{5,101},{6,38},{7,103},{8,40},{... | collective-permute-start | bytes 3194888 | tf_op jit(solution)/shard_map/ppermute | solution.py:75
  74.7 6.8 %shard_map.73.refs_2_.refs_15_ = f32[32,128,128]{2,1,0:T(8,128)S(1)} custom-call(s32[1,1,32]{2,1,0:T(1,128)S(1)} %copy-done.11, s32[256]{0:T(256)S(1)} %get-tuple-element.67.refs_1_, f32[18560,128]{1,0:T(8,128)S(1)} %get-tuple-element.68.refs_2_, f32[2080,128]{1,0:T(8,128)S(1)} %get-tuple-element.60.refs_3_.refs_0_, ...), custom_call_target="tpu_custom_call" | custom-call | bytes 32400000 | tf_op jit(solution)/shard_map/pallas_call | solution.py:540
  83.0 2.2 %collective-permute-done.34.refs_1_ = f32[2080,128]{1,0:T(8,128)S(1)} collective-permute-done((f32[2080,128]{1,0:T(8,128)S(1)}, f32[2080,128]{1,0:T(8,128)S(1)}, u32[]{:S(2)}, u32[]{:S(2)}) %collective-permute-start.34) | collective-permute-done | bytes 1064992 | tf_op jit(solution)/shard_map/ppermute | solution.py:75
  87.4 7.0 %collective-permute-done.41.refs_12_ = f32[2080,128]{1,0:T(8,128)S(1)} collective-permute-done((f32[2080,128]{1,0:T(8,128)S(1)}, f32[2080,128]{1,0:T(8,128)S(1)}, u32[]{:S(2)}, u32[]{:S(2)}) %collective-permute-start.41) | collective-permute-done | bytes 1064992 | tf_op jit(solution)/shard_map/ppermute | solution.py:75
  94.4 3.4 %collective-permute-start.48 = (f32[2080,128]{1,0:T(8,128)S(1)}, f32[2080,128]{1,0:T(8,128)S(1)}, u32[]{:S(2)}, u32[]{:S(2)}) collective-permute-start(f32[2080,128]{1,0:T(8,128)S(1)} %collective-permute-done.41.refs_12_), channel_id=1, source_target_pairs={{0,32},{1,97},{2,34},{3,99},{4,36},{5,101},{6,38},{7,103},{8,40},{... | collective-permute-start | bytes 3194888 | tf_op jit(solution)/shard_map/ppermute | solution.py:75
  98.2 8.6 %shard_map.75 = (f32[32,128,128]{2,1,0:T(8,128)S(1)}, f32[18560,128]{1,0:T(8,128)S(1)}, s32[256]{0:T(256)S(1)}) custom-call(s32[1,1,32]{2,1,0:T(1,128)S(1)} %copy-done.11, s32[256]{0:T(256)S(1)} %get-tuple-element.67.refs_1_, f32[18560,128]{1,0:T(8,128)S(1)} %get-tuple-element.68.refs_2_, ...), custom_call_target="tpu_custom_call", output_to_operand_aliasing={{0}: (15, {}), {1}: (2, {})} | custom-call | bytes 32400000 | tf_op jit(solution)/shard_map/pallas_call | solution.py:540
  110.8 4.3 %shard_map.77 = (f32[32,128,128]{2,1,0:T(8,128)S(1)}, s32[361]{0:T(512)S(1)}) custom-call(s32[1,1,32]{2,1,0:T(1,128)S(1)} %copy-done.11, s32[256]{0:T(256)S(1)} %get-tuple-element.74.refs_1_, f32[18560,128]{1,0:T(8,128)S(1)} %get-tuple-element.75.refs_2_, f32[2080,128]{1,0:T(8,128)S(1)} %collective-permute-done.39.refs_3_, ...), custom_call_target="tpu_custom_call", output_to_operand_aliasing={{0}: (5, {})} | custom-call | bytes 18000000 | tf_op jit(solution)/shard_map/pallas_call | solution.py:540
  117.2 2.2 %collective-permute-done.49.refs_4_ = f32[2080,128]{1,0:T(8,128)S(1)} collective-permute-done((f32[2080,128]{1,0:T(8,128)S(1)}, f32[2080,128]{1,0:T(8,128)S(1)}, u32[]{:S(2)}, u32[]{:S(2)}) %collective-permute-start.49) | collective-permute-done | bytes 1064992 | tf_op jit(solution)/shard_map/ppermute | solution.py:75
  119.4 2.4 %shard_map.78 = (f32[32,128,128]{2,1,0:T(8,128)S(1)}, f32[32,128,128]{2,1,0:T(8,128)S(1)}, f32[32,128,128]{2,1,0:T(8,128)S(1)}) custom-call(s32[361]{0:T(512)S(1)} %get-tuple-element.76.refs_0_, s32[1,1,32]{2,1,0:T(1,128)S(1)} %bitcast.63, f32[18560,128]{1,0:T(8,128)S(1)} %get-tuple-element.75.refs_2_, ...), custom_call_target="tpu_custom_call", output_to_operand_aliasing={{0}: (5, {})} | custom-call | bytes 18000000 | tf_op jit(solution)/shard_map/pallas_call | solution.py:553
  122.9 3.7 %collective-permute-done.47 = f32[8,128]{1,0:T(8,128)S(1)} collective-permute-done((f32[8,128]{1,0:T(8,128)S(1)}, f32[8,128]{1,0:T(8,128)S(1)}, u32[]{:S(2)}, u32[]{:S(2)}) %collective-permute-start.47) | collective-permute-done | bytes 4128 | tf_op jit(solution)/shard_map/ppermute | solution.py:61
  (66 shorter events, 35.4 us)
Async XLA Ops:
  3.5 34.7 %collective-permute-start.35 = (f32[4616,128]{1,0:T(8,128)S(1)}, f32[4616,128]{1,0:T(8,128)S(1)}, u32[]{:S(2)}, u32[]{:S(2)}) collective-permute-start(f32[4616,128]{1,0:T(8,128)S(1)} %get-tuple-element.62.refs_0_), channel_id=1, source_target_pairs={{0,2},{1,7},{2,4},{3,1},{4,6},{5,3},{6,0},{7,5},{8,10},{9,15},{10,... | collective-permute-start | bytes 7090184 | tf_op jit(solution)/shard_map/ppermute | solution.py:75
  10.8 8.2 %collective-permute-start.22 = (f32[776,128]{1,0:T(8,128)S(1)}, f32[776,128]{1,0:T(8,128)S(1)}, u32[]{:S(2)}, u32[]{:S(2)}) collective-permute-start(f32[776,128]{1,0:T(8,128)S(1)} %get-tuple-element.57.refs_4_), channel_id=1, source_target_pairs={{0,32},{1,97},{2,34},{3,99},{4,36},{5,101},{6,38},{7,103},{8,40},{... | collective-permute-start | bytes 1191944 | tf_op jit(solution)/shard_map/ppermute | solution.py:75
  13.5 8.2 %collective-permute-start.25 = (f32[640,128]{1,0:T(8,128)S(1)}, f32[640,128]{1,0:T(8,128)S(1)}, u32[]{:S(2)}, u32[]{:S(2)}) collective-permute-start(f32[640,128]{1,0:T(8,128)S(1)} %get-tuple-element.58.refs_8_), channel_id=1, source_target_pairs={{0,8},{1,25},{2,10},{3,27},{4,12},{5,29},{6,14},{7,31},{8,16},{9,1... | collective-permute-start | bytes 983048 | tf_op jit(solution)/shard_map/ppermute | solution.py:75
  14.0 8.5 %collective-permute-start.28 = (f32[640,128]{1,0:T(8,128)S(1)}, f32[640,128]{1,0:T(8,128)S(1)}, u32[]{:S(2)}, u32[]{:S(2)}) collective-permute-start(f32[640,128]{1,0:T(8,128)S(1)} %get-tuple-element.59.refs_12_), channel_id=1, source_target_pairs={{0,32},{1,97},{2,34},{3,99},{4,36},{5,101},{6,38},{7,103},{8,40},{... | collective-permute-start | bytes 983048 | tf_op jit(solution)/shard_map/ppermute | solution.py:75
  15.6 9.6 %collective-permute-start.20 = (f32[776,128]{1,0:T(8,128)S(1)}, f32[776,128]{1,0:T(8,128)S(1)}, u32[]{:S(2)}, u32[]{:S(2)}) collective-permute-start(f32[776,128]{1,0:T(8,128)S(1)} %collective-permute-done.19.refs_1_), channel_id=1, source_target_pairs={{0,8},{1,25},{2,10},{3,27},{4,12},{5,29},{6,14},{7,31},{8,16},{9,1... | collective-permute-start | bytes 1191944 | tf_op jit(solution)/shard_map/ppermute | solution.py:75
  19.0 8.2 %collective-permute-start.23 = (f32[776,128]{1,0:T(8,128)S(1)}, f32[776,128]{1,0:T(8,128)S(1)}, u32[]{:S(2)}, u32[]{:S(2)}) collective-permute-start(f32[776,128]{1,0:T(8,128)S(1)} %collective-permute-done.22.refs_5_), channel_id=1, source_target_pairs={{0,32},{1,97},{2,34},{3,99},{4,36},{5,101},{6,38},{7,103},{8,40},{... | collective-permute-start | bytes 1191944 | tf_op jit(solution)/shard_map/ppermute | solution.py:75
  21.7 8.2 %collective-permute-start.26 = (f32[640,128]{1,0:T(8,128)S(1)}, f32[640,128]{1,0:T(8,128)S(1)}, u32[]{:S(2)}, u32[]{:S(2)}) collective-permute-start(f32[640,128]{1,0:T(8,128)S(1)} %collective-permute-done.25.refs_9_), channel_id=1, source_target_pairs={{0,8},{1,25},{2,10},{3,27},{4,12},{5,29},{6,14},{7,31},{8,16},{9,1... | collective-permute-start | bytes 983048 | tf_op jit(solution)/shard_map/ppermute | solution.py:75
  22.5 8.2 %collective-permute-start.29 = (f32[640,128]{1,0:T(8,128)S(1)}, f32[640,128]{1,0:T(8,128)S(1)}, u32[]{:S(2)}, u32[]{:S(2)}) collective-permute-start(f32[640,128]{1,0:T(8,128)S(1)} %collective-permute-done.28.refs_13_), channel_id=1, source_target_pairs={{0,32},{1,97},{2,34},{3,99},{4,36},{5,101},{6,38},{7,103},{8,40},{... | collective-permute-start | bytes 983048 | tf_op jit(solution)/shard_map/ppermute | solution.py:75
  25.2 12.9 %collective-permute-start.21 = (f32[776,128]{1,0:T(8,128)S(1)}, f32[776,128]{1,0:T(8,128)S(1)}, u32[]{:S(2)}, u32[]{:S(2)}) collective-permute-start(f32[776,128]{1,0:T(8,128)S(1)} %collective-permute-done.20.refs_2_), channel_id=1, source_target_pairs={{0,8},{1,25},{2,10},{3,27},{4,12},{5,29},{6,14},{7,31},{8,16},{9,1... | collective-permute-start | bytes 1191944 | tf_op jit(solution)/shard_map/ppermute | solution.py:75
  27.2 11.0 %collective-permute-start.24 = (f32[776,128]{1,0:T(8,128)S(1)}, f32[776,128]{1,0:T(8,128)S(1)}, u32[]{:S(2)}, u32[]{:S(2)}) collective-permute-start(f32[776,128]{1,0:T(8,128)S(1)} %collective-permute-done.23.refs_6_), channel_id=1, source_target_pairs={{0,32},{1,97},{2,34},{3,99},{4,36},{5,101},{6,38},{7,103},{8,40},{... | collective-permute-start | bytes 1191944 | tf_op jit(solution)/shard_map/ppermute | solution.py:75
  38.2 28.1 %collective-permute-start.36 = (f32[4616,128]{1,0:T(8,128)S(1)}, f32[4616,128]{1,0:T(8,128)S(1)}, u32[]{:S(2)}, u32[]{:S(2)}) collective-permute-start(f32[4616,128]{1,0:T(8,128)S(1)} %shard_map.68.refs_0_), channel_id=1, source_target_pairs={{0,2},{1,7},{2,4},{3,1},{4,6},{5,3},{6,0},{7,5},{8,10},{9,15},{10,... | collective-permute-start | bytes 7090184 | tf_op jit(solution)/shard_map/ppermute | solution.py:75
  40.5 15.5 %collective-permute-start.31 = (f32[2080,128]{1,0:T(8,128)S(1)}, f32[2080,128]{1,0:T(8,128)S(1)}, u32[]{:S(2)}, u32[]{:S(2)}) collective-permute-start(f32[2080,128]{1,0:T(8,128)S(1)} %get-tuple-element.60.refs_3_.refs_0_), channel_id=1, source_target_pairs={{0,32},{1,97},{2,34},{3,99},{4,36},{5,101},{6,38},{7,103},{8,40},{... | collective-permute-start | bytes 3194888 | tf_op jit(solution)/shard_map/ppermute | solution.py:75
  44.1 14.1 %collective-permute-start.33 = (f32[2080,128]{1,0:T(8,128)S(1)}, f32[2080,128]{1,0:T(8,128)S(1)}, u32[]{:S(2)}, u32[]{:S(2)}) collective-permute-start(f32[2080,128]{1,0:T(8,128)S(1)} %get-tuple-element.61.refs_5_.refs_4_), channel_id=1, source_target_pairs={{0,8},{1,25},{2,10},{3,27},{4,12},{5,29},{6,14},{7,31},{8,16},{9,1... | collective-permute-start | bytes 3194888 | tf_op jit(solution)/shard_map/ppermute | solution.py:75
  44.8 26.6 %collective-permute-start.37 = (f32[2080,128]{1,0:T(8,128)S(1)}, f32[2080,128]{1,0:T(8,128)S(1)}, u32[]{:S(2)}, u32[]{:S(2)}) collective-permute-start(f32[2080,128]{1,0:T(8,128)S(1)} %get-tuple-element.69.refs_4_), channel_id=1, source_target_pairs={{0,32},{1,97},{2,34},{3,99},{4,36},{5,101},{6,38},{7,103},{8,40},{... | collective-permute-start | bytes 3194888 | tf_op jit(solution)/shard_map/ppermute | solution.py:75
  45.5 26.6 %collective-permute-start.38 = (f32[2080,128]{1,0:T(8,128)S(1)}, f32[2080,128]{1,0:T(8,128)S(1)}, u32[]{:S(2)}, u32[]{:S(2)}) collective-permute-start(f32[2080,128]{1,0:T(8,128)S(1)} %get-tuple-element.70.refs_6_), channel_id=1, source_target_pairs={{0,8},{1,25},{2,10},{3,27},{4,12},{5,29},{6,14},{7,31},{8,16},{9,1... | collective-permute-start | bytes 3194888 | tf_op jit(solution)/shard_map/ppermute | solution.py:75
  66.3 31.9 %collective-permute-start.43 = (f32[4616,128]{1,0:T(8,128)S(1)}, f32[4616,128]{1,0:T(8,128)S(1)}, u32[]{:S(2)}, u32[]{:S(2)}) collective-permute-start(f32[4616,128]{1,0:T(8,128)S(1)} %shard_map.71.refs_0_), channel_id=1, source_target_pairs={{0,2},{1,7},{2,4},{3,1},{4,6},{5,3},{6,0},{7,5},{8,10},{9,15},{10,... | collective-permute-start | bytes 7090184 | tf_op jit(solution)/shard_map/ppermute | solution.py:75
  67.7 15.3 %collective-permute-start.32 = (f32[2080,128]{1,0:T(8,128)S(1)}, f32[2080,128]{1,0:T(8,128)S(1)}, u32[]{:S(2)}, u32[]{:S(2)}) collective-permute-start(f32[2080,128]{1,0:T(8,128)S(1)} %collective-permute-done.31.refs_1_.refs_7_), channel_id=1, source_target_pairs={{0,32},{1,97},{2,34},{3,99},{4,36},{5,101},{6,38},{7,103},{8,40},{... | collective-permute-start | bytes 3194888 | tf_op jit(solution)/shard_map/ppermute | solution.py:75
  71.1 14.1 %collective-permute-start.34 = (f32[2080,128]{1,0:T(8,128)S(1)}, f32[2080,128]{1,0:T(8,128)S(1)}, u32[]{:S(2)}, u32[]{:S(2)}) collective-permute-start(f32[2080,128]{1,0:T(8,128)S(1)} %collective-permute-done.33.refs_2_.refs_9_.refs_5_), channel_id=1, source_target_pairs={{0,8},{1,25},{2,10},{3,27},{4,12},{5,29},{6,14},{7,31},{8,16},{9,1... | collective-permute-start | bytes 3194888 | tf_op jit(solution)/shard_map/ppermute | solution.py:75
  71.4 23.0 %collective-permute-start.41 = (f32[2080,128]{1,0:T(8,128)S(1)}, f32[2080,128]{1,0:T(8,128)S(1)}, u32[]{:S(2)}, u32[]{:S(2)}) collective-permute-start(f32[2080,128]{1,0:T(8,128)S(1)} %collective-permute-done.37.refs_8_), channel_id=1, source_target_pairs={{0,32},{1,97},{2,34},{3,99},{4,36},{5,101},{6,38},{7,103},{8,40},{... | collective-permute-start | bytes 3194888 | tf_op jit(solution)/shard_map/ppermute | solution.py:75
  72.0 25.8 %collective-permute-start.42 = (f32[2080,128]{1,0:T(8,128)S(1)}, f32[2080,128]{1,0:T(8,128)S(1)}, u32[]{:S(2)}, u32[]{:S(2)}) collective-permute-start(f32[2080,128]{1,0:T(8,128)S(1)} %collective-permute-done.38.refs_10_), channel_id=1, source_target_pairs={{0,8},{1,25},{2,10},{3,27},{4,12},{5,29},{6,14},{7,31},{8,16},{9,1... | collective-permute-start | bytes 3194888 | tf_op jit(solution)/shard_map/ppermute | solution.py:75
  85.2 21.6 %collective-permute-start.39 = (f32[2080,128]{1,0:T(8,128)S(1)}, f32[2080,128]{1,0:T(8,128)S(1)}, u32[]{:S(2)}, u32[]{:S(2)}) collective-permute-start(f32[2080,128]{1,0:T(8,128)S(1)} %get-tuple-element.71.refs_11_.refs_2_), channel_id=1, source_target_pairs={{0,32},{1,97},{2,34},{3,99},{4,36},{5,101},{6,38},{7,103},{8,40},{... | collective-permute-start | bytes 3194888 | tf_op jit(solution)/shard_map/ppermute | solution.py:75
  86.4 21.6 %collective-permute-start.40 = (f32[2080,128]{1,0:T(8,128)S(1)}, f32[2080,128]{1,0:T(8,128)S(1)}, u32[]{:S(2)}, u32[]{:S(2)}) collective-permute-start(f32[2080,128]{1,0:T(8,128)S(1)} %get-tuple-element.72.refs_13_.refs_6_), channel_id=1, source_target_pairs={{0,8},{1,25},{2,10},{3,27},{4,12},{5,29},{6,14},{7,31},{8,16},{9,1... | collective-permute-start | bytes 3194888 | tf_op jit(solution)/shard_map/ppermute | solution.py:75
  94.4 22.8 %collective-permute-start.48 = (f32[2080,128]{1,0:T(8,128)S(1)}, f32[2080,128]{1,0:T(8,128)S(1)}, u32[]{:S(2)}, u32[]{:S(2)}) collective-permute-start(f32[2080,128]{1,0:T(8,128)S(1)} %collective-permute-done.41.refs_12_), channel_id=1, source_target_pairs={{0,32},{1,97},{2,34},{3,99},{4,36},{5,101},{6,38},{7,103},{8,40},{... | collective-permute-start | bytes 3194888 | tf_op jit(solution)/shard_map/ppermute | solution.py:75
  97.8 21.6 %collective-permute-start.49 = (f32[2080,128]{1,0:T(8,128)S(1)}, f32[2080,128]{1,0:T(8,128)S(1)}, u32[]{:S(2)}, u32[]{:S(2)}) collective-permute-start(f32[2080,128]{1,0:T(8,128)S(1)} %collective-permute-done.42.refs_14_), channel_id=1, source_target_pairs={{0,8},{1,25},{2,10},{3,27},{4,12},{5,29},{6,14},{7,31},{8,16},{9,1... | collective-permute-start | bytes 3194888 | tf_op jit(solution)/shard_map/ppermute | solution.py:75
  (12 other events, 76.2 us)

commit v4 on v3

--- a/solution.py
+++ b/solution.py
@@ -100,11 +100,10 @@
     flip = row & 1
     base = lax.axis_index("col") * 64
 
-    def scan(i, n):
+    n = jnp.int32(0)
+    for i in range(32):
         codes[n] = i
-        return n + rpat[0, i >> 3, i & 7]
-
-    n = lax.fori_loop(0, 32, scan, jnp.int32(0))
+        n = n + rpat[0, i // 8, i % 8]
     m = jnp.minimum(n, 2 * R_HALF)
 
     def start(s, headers):
@@ -129,11 +128,10 @@
 
     header_a, header_b = lax.fori_loop(0, m, start, (blank(), blank()))
 
-    def scan_left(i, n):
-        lcodes[n] = i
-        return n + lpat[0, i & 3, i >> 2]
-
-    n_left = lax.fori_loop(0, 64, scan_left, jnp.int32(0))
+    n_left = jnp.int32(0)
+    for i in range(64):
+        lcodes[n_left] = i
+        n_left = n_left + lpat[0, i % 4, i // 4]
     m_left = jnp.minimum(n_left, L_CAP)
 
     def start_left(s, header):

time: 130 us -> 129 us (level)
  waiting for transfers between devices: 42.4 us -> 38.9 us
  starting transfers between devices: 50.1 us -> 51.9 us
    ppermute x30, waiting for transfers between devices: 38.7 us -> 35.2 us  [ring(): return lax.ppermute(array, AXES, pairs)]
    ppermute x30, starting transfers between devices: 49.1 us -> 50.8 us  [ring(): return lax.ppermute(array, AXES, pairs)]
  transfers between devices with their start and end apart: 32 -> 32, of which waited for: 13 -> 12; matrix products, arithmetic and copies ran while one was open for 0% -> 0% of each run, Pallas kernels for 22% -> 23%
where the time goes in v4:
time: 129 us
  starting transfers between devices  51.9 us (40%)
  waiting for transfers between devices  38.9 us (30%)
  Pallas kernels  36.4 us (28%)
    ppermute x30, starting transfers between devices, ring(): return lax.ppermute(array, AXES, pairs)  50.8 us
    ppermute x30, waiting for transfers between devices, ring(): return lax.ppermute(array, AXES, pairs)  35.2 us
    pallas_call x3, Pallas kernels, multiply(): pl.pallas_call(functools.partial(multiply_kernel, lows, halves, acc is No...  20.6 us
    pallas_call x3, Pallas kernels, hold(): pl.pallas_call(functools.partial(hold_kernel, step), out_shape=[shape, ja...  5.87 us
    ppermute x2, waiting for transfers between devices, swap(): return lax.ppermute(array, 'layer', [(0, 1), (1, 0)])  3.7 us
    pallas_call x1, Pallas kernels, local(): pl.pallas_call(pack_kernel, out_shape=[packed(R_PART)] * 2 + [packed(R_LA...  3.23 us
  transfers between devices with their start and end apart: 32, of which 12 were waited for; matrix products, arithmetic and copies ran while one was open for 0% of the time, Pallas kernels for 23%

profile of v4, /device:TPU:1, one launch (start us, length us, event | category | flops | bytes accessed | tf_op | source)
XLA Modules:
  0.0 129.1 jit_solution(16416148109104244892)
XLA Ops:
  0.0 3.2 %shard_map.66 = (f32[776,128]{1,0:T(8,128)S(1)}, f32[776,128]{1,0:T(8,128)S(1)}, f32[640,128]{1,0:T(8,128)S(1)}, f32[640,128]{1,0:T(8,128)S(1)}, f32[4616,128]{1,0:T(8,128)S(1)}) custom-call(s32[1,4,16]{2,1,0:T(4,128)} %lpat.1, s32[1,4,8]{2,1,0:T(4,128)} %rpat.1, f32[1,512,2048]{2,1,0:T(8,128)} %left.1, f32[1,512,1024]{2,1,0:T(8,128)} %right.1), custom_call_target="tpu_custom_call" | custom-call | tf_op jit(solution)/shard_map/pallas_call | solution.py:602
  3.2 4.3 %collective-permute-start.35 = (f32[4616,128]{1,0:T(8,128)S(1)}, f32[4616,128]{1,0:T(8,128)S(1)}, u32[]{:S(2)}, u32[]{:S(2)}) collective-permute-start(f32[4616,128]{1,0:T(8,128)S(1)} %get-tuple-element.62.refs_0_), channel_id=1, source_target_pairs={{0,2},{1,7},{2,4},{3,1},{4,6},{5,3},{6,0},{7,5},{8,10},{9,15},{10,... | collective-permute-start | bytes 7090184 | tf_op jit(solution)/shard_map/ppermute | solution.py:75
  7.6 2.6 %collective-permute-start.19 = (f32[776,128]{1,0:T(8,128)S(1)}, f32[776,128]{1,0:T(8,128)S(1)}, u32[]{:S(2)}, u32[]{:S(2)}) collective-permute-start(f32[776,128]{1,0:T(8,128)S(1)} %get-tuple-element.56.refs_0_), channel_id=1, source_target_pairs={{0,8},{1,25},{2,10},{3,27},{4,12},{5,29},{6,14},{7,31},{8,16},{9,1... | collective-permute-start | bytes 1191944 | tf_op jit(solution)/shard_map/ppermute | solution.py:75
  10.2 2.6 %collective-permute-start.22 = (f32[776,128]{1,0:T(8,128)S(1)}, f32[776,128]{1,0:T(8,128)S(1)}, u32[]{:S(2)}, u32[]{:S(2)}) collective-permute-start(f32[776,128]{1,0:T(8,128)S(1)} %get-tuple-element.57.refs_4_), channel_id=1, source_target_pairs={{0,32},{1,97},{2,34},{3,99},{4,36},{5,101},{6,38},{7,103},{8,40},{... | collective-permute-start | bytes 1191944 | tf_op jit(solution)/shard_map/ppermute | solution.py:75
  15.0 3.4 %collective-permute-start.20 = (f32[776,128]{1,0:T(8,128)S(1)}, f32[776,128]{1,0:T(8,128)S(1)}, u32[]{:S(2)}, u32[]{:S(2)}) collective-permute-start(f32[776,128]{1,0:T(8,128)S(1)} %collective-permute-done.19.refs_1_), channel_id=1, source_target_pairs={{0,8},{1,25},{2,10},{3,27},{4,12},{5,29},{6,14},{7,31},{8,16},{9,1... | collective-permute-start | bytes 1191944 | tf_op jit(solution)/shard_map/ppermute | solution.py:75
  18.4 2.6 %collective-permute-start.23 = (f32[776,128]{1,0:T(8,128)S(1)}, f32[776,128]{1,0:T(8,128)S(1)}, u32[]{:S(2)}, u32[]{:S(2)}) collective-permute-start(f32[776,128]{1,0:T(8,128)S(1)} %collective-permute-done.22.refs_5_), channel_id=1, source_target_pairs={{0,32},{1,97},{2,34},{3,99},{4,36},{5,101},{6,38},{7,103},{8,40},{... | collective-permute-start | bytes 1191944 | tf_op jit(solution)/shard_map/ppermute | solution.py:75
  21.9 2.6 %collective-permute-start.29 = (f32[640,128]{1,0:T(8,128)S(1)}, f32[640,128]{1,0:T(8,128)S(1)}, u32[]{:S(2)}, u32[]{:S(2)}) collective-permute-start(f32[640,128]{1,0:T(8,128)S(1)} %collective-permute-done.28.refs_13_), channel_id=1, source_target_pairs={{0,32},{1,97},{2,34},{3,99},{4,36},{5,101},{6,38},{7,103},{8,40},{... | collective-permute-start | bytes 983048 | tf_op jit(solution)/shard_map/ppermute | solution.py:75
  26.6 2.6 %collective-permute-start.24 = (f32[776,128]{1,0:T(8,128)S(1)}, f32[776,128]{1,0:T(8,128)S(1)}, u32[]{:S(2)}, u32[]{:S(2)}) collective-permute-start(f32[776,128]{1,0:T(8,128)S(1)} %collective-permute-done.23.refs_6_), channel_id=1, source_target_pairs={{0,32},{1,97},{2,34},{3,99},{4,36},{5,101},{6,38},{7,103},{8,40},{... | collective-permute-start | bytes 1191944 | tf_op jit(solution)/shard_map/ppermute | solution.py:75
  30.1 2.6 %collective-permute-start.30 = (f32[640,128]{1,0:T(8,128)S(1)}, f32[640,128]{1,0:T(8,128)S(1)}, u32[]{:S(2)}, u32[]{:S(2)}) collective-permute-start(f32[640,128]{1,0:T(8,128)S(1)} %collective-permute-done.29.refs_14_), channel_id=1, source_target_pairs={{0,32},{1,97},{2,34},{3,99},{4,36},{5,101},{6,38},{7,103},{8,40},{... | collective-permute-start | bytes 983048 | tf_op jit(solution)/shard_map/ppermute | solution.py:75
  32.7 2.7 %collective-permute-done.27.refs_11_.refs_3_ = f32[640,128]{1,0:T(8,128)S(1)} collective-permute-done((f32[640,128]{1,0:T(8,128)S(1)}, f32[640,128]{1,0:T(8,128)S(1)}, u32[]{:S(2)}, u32[]{:S(2)}) %collective-permute-start.27) | collective-permute-done | bytes 327712 | tf_op jit(solution)/shard_map/ppermute | solution.py:75
  37.8 2.4 %shard_map.67 = (f32[2080,128]{1,0:T(8,128)S(1)}, f32[2080,128]{1,0:T(8,128)S(1)}, f32[2080,128]{1,0:T(8,128)S(1)}, f32[2080,128]{1,0:T(8,128)S(1)}) custom-call(f32[776,128]{1,0:T(8,128)S(1)} %get-tuple-element.56.refs_0_, f32[776,128]{1,0:T(8,128)S(1)} %collective-permute-done.19.refs_1_, f32[776,128]{1,0:T(8,128)S(1)} %collective-permute-done.20.refs_2_, ...), custom_call_target="tpu_custom_call" | custom-call | bytes 252000000 | tf_op jit(solution)/shard_map/pallas_call | solution.py:624
  40.2 3.4 %collective-permute-start.31 = (f32[2080,128]{1,0:T(8,128)S(1)}, f32[2080,128]{1,0:T(8,128)S(1)}, u32[]{:S(2)}, u32[]{:S(2)}) collective-permute-start(f32[2080,128]{1,0:T(8,128)S(1)} %get-tuple-element.60.refs_3_.refs_0_), channel_id=1, source_target_pairs={{0,32},{1,97},{2,34},{3,99},{4,36},{5,101},{6,38},{7,103},{8,40},{... | collective-permute-start | bytes 3194888 | tf_op jit(solution)/shard_map/ppermute | solution.py:75
  49.2 6.3 %collective-permute-done.31.refs_1_.refs_7_ = f32[2080,128]{1,0:T(8,128)S(1)} collective-permute-done((f32[2080,128]{1,0:T(8,128)S(1)}, f32[2080,128]{1,0:T(8,128)S(1)}, u32[]{:S(2)}, u32[]{:S(2)}) %collective-permute-start.31) | collective-permute-done | bytes 1064992 | tf_op jit(solution)/shard_map/ppermute | solution.py:75
  55.5 2.2 %collective-permute-done.33.refs_2_.refs_9_.refs_5_ = f32[2080,128]{1,0:T(8,128)S(1)} collective-permute-done((f32[2080,128]{1,0:T(8,128)S(1)}, f32[2080,128]{1,0:T(8,128)S(1)}, u32[]{:S(2)}, u32[]{:S(2)}) %collective-permute-start.33) | collective-permute-done | bytes 1064992 | tf_op jit(solution)/shard_map/ppermute | solution.py:75
  57.7 7.9 %collective-permute-done.36.refs_0_ = f32[4616,128]{1,0:T(8,128)S(1)} collective-permute-done((f32[4616,128]{1,0:T(8,128)S(1)}, f32[4616,128]{1,0:T(8,128)S(1)}, u32[]{:S(2)}, u32[]{:S(2)}) %collective-permute-start.36) | collective-permute-done | bytes 2363424 | tf_op jit(solution)/shard_map/ppermute | solution.py:75
  67.0 3.4 %collective-permute-start.32 = (f32[2080,128]{1,0:T(8,128)S(1)}, f32[2080,128]{1,0:T(8,128)S(1)}, u32[]{:S(2)}, u32[]{:S(2)}) collective-permute-start(f32[2080,128]{1,0:T(8,128)S(1)} %collective-permute-done.31.refs_1_.refs_7_), channel_id=1, source_target_pairs={{0,32},{1,97},{2,34},{3,99},{4,36},{5,101},{6,38},{7,103},{8,40},{... | collective-permute-start | bytes 3194888 | tf_op jit(solution)/shard_map/ppermute | solution.py:75
  73.8 7.4 %shard_map.73.refs_2_.refs_15_ = f32[32,128,128]{2,1,0:T(8,128)S(1)} custom-call(s32[1,1,32]{2,1,0:T(1,128)S(1)} %copy-done.11, s32[256]{0:T(256)S(1)} %get-tuple-element.67.refs_1_, f32[18560,128]{1,0:T(8,128)S(1)} %get-tuple-element.68.refs_2_, f32[2080,128]{1,0:T(8,128)S(1)} %get-tuple-element.60.refs_3_.refs_0_, ...), custom_call_target="tpu_custom_call" | custom-call | bytes 32400000 | tf_op jit(solution)/shard_map/pallas_call | solution.py:538
  86.6 7.2 %collective-permute-done.41.refs_12_ = f32[2080,128]{1,0:T(8,128)S(1)} collective-permute-done((f32[2080,128]{1,0:T(8,128)S(1)}, f32[2080,128]{1,0:T(8,128)S(1)}, u32[]{:S(2)}, u32[]{:S(2)}) %collective-permute-start.41) | collective-permute-done | bytes 1064992 | tf_op jit(solution)/shard_map/ppermute | solution.py:75
  93.7 3.4 %collective-permute-start.48 = (f32[2080,128]{1,0:T(8,128)S(1)}, f32[2080,128]{1,0:T(8,128)S(1)}, u32[]{:S(2)}, u32[]{:S(2)}) collective-permute-start(f32[2080,128]{1,0:T(8,128)S(1)} %collective-permute-done.41.refs_12_), channel_id=1, source_target_pairs={{0,32},{1,97},{2,34},{3,99},{4,36},{5,101},{6,38},{7,103},{8,40},{... | collective-permute-start | bytes 3194888 | tf_op jit(solution)/shard_map/ppermute | solution.py:75
  97.4 9.2 %shard_map.75 = (f32[32,128,128]{2,1,0:T(8,128)S(1)}, f32[18560,128]{1,0:T(8,128)S(1)}, s32[256]{0:T(256)S(1)}) custom-call(s32[1,1,32]{2,1,0:T(1,128)S(1)} %copy-done.11, s32[256]{0:T(256)S(1)} %get-tuple-element.67.refs_1_, f32[18560,128]{1,0:T(8,128)S(1)} %get-tuple-element.68.refs_2_, ...), custom_call_target="tpu_custom_call", output_to_operand_aliasing={{0}: (15, {}), {1}: (2, {})} | custom-call | bytes 32400000 | tf_op jit(solution)/shard_map/pallas_call | solution.py:538
  107.8 5.2 %collective-permute-start.45 = (f32[8,128]{1,0:T(8,128)S(1)}, f32[8,128]{1,0:T(8,128)S(1)}, u32[]{:S(2)}, u32[]{:S(2)}) collective-permute-start(f32[8,128]{1,0:T(8,128)S(1)} %shard_map.76), channel_id=1, source_target_pairs={{0,4},{1,5},{2,6},{3,7},{4,0},{5,1},{6,2},{7,3},{8,12},{9,13},{10,... | collective-permute-start | bytes 12296 | tf_op jit(solution)/shard_map/ppermute | solution.py:75
  113.0 4.0 %shard_map.77 = (f32[32,128,128]{2,1,0:T(8,128)S(1)}, s32[361]{0:T(512)S(1)}) custom-call(s32[1,1,32]{2,1,0:T(1,128)S(1)} %copy-done.11, s32[256]{0:T(256)S(1)} %get-tuple-element.74.refs_1_, f32[18560,128]{1,0:T(8,128)S(1)} %get-tuple-element.75.refs_2_, f32[2080,128]{1,0:T(8,128)S(1)} %collective-permute-done.39.refs_3_, ...), custom_call_target="tpu_custom_call", output_to_operand_aliasing={{0}: (5, {})} | custom-call | bytes 18000000 | tf_op jit(solution)/shard_map/pallas_call | solution.py:538
  118.8 2.4 %shard_map.78 = (f32[32,128,128]{2,1,0:T(8,128)S(1)}, f32[32,128,128]{2,1,0:T(8,128)S(1)}, f32[32,128,128]{2,1,0:T(8,128)S(1)}) custom-call(s32[361]{0:T(512)S(1)} %get-tuple-element.76.refs_0_, s32[1,1,32]{2,1,0:T(1,128)S(1)} %bitcast.63, f32[18560,128]{1,0:T(8,128)S(1)} %get-tuple-element.75.refs_2_, ...), custom_call_target="tpu_custom_call", output_to_operand_aliasing={{0}: (5, {})} | custom-call | bytes 18000000 | tf_op jit(solution)/shard_map/pallas_call | solution.py:551
  122.3 3.7 %collective-permute-done.47 = f32[8,128]{1,0:T(8,128)S(1)} collective-permute-done((f32[8,128]{1,0:T(8,128)S(1)}, f32[8,128]{1,0:T(8,128)S(1)}, u32[]{:S(2)}, u32[]{:S(2)}) %collective-permute-start.47) | collective-permute-done | bytes 4128 | tf_op jit(solution)/shard_map/ppermute | solution.py:61
  (66 shorter events, 32.0 us)
Async XLA Ops:
  3.2 34.2 %collective-permute-start.35 = (f32[4616,128]{1,0:T(8,128)S(1)}, f32[4616,128]{1,0:T(8,128)S(1)}, u32[]{:S(2)}, u32[]{:S(2)}) collective-permute-start(f32[4616,128]{1,0:T(8,128)S(1)} %get-tuple-element.62.refs_0_), channel_id=1, source_target_pairs={{0,2},{1,7},{2,4},{3,1},{4,6},{5,3},{6,0},{7,5},{8,10},{9,15},{10,... | collective-permute-start | bytes 7090184 | tf_op jit(solution)/shard_map/ppermute | solution.py:75
  10.2 8.2 %collective-permute-start.22 = (f32[776,128]{1,0:T(8,128)S(1)}, f32[776,128]{1,0:T(8,128)S(1)}, u32[]{:S(2)}, u32[]{:S(2)}) collective-permute-start(f32[776,128]{1,0:T(8,128)S(1)} %get-tuple-element.57.refs_4_), channel_id=1, source_target_pairs={{0,32},{1,97},{2,34},{3,99},{4,36},{5,101},{6,38},{7,103},{8,40},{... | collective-permute-start | bytes 1191944 | tf_op jit(solution)/shard_map/ppermute | solution.py:75
  12.8 8.2 %collective-permute-start.25 = (f32[640,128]{1,0:T(8,128)S(1)}, f32[640,128]{1,0:T(8,128)S(1)}, u32[]{:S(2)}, u32[]{:S(2)}) collective-permute-start(f32[640,128]{1,0:T(8,128)S(1)} %get-tuple-element.58.refs_8_), channel_id=1, source_target_pairs={{0,8},{1,25},{2,10},{3,27},{4,12},{5,29},{6,14},{7,31},{8,16},{9,1... | collective-permute-start | bytes 983048 | tf_op jit(solution)/shard_map/ppermute | solution.py:75
  13.5 8.4 %collective-permute-start.28 = (f32[640,128]{1,0:T(8,128)S(1)}, f32[640,128]{1,0:T(8,128)S(1)}, u32[]{:S(2)}, u32[]{:S(2)}) collective-permute-start(f32[640,128]{1,0:T(8,128)S(1)} %get-tuple-element.59.refs_12_), channel_id=1, source_target_pairs={{0,32},{1,97},{2,34},{3,99},{4,36},{5,101},{6,38},{7,103},{8,40},{... | collective-permute-start | bytes 983048 | tf_op jit(solution)/shard_map/ppermute | solution.py:75
  15.0 9.5 %collective-permute-start.20 = (f32[776,128]{1,0:T(8,128)S(1)}, f32[776,128]{1,0:T(8,128)S(1)}, u32[]{:S(2)}, u32[]{:S(2)}) collective-permute-start(f32[776,128]{1,0:T(8,128)S(1)} %collective-permute-done.19.refs_1_), channel_id=1, source_target_pairs={{0,8},{1,25},{2,10},{3,27},{4,12},{5,29},{6,14},{7,31},{8,16},{9,1... | collective-permute-start | bytes 1191944 | tf_op jit(solution)/shard_map/ppermute | solution.py:75
  18.4 8.2 %collective-permute-start.23 = (f32[776,128]{1,0:T(8,128)S(1)}, f32[776,128]{1,0:T(8,128)S(1)}, u32[]{:S(2)}, u32[]{:S(2)}) collective-permute-start(f32[776,128]{1,0:T(8,128)S(1)} %collective-permute-done.22.refs_5_), channel_id=1, source_target_pairs={{0,32},{1,97},{2,34},{3,99},{4,36},{5,101},{6,38},{7,103},{8,40},{... | collective-permute-start | bytes 1191944 | tf_op jit(solution)/shard_map/ppermute | solution.py:75
  24.5 12.9 %collective-permute-start.21 = (f32[776,128]{1,0:T(8,128)S(1)}, f32[776,128]{1,0:T(8,128)S(1)}, u32[]{:S(2)}, u32[]{:S(2)}) collective-permute-start(f32[776,128]{1,0:T(8,128)S(1)} %collective-permute-done.20.refs_2_), channel_id=1, source_target_pairs={{0,8},{1,25},{2,10},{3,27},{4,12},{5,29},{6,14},{7,31},{8,16},{9,1... | collective-permute-start | bytes 1191944 | tf_op jit(solution)/shard_map/ppermute | solution.py:75
  26.6 10.9 %collective-permute-start.24 = (f32[776,128]{1,0:T(8,128)S(1)}, f32[776,128]{1,0:T(8,128)S(1)}, u32[]{:S(2)}, u32[]{:S(2)}) collective-permute-start(f32[776,128]{1,0:T(8,128)S(1)} %collective-permute-done.23.refs_6_), channel_id=1, source_target_pairs={{0,32},{1,97},{2,34},{3,99},{4,36},{5,101},{6,38},{7,103},{8,40},{... | collective-permute-start | bytes 1191944 | tf_op jit(solution)/shard_map/ppermute | solution.py:75
  37.5 28.1 %collective-permute-start.36 = (f32[4616,128]{1,0:T(8,128)S(1)}, f32[4616,128]{1,0:T(8,128)S(1)}, u32[]{:S(2)}, u32[]{:S(2)}) collective-permute-start(f32[4616,128]{1,0:T(8,128)S(1)} %shard_map.68.refs_0_), channel_id=1, source_target_pairs={{0,2},{1,7},{2,4},{3,1},{4,6},{5,3},{6,0},{7,5},{8,10},{9,15},{10,... | collective-permute-start | bytes 7090184 | tf_op jit(solution)/shard_map/ppermute | solution.py:75
  40.2 15.3 %collective-permute-start.31 = (f32[2080,128]{1,0:T(8,128)S(1)}, f32[2080,128]{1,0:T(8,128)S(1)}, u32[]{:S(2)}, u32[]{:S(2)}) collective-permute-start(f32[2080,128]{1,0:T(8,128)S(1)} %get-tuple-element.60.refs_3_.refs_0_), channel_id=1, source_target_pairs={{0,32},{1,97},{2,34},{3,99},{4,36},{5,101},{6,38},{7,103},{8,40},{... | collective-permute-start | bytes 3194888 | tf_op jit(solution)/shard_map/ppermute | solution.py:75
  43.6 14.1 %collective-permute-start.33 = (f32[2080,128]{1,0:T(8,128)S(1)}, f32[2080,128]{1,0:T(8,128)S(1)}, u32[]{:S(2)}, u32[]{:S(2)}) collective-permute-start(f32[2080,128]{1,0:T(8,128)S(1)} %get-tuple-element.61.refs_5_.refs_4_), channel_id=1, source_target_pairs={{0,8},{1,25},{2,10},{3,27},{4,12},{5,29},{6,14},{7,31},{8,16},{9,1... | collective-permute-start | bytes 3194888 | tf_op jit(solution)/shard_map/ppermute | solution.py:75
  44.1 26.6 %collective-permute-start.37 = (f32[2080,128]{1,0:T(8,128)S(1)}, f32[2080,128]{1,0:T(8,128)S(1)}, u32[]{:S(2)}, u32[]{:S(2)}) collective-permute-start(f32[2080,128]{1,0:T(8,128)S(1)} %get-tuple-element.69.refs_4_), channel_id=1, source_target_pairs={{0,32},{1,97},{2,34},{3,99},{4,36},{5,101},{6,38},{7,103},{8,40},{... | collective-permute-start | bytes 3194888 | tf_op jit(solution)/shard_map/ppermute | solution.py:75
  44.9 26.4 %collective-permute-start.38 = (f32[2080,128]{1,0:T(8,128)S(1)}, f32[2080,128]{1,0:T(8,128)S(1)}, u32[]{:S(2)}, u32[]{:S(2)}) collective-permute-start(f32[2080,128]{1,0:T(8,128)S(1)} %get-tuple-element.70.refs_6_), channel_id=1, source_target_pairs={{0,8},{1,25},{2,10},{3,27},{4,12},{5,29},{6,14},{7,31},{8,16},{9,1... | collective-permute-start | bytes 3194888 | tf_op jit(solution)/shard_map/ppermute | solution.py:75
  65.6 31.9 %collective-permute-start.43 = (f32[4616,128]{1,0:T(8,128)S(1)}, f32[4616,128]{1,0:T(8,128)S(1)}, u32[]{:S(2)}, u32[]{:S(2)}) collective-permute-start(f32[4616,128]{1,0:T(8,128)S(1)} %shard_map.71.refs_0_), channel_id=1, source_target_pairs={{0,2},{1,7},{2,4},{3,1},{4,6},{5,3},{6,0},{7,5},{8,10},{9,15},{10,... | collective-permute-start | bytes 7090184 | tf_op jit(solution)/shard_map/ppermute | solution.py:75
  67.0 15.3 %collective-permute-start.32 = (f32[2080,128]{1,0:T(8,128)S(1)}, f32[2080,128]{1,0:T(8,128)S(1)}, u32[]{:S(2)}, u32[]{:S(2)}) collective-permute-start(f32[2080,128]{1,0:T(8,128)S(1)} %collective-permute-done.31.refs_1_.refs_7_), channel_id=1, source_target_pairs={{0,32},{1,97},{2,34},{3,99},{4,36},{5,101},{6,38},{7,103},{8,40},{... | collective-permute-start | bytes 3194888 | tf_op jit(solution)/shard_map/ppermute | solution.py:75
  70.4 14.1 %collective-permute-start.34 = (f32[2080,128]{1,0:T(8,128)S(1)}, f32[2080,128]{1,0:T(8,128)S(1)}, u32[]{:S(2)}, u32[]{:S(2)}) collective-permute-start(f32[2080,128]{1,0:T(8,128)S(1)} %collective-permute-done.33.refs_2_.refs_9_.refs_5_), channel_id=1, source_target_pairs={{0,8},{1,25},{2,10},{3,27},{4,12},{5,29},{6,14},{7,31},{8,16},{9,1... | collective-permute-start | bytes 3194888 | tf_op jit(solution)/shard_map/ppermute | solution.py:75
  70.7 23.0 %collective-permute-start.41 = (f32[2080,128]{1,0:T(8,128)S(1)}, f32[2080,128]{1,0:T(8,128)S(1)}, u32[]{:S(2)}, u32[]{:S(2)}) collective-permute-start(f32[2080,128]{1,0:T(8,128)S(1)} %collective-permute-done.37.refs_8_), channel_id=1, source_target_pairs={{0,32},{1,97},{2,34},{3,99},{4,36},{5,101},{6,38},{7,103},{8,40},{... | collective-permute-start | bytes 3194888 | tf_op jit(solution)/shard_map/ppermute | solution.py:75
  71.2 25.9 %collective-permute-start.42 = (f32[2080,128]{1,0:T(8,128)S(1)}, f32[2080,128]{1,0:T(8,128)S(1)}, u32[]{:S(2)}, u32[]{:S(2)}) collective-permute-start(f32[2080,128]{1,0:T(8,128)S(1)} %collective-permute-done.38.refs_10_), channel_id=1, source_target_pairs={{0,8},{1,25},{2,10},{3,27},{4,12},{5,29},{6,14},{7,31},{8,16},{9,1... | collective-permute-start | bytes 3194888 | tf_op jit(solution)/shard_map/ppermute | solution.py:75
  84.5 22.1 %collective-permute-start.39 = (f32[2080,128]{1,0:T(8,128)S(1)}, f32[2080,128]{1,0:T(8,128)S(1)}, u32[]{:S(2)}, u32[]{:S(2)}) collective-permute-start(f32[2080,128]{1,0:T(8,128)S(1)} %get-tuple-element.71.refs_11_.refs_2_), channel_id=1, source_target_pairs={{0,32},{1,97},{2,34},{3,99},{4,36},{5,101},{6,38},{7,103},{8,40},{... | collective-permute-start | bytes 3194888 | tf_op jit(solution)/shard_map/ppermute | solution.py:75
  85.8 21.6 %collective-permute-start.40 = (f32[2080,128]{1,0:T(8,128)S(1)}, f32[2080,128]{1,0:T(8,128)S(1)}, u32[]{:S(2)}, u32[]{:S(2)}) collective-permute-start(f32[2080,128]{1,0:T(8,128)S(1)} %get-tuple-element.72.refs_13_.refs_6_), channel_id=1, source_target_pairs={{0,8},{1,25},{2,10},{3,27},{4,12},{5,29},{6,14},{7,31},{8,16},{9,1... | collective-permute-start | bytes 3194888 | tf_op jit(solution)/shard_map/ppermute | solution.py:75
  93.7 23.4 %collective-permute-start.48 = (f32[2080,128]{1,0:T(8,128)S(1)}, f32[2080,128]{1,0:T(8,128)S(1)}, u32[]{:S(2)}, u32[]{:S(2)}) collective-permute-start(f32[2080,128]{1,0:T(8,128)S(1)} %collective-permute-done.41.refs_12_), channel_id=1, source_target_pairs={{0,32},{1,97},{2,34},{3,99},{4,36},{5,101},{6,38},{7,103},{8,40},{... | collective-permute-start | bytes 3194888 | tf_op jit(solution)/shard_map/ppermute | solution.py:75
  97.2 21.6 %collective-permute-start.49 = (f32[2080,128]{1,0:T(8,128)S(1)}, f32[2080,128]{1,0:T(8,128)S(1)}, u32[]{:S(2)}, u32[]{:S(2)}) collective-permute-start(f32[2080,128]{1,0:T(8,128)S(1)} %collective-permute-done.42.refs_14_), channel_id=1, source_target_pairs={{0,8},{1,25},{2,10},{3,27},{4,12},{5,29},{6,14},{7,31},{8,16},{9,1... | collective-permute-start | bytes 3194888 | tf_op jit(solution)/shard_map/ppermute | solution.py:75
  107.7 9.3 %collective-permute-start.44 = (f32[8,128]{1,0:T(8,128)S(1)}, f32[8,128]{1,0:T(8,128)S(1)}, u32[]{:S(2)}, u32[]{:S(2)}) collective-permute-start(f32[8,128]{1,0:T(8,128)S(1)} %shard_map.76), channel_id=1, source_target_pairs={{0,2},{1,7},{2,4},{3,1},{4,6},{5,3},{6,0},{7,5},{8,10},{9,15},{10,... | collective-permute-start | bytes 12296 | tf_op jit(solution)/shard_map/ppermute | solution.py:75
  107.8 9.2 %collective-permute-start.45 = (f32[8,128]{1,0:T(8,128)S(1)}, f32[8,128]{1,0:T(8,128)S(1)}, u32[]{:S(2)}, u32[]{:S(2)}) collective-permute-start(f32[8,128]{1,0:T(8,128)S(1)} %shard_map.76), channel_id=1, source_target_pairs={{0,4},{1,5},{2,6},{3,7},{4,0},{5,1},{6,2},{7,3},{8,12},{9,13},{10,... | collective-permute-start | bytes 12296 | tf_op jit(solution)/shard_map/ppermute | solution.py:75
  (12 other events, 75.8 us)
